TPU v7x, 32 devices: a whole 2x2x4 slice. The times are simulated.
32 devices in a mesh: seq: 8 (over z, y), head: 4 (over x, core).
Axes of the slice: x: 2, y: 2, z: 4, core: 2. Of those that a mesh axis runs over, the one named last changes fastest.
Arguments:
- queries: bfloat16 [1024, 16, 128], P('seq', 'head'), may hold values from -6 to 6
- keys: bfloat16 [1024, 2, 16, 128], P('seq', None, 'head'), may hold values from -6 to 6
- values: bfloat16 [1024, 2, 16, 128], P('seq', None, 'head'), may hold values from -6 to 6
- betas: float32 [1024, 2, 16], P('seq', None, 'head'), may hold values from 0.5 to 2, as said below
- gain: float32 [128], replicated, may hold values from 0.1 to 1.9
- out_grad: bfloat16 [1024, 16, 128], P('seq', 'head'), may hold values from -6 to 6
Outputs:
- normed_out: bfloat16 [1024, 16, 128], P('seq', 'head')
- query_grad: bfloat16 [1024, 16, 128], P('seq', 'head')
- key_grad: bfloat16 [1024, 2, 16, 128], P('seq', None, 'head')
- value_grad: bfloat16 [1024, 2, 16, 128], P('seq', None, 'head')
- beta_grad: float32 [1024, 2, 16], P('seq', None, 'head')
- gain_grad: float32 [128], replicated
Inputs may be any that keep to these rules, and one draw needn't show every extreme that they name: `betas`: every step size lies strictly between 0 and 2.
All inputs are finite; a program needn't handle non-finite values.
Results may differ from a plain program's by a relative error of at most 0.003.
Values sent between devices are 32-bit elements; how exact they have to be, the bound alone decides.
No kernel may reach another device: no remote copies, remote signals or barrier semaphores. Data moves between devices by JAX's collectives and lax.ppermute only.
A program may use at most 128 MiB of HBM per device.

v0:
```python
import jax
import jax.numpy as jnp
from jax import lax
from jax.sharding import PartitionSpec as P

GROUP = 128


EPS = 1e-06
HIGH_ACCURACY = lax.Precision.HIGHEST


def passed_along(value, axis, steps):
    count = lax.axis_size(axis)
    leading, last = (max(0, -steps), min(count, count - steps))
    return lax.ppermute(value, axis, [(source, source + steps) for source in range(leading, last)])


def prefix(array, axis, combine, identity):
    count, position = (lax.axis_size(axis), lax.axis_index(axis))
    everything = jax.tree.map(lambda part: lax.all_gather(part, axis), array)
    start = jax.tree.map(
        lambda part, zero: jnp.broadcast_to(jnp.asarray(zero, part.dtype), part.shape),
        array,
        identity,
    )

    def lap(k, before):
        at = count - 1 - k
        reached = at > position
        new = combine(before, jax.tree.map(lambda part: part[at], everything))
        return jax.tree.map(lambda a, b: jnp.where(reached, a, b), new, before)

    return lax.fori_loop(0, count, lap, start)


def unit_rows(vectors):
    return vectors * lax.rsqrt(jnp.sum(vectors * vectors, axis=-1, keepdims=True) + EPS)


def group_parts(group_offset, query_block_rows, key_block_rows, value_blk, beta_blk):
    group_width = key_block_rows.shape[1]
    half_width = query_block_rows.shape[1]
    key_dim = key_block_rows.shape[2]
    key_gram = jnp.einsum("hik,hjk->hij", key_block_rows, key_block_rows, precision=HIGH_ACCURACY)
    row_index = lax.broadcasted_iota(jnp.int32, (group_width, group_width), 0)
    col_index = lax.broadcasted_iota(jnp.int32, (group_width, group_width), 1)
    strict = (col_index < row_index).astype(jnp.float32)
    unit_lower = jnp.eye(group_width, dtype=jnp.float32) + beta_blk[:, :, None] * key_gram * strict
    right_side = jnp.concatenate(
        [beta_blk[:, :, None] * key_block_rows, beta_blk[:, :, None] * value_blk], axis=-1
    )
    solved = jax.scipy.linalg.solve_triangular(
        unit_lower, right_side, lower=True, unit_diagonal=True
    )
    weighted_keys = solved[:, :, :key_dim]
    corrected_values = solved[:, :, key_dim:]
    pseudo_values = corrected_values - jnp.einsum(
        "zsr,zrn->zsn", weighted_keys, group_offset, precision=HIGH_ACCURACY
    )
    token_index = lax.broadcasted_iota(jnp.int32, (half_width, group_width), 0)
    step_index = lax.broadcasted_iota(jnp.int32, (half_width, group_width), 1)
    visible = (step_index <= 2 * token_index + 1).astype(jnp.float32)
    scores = (
        jnp.einsum("htk,hck->htc", query_block_rows, key_block_rows, precision=HIGH_ACCURACY)
        * visible
    )
    output_rows = jnp.einsum(
        "asw,awl->asl", query_block_rows, group_offset, precision=HIGH_ACCURACY
    )
    output_rows = output_rows + jnp.einsum(
        "htc,hcv->htv", scores, pseudo_values, precision=HIGH_ACCURACY
    )
    final_state = group_offset + jnp.einsum(
        "yeb,yeo->ybo", key_block_rows, pseudo_values, precision=HIGH_ACCURACY
    )
    return (output_rows, final_state, weighted_keys, scores)


def group_apply(group_offset, query_block_rows, key_block_rows, value_blk, beta_blk):
    output_rows, final_state, weighted_keys, scores = group_parts(
        group_offset, query_block_rows, key_block_rows, value_blk, beta_blk
    )
    return (output_rows, final_state)


def compose(earlier, later):
    trans_early, state_early = earlier
    trans_late, state_late = later
    product = jnp.einsum("hij,hjk->hik", trans_late, trans_early, precision=HIGH_ACCURACY)
    carried = (
        jnp.einsum("hij,hjk->hik", trans_late, state_early, precision=HIGH_ACCURACY) + state_late
    )
    return (product, carried)


def local(queries, keys, values, betas, gain, out_grad):
    tok_local, heads_local, key_dim = queries.shape
    value_dim = values.shape[-1]
    substeps = keys.shape[1]
    group_width = GROUP
    half_width = group_width // substeps
    group_count = tok_local * substeps // group_width
    q_unit, q_pullback = jax.vjp(unit_rows, queries.astype(jnp.float32))
    k_unit, k_pullback = jax.vjp(unit_rows, keys.astype(jnp.float32))
    q_groups = q_unit.reshape(group_count, half_width, heads_local, key_dim).transpose(0, 2, 1, 3)
    k_groups = k_unit.reshape(group_count, group_width, heads_local, key_dim).transpose(0, 2, 1, 3)
    v_groups = (
        values.astype(jnp.float32)
        .reshape(group_count, group_width, heads_local, value_dim)
        .transpose(0, 2, 1, 3)
    )
    b_groups = betas.reshape(group_count, group_width, heads_local).transpose(0, 2, 1)
    grad_groups = (
        out_grad.astype(jnp.float32)
        .reshape(group_count, half_width, heads_local, value_dim)
        .transpose(0, 2, 1, 3)
    )
    eye_heads = jnp.broadcast_to(
        jnp.eye(key_dim, dtype=jnp.float32), (heads_local, key_dim, key_dim)
    )
    zero_state = jnp.zeros((heads_local, key_dim, value_dim), jnp.float32)

    def local_step(carry, items):
        local_state, transfer = carry
        query_block_rows, key_block_rows, value_blk, beta_blk = items
        output_rows, final_state, weighted_keys, scores = group_parts(
            local_state, query_block_rows, key_block_rows, value_blk, beta_blk
        )
        reduced = query_block_rows - jnp.einsum(
            "htc,hck->htk", scores, weighted_keys, precision=HIGH_ACCURACY
        )
        carried_rows = jnp.einsum("htk,hkj->htj", reduced, transfer, precision=HIGH_ACCURACY)
        weighted = jnp.einsum("hck,hkj->hcj", weighted_keys, transfer, precision=HIGH_ACCURACY)
        transfer_next = transfer - jnp.einsum(
            "hck,hcj->hkj", key_block_rows, weighted, precision=HIGH_ACCURACY
        )
        return ((final_state, transfer_next), (output_rows, carried_rows, local_state, transfer))

    group_inputs = (q_groups, k_groups, v_groups, b_groups)
    (shard_state, shard_trans), (local_out, carried_query_rows, local_starts, trans_starts) = (
        lax.scan(local_step, (zero_state, eye_heads), group_inputs)
    )
    seq_count = lax.axis_size("seq")

    def chain_turn(position, received):
        passed = (
            jnp.einsum("hij,hjk->hik", shard_trans, received, precision=HIGH_ACCURACY) + shard_state
        )
        return passed_along(passed, "seq", 1)

    entry_state = lax.fori_loop(0, seq_count - 1, chain_turn, zero_state)

    def replay_step(memory_matrix, items):
        block_out, final_state = group_apply(memory_matrix, *items)
        return (final_state, (block_out, memory_matrix))

    _, (output_rows, starts) = lax.scan(replay_step, entry_state, group_inputs)
    inv_rms = lax.rsqrt(jnp.mean(output_rows * output_rows, axis=-1, keepdims=True) + EPS)
    normal_out = output_rows * inv_rms
    normed = gain * normal_out
    gain_part = jnp.sum(grad_groups * normal_out, axis=(0, 1, 2))
    scaled_grad = grad_groups * gain
    output_adjoint = inv_rms * (
        scaled_grad - normal_out * jnp.mean(scaled_grad * normal_out, axis=-1, keepdims=True)
    )
    partition_adjoint = jnp.einsum(
        "beuc,beur->ecr", carried_query_rows, output_adjoint, precision=HIGH_ACCURACY
    )
    shard_trans_t = jnp.swapaxes(shard_trans, 1, 2)
    exit_adjoint = prefix(
        (shard_trans_t, partition_adjoint), "seq", compose, (eye_heads, zero_state)
    )[1]

    def back_step(adjoint, items):
        group_offset, query_block_rows, key_block_rows, value_blk, beta_blk, grad_blk = items
        _, pullback = jax.vjp(
            group_apply, group_offset, query_block_rows, key_block_rows, value_blk, beta_blk
        )
        d_start, d_query, d_key, d_value, d_beta = pullback((grad_blk, adjoint))
        return (d_start, (d_query, d_key, d_value, d_beta))

    _, (dq_groups, dk_groups, dv_groups, db_groups) = lax.scan(
        back_step,
        exit_adjoint,
        (starts, q_groups, k_groups, v_groups, b_groups, output_adjoint),
        reverse=True,
    )
    dq_unit = dq_groups.transpose(0, 2, 1, 3).reshape(tok_local, heads_local, key_dim)
    dk_unit = dk_groups.transpose(0, 2, 1, 3).reshape(tok_local, substeps, heads_local, key_dim)
    query_grad = q_pullback(dq_unit)[0].astype(jnp.bfloat16)
    key_grad = k_pullback(dk_unit)[0].astype(jnp.bfloat16)
    value_grad = (
        dv_groups.transpose(0, 2, 1, 3)
        .reshape(tok_local, substeps, heads_local, value_dim)
        .astype(jnp.bfloat16)
    )
    beta_grad = db_groups.transpose(0, 2, 1).reshape(tok_local, substeps, heads_local)
    normed_out = (
        normed.transpose(0, 2, 1, 3).reshape(tok_local, heads_local, value_dim).astype(jnp.bfloat16)
    )
    gain_grad = lax.psum(gain_part, ("seq", "head"))
    return (normed_out, query_grad, key_grad, value_grad, beta_grad, gain_grad)


def solution(mesh):
    return jax.shard_map(
        local,
        mesh=mesh,
        in_specs=(
            P("seq", "head", None),
            P("seq", None, "head", None),
            P("seq", None, "head", None),
            P("seq", None, "head"),
            P(),
            P("seq", "head", None),
        ),
        out_specs=(
            P("seq", "head", None),
            P("seq", "head", None),
            P("seq", None, "head", None),
            P("seq", None, "head", None),
            P("seq", None, "head"),
            P(),
        ),
        check_vma=False,
    )
```

profile of v0, /device:TPU:0, one launch (start us, length us, event | category | flops | bytes accessed | tf_op | source)
XLA Modules:
  0.0 472.4 jit_solution(5216370581937813828)
XLA Ops:
  7.3 1.4 fusion.163
  8.9 1.3 convert_multiply_fusion.2
  12.0 89.0 %while.80 = (s32[]{:T(128)}, f32[4,128,128]{2,1,0:T(8,128)S(1)}, f32[4,128,128]{2,1,0:T(8,128)S(1)}, f32[2,4,64,128]{3,2,1,0:T(8,128)S(1)}, f32[2,4,128,128]{3,2...) while((s32[]{:T(128)}, f32[4,128,128]{2,1,0:T(8,128)S(1)}, ...), condition=%wide.region_3.5_spmd.clone, body=%wide.region_2.4_spmd.clone.sunk | while | flops 856752384 | bytes 9022100 | solution.py:142
  13.0 39.3 %custom-call.28 = f32[4,1,128,128]{2,3,1,0:T(8,128)S(1)} custom-call(f32[4,1,128,128]{3,2,1,0:T(8,128)S(1)} %fusion.385), custom_call_target="InvertDiagBlocksLowerTriangular" | custom-call | tf_op jit(solution)/shard_map/while/body/eval_jaxpr/jit(_solve_triangular)/vmap()/triangular_solve/custom-call.1 | solution.py:53
  57.4 39.3 %custom-call.28 = f32[4,1,128,128]{2,3,1,0:T(8,128)S(1)} custom-call(f32[4,1,128,128]{3,2,1,0:T(8,128)S(1)} %fusion.385), custom_call_target="InvertDiagBlocksLowerTriangular" | custom-call | tf_op jit(solution)/shard_map/while/body/eval_jaxpr/jit(_solve_triangular)/vmap()/triangular_solve/custom-call.1 | solution.py:53
  102.1 86.5 %while.77 = (s32[]{:T(128)}, f32[4,128,128]{2,1,0:T(8,128)S(1)}, f32[4,128,128]{2,1,0:T(8,128)S(1)}, f32[4,128,128]{2,1,0:T(8,128)S(1)}, s32[]{:T(128)}) while((s32[]{:T(128)}, f32[4,128,128]{2,1,0:T(8,128)S(1)}, f32[4,128,128]{2,1,0:T(8,128)S(1)}, f32[4,128,128]{2,1,0:T(8,128)S(1)}, s32[]{:T(128)}) %tuple.178), condition=%wide.region_5.7_spmd, body=%wide.region_4.6_spmd.sunk | while | flops 100728832 | bytes 2097253 | solution.py:152
  102.5 4.9 %collective-permute-start = (f32[4,128,128]{2,1,0:T(8,128)S(1)}, f32[4,128,128]{2,1,0:T(8,128)S(1)}, u32[]{:S(2)}, u32[]{:S(2)}) collective-permute-start(f32[4,128,128]{2,1,0:T(8,128)S(1)} %convolution_add_fusion.19), channel_id=1, source_target_pairs={{0,4},{4,8},{8,12},{12,16},{16,20},{20,24},{24,28},{1,5},{5,9},{9,... | collective-permute-start | bytes 786440 | tf_op jit(solution)/shard_map/while/body/eval_jaxpr/ppermute | solution.py:16
  107.4 5.5 %collective-permute-done = f32[4,128,128]{2,1,0:T(8,128)S(1)} collective-permute-done((f32[4,128,128]{2,1,0:T(8,128)S(1)}, f32[4,128,128]{2,1,0:T(8,128)S(1)}, u32[]{:S(2)}, u32[]{:S(2)}) %collective-permute-start) | collective-permute-done | bytes 262176 | tf_op jit(solution)/shard_map/while/body/eval_jaxpr/ppermute | solution.py:16
  113.3 4.4 collective-permute-start
  117.7 4.6 collective-permute-done
  122.8 9.4 %collective-permute-start = (f32[4,128,128]{2,1,0:T(8,128)S(1)}, f32[4,128,128]{2,1,0:T(8,128)S(1)}, u32[]{:S(2)}, u32[]{:S(2)}) collective-permute-start(f32[4,128,128]{2,1,0:T(8,128)S(1)} %convolution_add_fusion.19), channel_id=1, source_target_pairs={{0,4},{4,8},{8,12},{12,16},{16,20},{20,24},{24,28},{1,5},{5,9},{9,... | collective-permute-start | bytes 786440 | tf_op jit(solution)/shard_map/while/body/eval_jaxpr/ppermute | solution.py:16
  132.2 9.6 %collective-permute-done = f32[4,128,128]{2,1,0:T(8,128)S(1)} collective-permute-done((f32[4,128,128]{2,1,0:T(8,128)S(1)}, f32[4,128,128]{2,1,0:T(8,128)S(1)}, u32[]{:S(2)}, u32[]{:S(2)}) %collective-permute-start) | collective-permute-done | bytes 262176 | tf_op jit(solution)/shard_map/while/body/eval_jaxpr/ppermute | solution.py:16
  142.1 6.2 %collective-permute-start = (f32[4,128,128]{2,1,0:T(8,128)S(1)}, f32[4,128,128]{2,1,0:T(8,128)S(1)}, u32[]{:S(2)}, u32[]{:S(2)}) collective-permute-start(f32[4,128,128]{2,1,0:T(8,128)S(1)} %convolution_add_fusion.19), channel_id=1, source_target_pairs={{0,4},{4,8},{8,12},{12,16},{16,20},{20,24},{24,28},{1,5},{5,9},{9,... | collective-permute-start | bytes 786440 | tf_op jit(solution)/shard_map/while/body/eval_jaxpr/ppermute | solution.py:16
  148.4 5.4 %collective-permute-done = f32[4,128,128]{2,1,0:T(8,128)S(1)} collective-permute-done((f32[4,128,128]{2,1,0:T(8,128)S(1)}, f32[4,128,128]{2,1,0:T(8,128)S(1)}, u32[]{:S(2)}, u32[]{:S(2)}) %collective-permute-start) | collective-permute-done | bytes 262176 | tf_op jit(solution)/shard_map/while/body/eval_jaxpr/ppermute | solution.py:16
  154.2 10.6 %collective-permute-start = (f32[4,128,128]{2,1,0:T(8,128)S(1)}, f32[4,128,128]{2,1,0:T(8,128)S(1)}, u32[]{:S(2)}, u32[]{:S(2)}) collective-permute-start(f32[4,128,128]{2,1,0:T(8,128)S(1)} %convolution_add_fusion.19), channel_id=1, source_target_pairs={{0,4},{4,8},{8,12},{12,16},{16,20},{20,24},{24,28},{1,5},{5,9},{9,... | collective-permute-start | bytes 786440 | tf_op jit(solution)/shard_map/while/body/eval_jaxpr/ppermute | solution.py:16
  164.8 3.9 collective-permute-done
  169.1 5.3 %collective-permute-start = (f32[4,128,128]{2,1,0:T(8,128)S(1)}, f32[4,128,128]{2,1,0:T(8,128)S(1)}, u32[]{:S(2)}, u32[]{:S(2)}) collective-permute-start(f32[4,128,128]{2,1,0:T(8,128)S(1)} %convolution_add_fusion.19), channel_id=1, source_target_pairs={{0,4},{4,8},{8,12},{12,16},{16,20},{20,24},{24,28},{1,5},{5,9},{9,... | collective-permute-start | bytes 786440 | tf_op jit(solution)/shard_map/while/body/eval_jaxpr/ppermute | solution.py:16
  174.4 4.3 collective-permute-done
  179.1 5.6 %collective-permute-start = (f32[4,128,128]{2,1,0:T(8,128)S(1)}, f32[4,128,128]{2,1,0:T(8,128)S(1)}, u32[]{:S(2)}, u32[]{:S(2)}) collective-permute-start(f32[4,128,128]{2,1,0:T(8,128)S(1)} %convolution_add_fusion.19), channel_id=1, source_target_pairs={{0,4},{4,8},{8,12},{12,16},{16,20},{20,24},{24,28},{1,5},{5,9},{9,... | collective-permute-start | bytes 786440 | tf_op jit(solution)/shard_map/while/body/eval_jaxpr/ppermute | solution.py:16
  184.7 3.9 collective-permute-done
  188.6 86.9 %while.78 = (s32[]{:T(128)}, f32[4,128,128]{2,1,0:T(8,128)S(1)}, f32[2,4,64,128]{3,2,1,0:T(8,128)S(1)}, f32[2,4,128,128]{3,2,1,0:T(8,128)S(1)}, f32[2,4,128,128]...) while((s32[]{:T(128)}, f32[4,128,128]{2,1,0:T(8,128)S(1)}, ...), condition=%wide.region_7.9_spmd, body=%wide.region_6.8_spmd.sunk | while | flops 655229184 | bytes 7711361 | solution.py:158
  190.0 39.3 %custom-call.26 = f32[4,1,128,128]{2,3,1,0:T(8,128)S(1)} custom-call(f32[4,1,128,128]{3,2,1,0:T(8,128)S(1)} %fusion.313), custom_call_target="InvertDiagBlocksLowerTriangular" | custom-call | tf_op jit(solution)/shard_map/while/body/eval_jaxpr/jit(_solve_triangular)/vmap()/triangular_solve/custom-call.1 | solution.py:53
  233.4 39.3 %custom-call.26 = f32[4,1,128,128]{2,3,1,0:T(8,128)S(1)} custom-call(f32[4,1,128,128]{3,2,1,0:T(8,128)S(1)} %fusion.313), custom_call_target="InvertDiagBlocksLowerTriangular" | custom-call | tf_op jit(solution)/shard_map/while/body/eval_jaxpr/jit(_solve_triangular)/vmap()/triangular_solve/custom-call.1 | solution.py:53
  275.5 0.9 copy.214
  276.9 1.1 fusion.173
  278.1 2.3 convolution_bitcast_fusion.1
  281.1 44.8 %psum.7 = f32[128]{0:T(128)} all-reduce(f32[128]{0:T(128)S(1)} %get-tuple-element.715), channel_id=1, replica_groups=mesh['seq'=8,'head'=4] {'seq','head'}, use_global_device_ids=true, to_apply=%region_20.22 | all-reduce | flops 128 | bytes 1024 | tf_op jit(solution)/shard_map/psum | solution.py:202
  326.6 9.1 %all-gather.7.cloned.1.call-done = f32[32,128,128]{2,1,0:T(8,128)} async-done(((f32[4,128,128]{2,1,0:T(8,128)}), f32[32,128,128]{2,1,0:T(8,128)}) %all-gather.7.cloned.1.call-update) | async-done | bytes 2097168 | tf_op jit(solution)/shard_map/all_gather | solution.py:21
  335.7 11.9 %while.81 = (s32[]{:T(128)}, f32[4,128,128]{2,1,0:T(8,128)S(1)}, s32[]{:T(128)}, f32[8,4,128,128]{3,2,1,0:T(8,128)}, f32[8,4,128,128]{3,2,1,0:T(8,128)}, /*index=5*/s32[]{:T(128)}, s32[]{:T(128)}, s32[]{:T(128)}, s32[]{:T(128)}) while((s32[]{:T(128)}, f32[4,128,128]{2,1,0:T(8,128)S(1)}, s32[]{:T(128)}, ...), condition=%wide.region_11.13_spmd.clone, body=%wide.region_10.12_spmd.clone.sunk | while | flops 100925448 | bytes 1837733 | solution.py:34
  335.8 1.4 fusion.392
  337.3 1.4 fusion.392
  338.7 1.4 fusion.392
  340.2 1.4 fusion.392
  341.7 1.4 fusion.392
  343.2 1.4 fusion.392
  344.7 1.4 fusion.392
  346.2 1.4 fusion.392
  348.3 0.8 broadcast.235
  349.2 107.7 %while.79 = (s32[]{:T(128)}, f32[4,128,128]{2,1,0:T(8,128)S(1)}, f32[2,4,64,128]{3,2,1,0:T(8,128)}, f32[2,4,128,128]{3,2,1,0:T(8,128)}, bf16[2,4,128,128]{3,2,1,...) while((s32[]{:T(128)}, f32[4,128,128]{2,1,0:T(8,128)S(1)}, ...), condition=%wide.region_16.18_spmd, body=%wide.region_12.17_spmd.sunk | while | flops 1864859392 | bytes 28562280 | solution.py:183
  352.4 0.8 add_bitcast_fusion.2
  353.2 40.1 %custom-call.27 = f32[4,1,128,128]{2,3,1,0:T(8,128)S(1)} custom-call(f32[4,1,128,128]{3,2,1,0:T(8,128)} %add_bitcast_fusion.2), custom_call_target="InvertDiagBlocksLowerTriangular" | custom-call | tf_op jit(solution)/shard_map/while/body/eval_jaxpr/jvp(jit(_solve_triangular))/vmap()/triangular_solve/custom-call.1 | solution.py:53
  406.2 0.8 add_bitcast_fusion.2
  407.1 40.1 %custom-call.27 = f32[4,1,128,128]{2,3,1,0:T(8,128)S(1)} custom-call(f32[4,1,128,128]{3,2,1,0:T(8,128)} %add_bitcast_fusion.2), custom_call_target="InvertDiagBlocksLowerTriangular" | custom-call | tf_op jit(solution)/shard_map/while/body/eval_jaxpr/jvp(jit(_solve_triangular))/vmap()/triangular_solve/custom-call.1 | solution.py:53
  456.9 1.2 copy.221
  458.1 1.1 fusion.167
  459.4 1.9 fusion.165
  462.5 1.4 fusion.162
  463.8 0.9 copy.227
  (228 shorter events, 54.0 us)
Async XLA Ops:
  7.2 3.1 copy-start.15
  7.2 3.4 copy-start.14
  7.2 319.5 %all-gather.5.cloned.1.call-start = ((), (), s32[]{:S(2)}) async-start(), calls=%async_computation | async-start | bytes 2359296 | tf_op jit(solution)/shard_map/all_gather | solution.py:21
  8.7 2.1 copy-start.1
  8.9 2.1 copy-start.5
  11.3 0.6 copy-start.13
  100.9 1.1 copy-start.7
  101.8 233.9 %all-gather.7.cloned.1.call-start = ((), (), s32[]{:S(2)}) async-start(), calls=%async_computation.1 | async-start | bytes 2359296 | tf_op jit(solution)/shard_map/all_gather | solution.py:21
  102.5 10.4 %collective-permute-start = (f32[4,128,128]{2,1,0:T(8,128)S(1)}, f32[4,128,128]{2,1,0:T(8,128)S(1)}, u32[]{:S(2)}, u32[]{:S(2)}) collective-permute-start(f32[4,128,128]{2,1,0:T(8,128)S(1)} %convolution_add_fusion.19), channel_id=1, source_target_pairs={{0,4},{4,8},{8,12},{12,16},{16,20},{20,24},{24,28},{1,5},{5,9},{9,... | collective-permute-start | bytes 786440 | tf_op jit(solution)/shard_map/while/body/eval_jaxpr/ppermute | solution.py:16
  113.3 9.1 %collective-permute-start = (f32[4,128,128]{2,1,0:T(8,128)S(1)}, f32[4,128,128]{2,1,0:T(8,128)S(1)}, u32[]{:S(2)}, u32[]{:S(2)}) collective-permute-start(f32[4,128,128]{2,1,0:T(8,128)S(1)} %convolution_add_fusion.19), channel_id=1, source_target_pairs={{0,4},{4,8},{8,12},{12,16},{16,20},{20,24},{24,28},{1,5},{5,9},{9,... | collective-permute-start | bytes 786440 | tf_op jit(solution)/shard_map/while/body/eval_jaxpr/ppermute | solution.py:16
  122.8 19.0 %collective-permute-start = (f32[4,128,128]{2,1,0:T(8,128)S(1)}, f32[4,128,128]{2,1,0:T(8,128)S(1)}, u32[]{:S(2)}, u32[]{:S(2)}) collective-permute-start(f32[4,128,128]{2,1,0:T(8,128)S(1)} %convolution_add_fusion.19), channel_id=1, source_target_pairs={{0,4},{4,8},{8,12},{12,16},{16,20},{20,24},{24,28},{1,5},{5,9},{9,... | collective-permute-start | bytes 786440 | tf_op jit(solution)/shard_map/while/body/eval_jaxpr/ppermute | solution.py:16
  142.1 11.6 %collective-permute-start = (f32[4,128,128]{2,1,0:T(8,128)S(1)}, f32[4,128,128]{2,1,0:T(8,128)S(1)}, u32[]{:S(2)}, u32[]{:S(2)}) collective-permute-start(f32[4,128,128]{2,1,0:T(8,128)S(1)} %convolution_add_fusion.19), channel_id=1, source_target_pairs={{0,4},{4,8},{8,12},{12,16},{16,20},{20,24},{24,28},{1,5},{5,9},{9,... | collective-permute-start | bytes 786440 | tf_op jit(solution)/shard_map/while/body/eval_jaxpr/ppermute | solution.py:16
  154.2 14.5 %collective-permute-start = (f32[4,128,128]{2,1,0:T(8,128)S(1)}, f32[4,128,128]{2,1,0:T(8,128)S(1)}, u32[]{:S(2)}, u32[]{:S(2)}) collective-permute-start(f32[4,128,128]{2,1,0:T(8,128)S(1)} %convolution_add_fusion.19), channel_id=1, source_target_pairs={{0,4},{4,8},{8,12},{12,16},{16,20},{20,24},{24,28},{1,5},{5,9},{9,... | collective-permute-start | bytes 786440 | tf_op jit(solution)/shard_map/while/body/eval_jaxpr/ppermute | solution.py:16
  169.1 9.6 %collective-permute-start = (f32[4,128,128]{2,1,0:T(8,128)S(1)}, f32[4,128,128]{2,1,0:T(8,128)S(1)}, u32[]{:S(2)}, u32[]{:S(2)}) collective-permute-start(f32[4,128,128]{2,1,0:T(8,128)S(1)} %convolution_add_fusion.19), channel_id=1, source_target_pairs={{0,4},{4,8},{8,12},{12,16},{16,20},{20,24},{24,28},{1,5},{5,9},{9,... | collective-permute-start | bytes 786440 | tf_op jit(solution)/shard_map/while/body/eval_jaxpr/ppermute | solution.py:16
  179.1 9.5 %collective-permute-start = (f32[4,128,128]{2,1,0:T(8,128)S(1)}, f32[4,128,128]{2,1,0:T(8,128)S(1)}, u32[]{:S(2)}, u32[]{:S(2)}) collective-permute-start(f32[4,128,128]{2,1,0:T(8,128)S(1)} %convolution_add_fusion.19), channel_id=1, source_target_pairs={{0,4},{4,8},{8,12},{12,16},{16,20},{20,24},{24,28},{1,5},{5,9},{9,... | collective-permute-start | bytes 786440 | tf_op jit(solution)/shard_map/while/body/eval_jaxpr/ppermute | solution.py:16
  188.6 88.0 %copy-start.16 = (f32[128]{0:T(128)S(1)}, f32[128]{0:T(128)}, u32[]{:S(2)}) copy-start(f32[128]{0:T(128)} %param.22) | copy-start | bytes 1540
  394.9 3.6 copy-start.11
  398.8 2.8 copy-start.12
  398.9 2.8 copy-start.2
  399.5 2.6 copy-start.8
  402.1 0.8 copy-start.3
  402.3 0.7 copy-start.9
  448.8 3.6 copy-start.11
  452.7 2.8 copy-start.12
  452.7 2.8 copy-start.2
  453.4 2.6 copy-start.8
  456.0 0.8 copy-start.3
  456.2 0.7 copy-start.9
  456.9 4.5 copy-start.4
  456.9 4.8 %copy-start = (bf16[128,2,4,128]{3,2,1,0:T(4,128)(2,1)S(1)}, bf16[128,2,4,128]{3,2,1,0:T(4,128)(2,1)}, u32[]{:S(2)}) copy-start(bf16[128,2,4,128]{3,2,1,0:T(4,128)(2,1)} %param.19) | copy-start | bytes 786436
  456.9 5.6 %copy-start.6 = (f32[128,2,4]{2,1,0:T(2,128)S(1)}, f32[128,2,4]{2,1,0:T(2,128)}, u32[]{:S(2)}) copy-start(f32[128,2,4]{2,1,0:T(2,128)} %copy-done.5) | copy-start | bytes 12292
  459.4 4.4 copy-start.10
Sparse Core Ops, SparseCore 0:
  101.9 60.3 all-gather.4
  280.5 55.2 all-gather.6
where the time goes:
time: 473 us; the launch traced here: 472 us
  other arithmetic  252 us (53%)
  matrix products  55.6 us (12%)
  starting transfers between devices  46.7 us (10%)
  waiting for transfers between devices  46.2 us (10%)
  blocking collectives  44.8 us (9%)
  between operations  14.4 us (3%)
  local copies, waits for them, and re-layouts  11 us (2%)
    another operation x20, other arithmetic, group_parts(): jax.scipy.linalg.solve_triangular(unit_lower, right_side, lower=True, uni...  240 us
    ppermute x7, starting transfers between devices, passed_along(): lax.ppermute(value, axis, [(source, source + steps) for source in range(l...  46.5 us
    psum x1, blocking collectives, local(): gain_grad = lax.psum(gain_part, ('seq', 'head'))  44.8 us
    ppermute x7, waiting for transfers between devices, passed_along(): lax.ppermute(value, axis, [(source, source + steps) for source in range(l...  37.1 us
    dot_general x8, matrix products, compose(): jnp.einsum('hij,hjk->hik', trans_late, state_early, precision=HIGH_ACCURACY)  11.4 us
  transfers between devices with their start and end apart: 9, of which 8 were waited for; matrix products, arithmetic and copies ran while one was open for 20% of the time, Pallas kernels for 0%

commit v1 on v0

v1 whole, which is shorter than its diff:
```python
import functools

import jax
import jax.numpy as jnp
from jax import lax
from jax.experimental import pallas as pl
from jax.experimental.pallas import tpu as pltpu
from jax.sharding import PartitionSpec as P

EPS = 1e-06
GROUP = 4
HALF = 128
BASE = 16
F32 = jnp.float32
BF16 = jnp.bfloat16


def mm(a, b, ta=False, tb=False):
    dims = (((0 if ta else 1,), (1 if tb else 0,)), ((), ()))
    return lax.dot_general(
        a, b, dims, precision=lax.Precision.HIGH, preferred_element_type=F32
    )


def exact_nt(a, b):
    return lax.dot_general(a, b, (((1,), (1,)), ((), ())), preferred_element_type=F32)


def iota(shape, dim):
    return lax.broadcasted_iota(jnp.int32, shape, dim)


def row_of(column):
    square = jnp.where(iota((HALF, HALF), 0) == iota((HALF, HALF), 1), column, 0.0)
    return jnp.sum(square, axis=0, keepdims=True)


def rate_column(rates, head):
    return jnp.sum(jnp.where(iota(rates.shape, 1) == head, rates, 0.0), axis=1, keepdims=True)


def small_inverses(lower, rate_row):
    blocks = HALF // BASE
    lane = iota((BASE, HALF), 1)
    row = iota((BASE, HALF), 0)
    packed = jnp.zeros((BASE, HALF), F32)
    for b in range(blocks):
        packed = jnp.where(lane // BASE == b, lower[b * BASE : (b + 1) * BASE], packed)
    scaled = packed * rate_row
    for j in range(BASE - 1):
        index = lane // BASE * BASE + j
        factor = jnp.take_along_axis(scaled, index, axis=1, mode="promise_in_bounds")
        packed = packed - jnp.where(row > j, factor, 0.0) * packed[j : j + 1]
    return jnp.concatenate(
        [jnp.where(lane // BASE == b, packed, 0.0) for b in range(blocks)], axis=0
    )


def first_kernel(
    group, k_ref, v_ref, rates_ref, ts0, ts1, ts2, ts3, ku_ref, n_ref, w_ref, e_ref, kf, vf
):
    me = lax.rem(lax.axis_index("seq"), group)
    kf[...] = k_ref[...].astype(F32)
    vf[...] = v_ref[...].astype(F32)
    heads = range(len((ts0, ts1, ts2, ts3)))
    steps = rates_ref.shape[0]
    stride = kf.shape[0] // steps
    rates = rates_ref[...]
    strict = iota((HALF, HALF), 1) < iota((HALF, HALF), 0)
    unit, vals, rate, rate_rows, diag, cross = [], [], [], [], [], []
    for i in heads:
        head = me ^ i
        raw = kf[pl.ds(head, steps, stride=stride), :]
        inv = lax.rsqrt(jnp.sum(raw * raw, axis=1, keepdims=True) + EPS)
        column = rate_column(rates, head)
        unit.append(raw * inv)
        ku_ref[i] = unit[i]
        vals.append(vf[pl.ds(head, steps, stride=stride), :])
        rate.append(column)
        rate_rows.append([row_of(column[:HALF]), row_of(column[HALF:])])
        inv_rows = [row_of(inv[:HALF]), row_of(inv[HALF:])]
        raw16 = raw.astype(BF16)
        halves = [raw16[:HALF], raw16[HALF:]]
        diag.append(
            [
                jnp.where(
                    strict,
                    exact_nt(halves[b], halves[b])
                    * inv[b * HALF : (b + 1) * HALF]
                    * inv_rows[b],
                    0.0,
                )
                for b in range(2)
            ]
        )
        cross.append(exact_nt(halves[1], halves[0]) * inv[HALF:] * inv_rows[0])
    jobs = [(i, b) for i in heads for b in range(2)]
    inverse = {job: small_inverses(diag[job[0]][job[1]], rate_rows[job[0]][job[1]]) for job in jobs}
    size = BASE
    while size < HALF:
        r, c = iota((HALF, HALF), 0) // size, iota((HALF, HALF), 1) // size
        below = (r % 2 == 1) & (c == r - 1)
        part = {(i, b): jnp.where(below, diag[i][b], 0.0) for i, b in jobs}
        right = {
            (i, b): part[i, b] - mm(part[i, b] * rate_rows[i][b], inverse[i, b]) for i, b in jobs
        }
        inverse = {
            (i, b): inverse[i, b]
            + right[i, b]
            - mm(inverse[i, b] * rate_rows[i][b], right[i, b])
            for i, b in jobs
        }
        size *= 2
    right = [cross[i] - mm(cross[i] * rate_rows[i][0], inverse[i, 0]) for i in heads]
    joined = [right[i] - mm(inverse[i, 1] * rate_rows[i][1], right[i]) for i in heads]
    solved = []
    for i in heads:
        n_ref[i, :HALF, :HALF] = inverse[i, 0]
        n_ref[i, :HALF, HALF:] = jnp.zeros((HALF, HALF), F32)
        n_ref[i, HALF:, :HALF] = joined[i]
        n_ref[i, HALF:, HALF:] = inverse[i, 1]
        both = jnp.concatenate([unit[i], vals[i]], axis=1)
        top = both[:HALF] - mm(inverse[i, 0] * rate_rows[i][0], both[:HALF])
        low = jnp.concatenate(
            [joined[i] * rate_rows[i][0], inverse[i, 1] * rate_rows[i][1]], axis=1
        )
        bottom = both[HALF:] - mm(low, both)
        solved.append(jnp.concatenate([top, bottom], axis=0))
    eye = (iota((HALF, 2 * HALF), 0) == iota((HALF, 2 * HALF), 1)).astype(F32)
    sign = jnp.where(iota((HALF, 2 * HALF), 1) < HALF, -1.0, 1.0)
    for i, ts in zip(heads, (ts0, ts1, ts2, ts3)):
        w_ref[i] = solved[i][:, :HALF]
        e_ref[i] = solved[i][:, HALF:]
        ts[...] = eye + sign * mm(unit[i], rate[i] * solved[i], ta=True)


def second_kernel(
    group, q_ref, rates_ref, ku_ref, n_ref, w_ref, e_ref, qu_ref, s_ref, qc_ref, o_ref, kx_ref, qf
):
    me = lax.rem(lax.axis_index("seq"), group)
    qf[...] = q_ref[...].astype(F32)
    heads, steps = ku_ref.shape[:2]
    tokens = steps // 2
    stride = qf.shape[0] // tokens
    rates = rates_ref[...]
    seen = iota((tokens, steps), 1) <= 2 * iota((tokens, steps), 0) + 1
    for i in range(heads):
        head = me ^ i
        raw = qf[pl.ds(head, tokens, stride=stride), :]
        unit = raw * lax.rsqrt(jnp.sum(raw * raw, axis=1, keepdims=True) + EPS)
        qu_ref[i] = unit
        rate = rate_column(rates, head)
        scores = jnp.where(seen, mm(unit, ku_ref[i], tb=True), 0.0)
        s_ref[i] = scores
        weighted = rate * jnp.concatenate([w_ref[i], e_ref[i]], axis=1)
        seen_rows = mm(scores, weighted)
        qc_ref[i] = unit - seen_rows[:, :HALF]
        o_ref[i] = seen_rows[:, HALF:]
        kx_ref[i] = ku_ref[i] - mm(n_ref[i], rate * ku_ref[i], ta=True)


def join_kernel(group, p0, p1, p2, p3, starts_ref, total_ref, maps_ref):
    me = lax.rem(lax.axis_index("seq"), group)
    for i, piece in enumerate((p0, p1, p2, p3)):
        maps_ref[me ^ i] = piece[...]
    state = jnp.zeros((HALF, HALF), F32)
    for j in range(group):
        starts_ref[j] = state
        own = maps_ref[j, :, HALF:]
        state = own if j == 0 else mm(maps_ref[j, :, :HALF], state) + own
    total_ref[...] = state


def products_kernel(group, maps_ref, before_ref, after_ref):
    eye = (iota((HALF, HALF), 0) == iota((HALF, HALF), 1)).astype(F32)
    before, after = None, None
    for j in range(group + 1):
        before_ref[j] = eye if before is None else before
        if j < group:
            step = maps_ref[j, :, :HALF]
            before = step if before is None else mm(step, before)
    for j in reversed(range(group)):
        after_ref[j] = eye if after is None else after
        step = maps_ref[j, :, :HALF]
        after = step if after is None else mm(after, step)


def spread_kernel(group, transposed, entry_ref, starts_ref, maps_ref, o0, o1, o2, o3):
    me = lax.rem(lax.axis_index("seq"), group)
    entry = entry_ref[...]
    for i, out in enumerate((o0, o1, o2, o3)):
        out[...] = starts_ref[me ^ i] + mm(maps_ref[me ^ i], entry, ta=transposed)


def read_kernel(
    group,
    s0,
    s1,
    s2,
    s3,
    og_ref,
    gain_ref,
    qc_ref,
    o_ref,
    w_ref,
    e_ref,
    p0,
    p1,
    p2,
    p3,
    out_ref,
    grad_ref,
    err_ref,
    gf,
    of,
):
    me = lax.rem(lax.axis_index("seq"), group)
    gf[...] = og_ref[...].astype(F32)
    tokens = qc_ref.shape[1]
    stride = gf.shape[0] // tokens
    gain = gain_ref[...]
    gain_part = jnp.zeros((1, HALF), F32)
    for i, (state_ref, part) in enumerate(zip((s0, s1, s2, s3), (p0, p1, p2, p3))):
        head = me ^ i
        state = state_ref[...]
        read = o_ref[i] + mm(qc_ref[i], state)
        inv_rms = lax.rsqrt(jnp.mean(read * read, axis=1, keepdims=True) + EPS)
        normal = read * inv_rms
        of[pl.ds(head, tokens, stride=stride), :] = gain * normal
        given = gf[pl.ds(head, tokens, stride=stride), :]
        gain_part = gain_part + jnp.sum(given * normal, axis=0, keepdims=True)
        scaled = given * gain
        grad = inv_rms * (scaled - normal * jnp.mean(scaled * normal, axis=1, keepdims=True))
        grad_ref[i] = grad
        part[:HALF, :] = mm(qc_ref[i], grad, ta=True)
        err_ref[i] = e_ref[i] - mm(w_ref[i], state)
    for part in (p0, p1, p2, p3):
        part[HALF:, :] = jnp.broadcast_to(gain_part, (8, HALF))
    out_ref[...] = of[...].astype(BF16)


def early_kernel(
    group,
    s0,
    s1,
    s2,
    s3,
    q_ref,
    rates_ref,
    grad_ref,
    err_ref,
    qu_ref,
    ku_ref,
    sc_ref,
    n_ref,
    dq_ref,
    dk_ref,
    z_ref,
    qf,
    df,
):
    me = lax.rem(lax.axis_index("seq"), group)
    qf[...] = q_ref[...].astype(F32)
    heads, steps = ku_ref.shape[:2]
    tokens = steps // 2
    stride = qf.shape[0] // tokens
    rates = rates_ref[...]
    seen = iota((tokens, steps), 1) <= 2 * iota((tokens, steps), 0) + 1
    for i, state_ref in enumerate((s0, s1, s2, s3)):
        head = me ^ i
        rate = rate_column(rates, head)
        grad = grad_ref[i]
        unit = qu_ref[i]
        d_scores = jnp.where(seen, mm(grad, rate * err_ref[i], tb=True), 0.0)
        d_unit = mm(grad, state_ref[...], tb=True) + mm(d_scores, ku_ref[i])
        raw = qf[pl.ds(head, tokens, stride=stride), :]
        inv = lax.rsqrt(jnp.sum(raw * raw, axis=1, keepdims=True) + EPS)
        df[pl.ds(head, tokens, stride=stride), :] = inv * (
            d_unit - unit * jnp.sum(unit * d_unit, axis=1, keepdims=True)
        )
        dk_ref[i] = mm(d_scores, unit, ta=True)
        d_pseudo = mm(sc_ref[i], grad, ta=True)
        z_ref[i] = d_pseudo - mm(n_ref[i], rate * d_pseudo, ta=True)
    dq_ref[...] = df[...].astype(BF16)


def join_back_kernel(group, p0, p1, p2, p3, maps_ref, starts_ref, total_ref, parts):
    me = lax.rem(lax.axis_index("seq"), group)
    gain = jnp.zeros((8, HALF), F32)
    for i, piece in enumerate((p0, p1, p2, p3)):
        parts[me ^ i] = piece[:HALF, :]
        gain = gain + piece[HALF:, :]
    adjoint = jnp.zeros((HALF, HALF), F32)
    for j in reversed(range(group)):
        starts_ref[j] = adjoint
        own = parts[j]
        adjoint = own if j == group - 1 else mm(maps_ref[j, :, :HALF], adjoint, ta=True) + own
    total_ref[:HALF, :] = adjoint
    total_ref[HALF:, :] = gain


def last_kernel(
    group,
    a0,
    a1,
    a2,
    a3,
    s0,
    s1,
    s2,
    s3,
    k_ref,
    rates_ref,
    ku_ref,
    kx_ref,
    err_ref,
    z_ref,
    dk0_ref,
    dk_ref,
    dv_ref,
    db_ref,
    kf,
    df,
    vf,
):
    me = lax.rem(lax.axis_index("seq"), group)
    kf[...] = k_ref[...].astype(F32)
    heads, steps = ku_ref.shape[:2]
    stride = kf.shape[0] // steps
    rates = rates_ref[...]
    strict = iota((steps, steps), 1) < iota((steps, steps), 0)
    d_rates = jnp.zeros(rates.shape, F32)
    for i, (adjoint_ref, state_ref) in enumerate(zip((a0, a1, a2, a3), (s0, s1, s2, s3))):
        head = me ^ i
        adjoint, state = adjoint_ref[...], state_ref[...]
        rate = rate_column(rates, head)
        unit, err = ku_ref[i], err_ref[i]
        pseudo = rate * err
        z = z_ref[i] + mm(kx_ref[i], adjoint)
        d_value = rate * z
        d_rate = jnp.sum(z * err, axis=1, keepdims=True)
        d_rates = jnp.where(iota(rates.shape, 1) == head, d_rate, d_rates)
        vf[pl.ds(head, steps, stride=stride), :] = d_value
        d_lower = jnp.where(strict, mm(d_value, pseudo, tb=True), 0.0)
        d_unit = dk0_ref[i] + mm(pseudo, adjoint, tb=True) - mm(d_value, state, tb=True)
        d_unit = d_unit - mm(d_lower, unit) - mm(d_lower, unit, ta=True)
        raw = kf[pl.ds(head, steps, stride=stride), :]
        inv = lax.rsqrt(jnp.sum(raw * raw, axis=1, keepdims=True) + EPS)
        df[pl.ds(head, steps, stride=stride), :] = inv * (
            d_unit - unit * jnp.sum(unit * d_unit, axis=1, keepdims=True)
        )
    dk_ref[...] = df[...].astype(BF16)
    dv_ref[...] = vf[...].astype(BF16)
    db_ref[...] = d_rates


def f32(*shape):
    return jax.ShapeDtypeStruct(shape, F32)


def b16(*shape):
    return jax.ShapeDtypeStruct(shape, BF16)


def call(body, outs, *args, scratch=()):
    return pl.pallas_call(
        body,
        out_shape=outs,
        scratch_shapes=[pltpu.VMEM(s, F32) for s in scratch],
        compiler_params=pltpu.CompilerParams(vmem_limit_bytes=56 * 1024 * 1024),
    )(*args)


def swapped(pieces, group):
    count = lax.axis_size("seq")
    return [
        piece if i == 0 else lax.ppermute(piece, "seq", [(d, d ^ i) for d in range(count)])
        for i, piece in enumerate(pieces)
    ]


def local(queries, keys, values, betas, gain, out_grad):
    tokens, heads, dim = queries.shape
    substeps = keys.shape[1]
    steps = tokens * substeps
    group = GROUP
    count = lax.axis_size("seq")
    groups = count // group
    bind = functools.partial
    q2 = queries.reshape(tokens * heads, dim)
    g2 = out_grad.reshape(tokens * heads, dim)
    k2 = keys.reshape(steps * heads, dim)
    v2 = values.reshape(steps * heads, dim)
    rates = betas.reshape(steps, heads)
    gain2 = gain.reshape(1, dim)

    *maps, ku, inverse, w, e = call(
        bind(first_kernel, group),
        [f32(dim, 2 * dim)] * heads
        + [
            f32(heads, steps, dim),
            f32(heads, steps, steps),
            f32(heads, steps, dim),
            f32(heads, steps, dim),
        ],
        k2,
        v2,
        rates,
        scratch=[(steps * heads, dim)] * 2,
    )
    got = swapped(maps, group)
    qu, scores, qc, o_part, kx = call(
        bind(second_kernel, group),
        [
            f32(heads, tokens, dim),
            f32(heads, tokens, steps),
            f32(heads, tokens, dim),
            f32(heads, tokens, dim),
            f32(heads, steps, dim),
        ],
        q2,
        rates,
        ku,
        inverse,
        w,
        e,
        scratch=[(tokens * heads, dim)],
    )
    starts, total, by_place = call(
        bind(join_kernel, group),
        [f32(group, dim, dim), f32(dim, dim), f32(group, dim, 2 * dim)],
        *got,
    )
    ahead = [(d, d + group) for d in range(count - group)]
    behind = [(d + group, d) for d in range(count - group)]
    entry = lax.ppermute(total, "seq", ahead)
    before, after = call(
        bind(products_kernel, group), [f32(group + 1, dim, dim), f32(group, dim, dim)], by_place
    )
    for _ in range(groups - 2):
        passed = jnp.dot(before[group], entry, precision=lax.Precision.HIGHEST) + total
        entry = lax.ppermute(passed, "seq", ahead)
    states = call(
        bind(spread_kernel, group, False), [f32(dim, dim)] * heads, entry, starts, before
    )
    states = swapped(states, group)
    *parts, normed, o_grad, err = call(
        bind(read_kernel, group),
        [f32(dim + 8, dim)] * heads
        + [b16(tokens * heads, dim), f32(heads, tokens, dim), f32(heads, steps, dim)],
        *states,
        g2,
        gain2,
        qc,
        o_part,
        w,
        e,
        scratch=[(tokens * heads, dim)] * 2,
    )
    got_parts = swapped(parts, group)
    dq, dk0, z0 = call(
        bind(early_kernel, group),
        [b16(tokens * heads, dim), f32(heads, steps, dim), f32(heads, steps, dim)],
        *states,
        q2,
        rates,
        o_grad,
        err,
        qu,
        ku,
        scores,
        inverse,
        scratch=[(tokens * heads, dim)] * 2,
    )
    starts, total = call(
        bind(join_back_kernel, group),
        [f32(group, dim, dim), f32(dim + 8, dim)],
        *got_parts,
        by_place,
        scratch=[(group, dim, dim)],
    )
    if groups == 2:
        other = lax.ppermute(total, "seq", [(d, d ^ group) for d in range(count)])
        here = lax.axis_index("seq") < group
        entry = jnp.where(here, other[:dim], 0.0)
        gain_sum = total[dim] + other[dim]
        head_count = lax.axis_size("head")
        hops = 1
        while hops < head_count:
            gain_sum = gain_sum + lax.ppermute(
                gain_sum, "head", [(d, d ^ hops) for d in range(head_count)]
            )
            hops *= 2
    else:
        entry = lax.ppermute(total[:dim], "seq", behind)
        gain_sum = lax.psum(parts[0][dim], ("seq", "head"))
    for _ in range(groups - 2):
        passed = (
            jnp.dot(before[group].T, entry, precision=lax.Precision.HIGHEST) + total[:dim]
        )
        entry = lax.ppermute(passed, "seq", behind)
    adjoints = call(
        bind(spread_kernel, group, True), [f32(dim, dim)] * heads, entry, starts, after
    )
    adjoints = swapped(adjoints, group)
    dk, dv, db = call(
        bind(last_kernel, group),
        [b16(steps * heads, dim), b16(steps * heads, dim), f32(steps, heads)],
        *adjoints,
        *states,
        k2,
        rates,
        ku,
        kx,
        err,
        z0,
        dk0,
        scratch=[(steps * heads, dim)] * 3,
    )
    return (
        normed.reshape(tokens, heads, dim),
        dq.reshape(tokens, heads, dim),
        dk.reshape(tokens, substeps, heads, dim),
        dv.reshape(tokens, substeps, heads, dim),
        db.reshape(tokens, substeps, heads),
        gain_sum,
    )


def solution(mesh):
    return jax.shard_map(
        local,
        mesh=mesh,
        in_specs=(
            P("seq", "head", None),
            P("seq", None, "head", None),
            P("seq", None, "head", None),
            P("seq", None, "head"),
            P(),
            P("seq", "head", None),
        ),
        out_specs=(
            P("seq", "head", None),
            P("seq", "head", None),
            P("seq", None, "head", None),
            P("seq", None, "head", None),
            P("seq", None, "head"),
            P(),
        ),
        check_vma=False,
    )
```

time: 473 us -> 86 us (0.18)
  other arithmetic: 252 us -> 1.83 us
  matrix products: 55.6 us -> 0 us
  blocking collectives: 44.8 us -> 0 us
  Pallas kernels: 0 us -> 36.9 us
  waiting for transfers between devices: 46.2 us -> 15.1 us
  starting transfers between devices: 46.7 us -> 24.8 us
  between operations: 14.4 us -> 0.72 us
  local copies, waits for them, and re-layouts: 11 us -> 6.24 us
    another operation x20 -> x0, other arithmetic: 240 us -> none  [group_parts(): jax.scipy.linalg.solve_triangular(unit_lower, right_side, lower=True, uni...]
    dot_general x76 -> x0, matrix products: 49 us -> none  [the longest x8 11.4 us: compose(): jnp.einsum('hij,hjk->hik', trans_late, state_early, precision=HIGH_ACCURACY)]
    psum x1 -> x0, blocking collectives: 44.8 us -> none  [local(): gain_grad = lax.psum(gain_part, ('seq', 'head'))]
    pallas_call x0 -> x10, Pallas kernels: none -> 36.9 us  [call(): pl.pallas_call(body, out_shape=outs, scratch_shapes=[pltpu.VMEM(s, F32) f...]
    ppermute x7 -> x16, waiting for transfers between devices: 37.1 us -> 15.1 us  [the longest x12 11.4 us: swapped(): lax.ppermute(piece, 'seq', [(d, d ^ i) for d in range(count)])]
    ppermute x7 -> x16, starting transfers between devices: 46.5 us -> 24.8 us  [the longest x12 15 us: swapped(): lax.ppermute(piece, 'seq', [(d, d ^ i) for d in range(count)])]
    all_gather x2 -> x0, waiting for transfers between devices: 9.09 us -> none  [prefix(): everything = jax.tree.map(lambda part: lax.all_gather(part, axis), array)]
    another operation x10 -> x0, matrix products: 6.52 us -> none  [group_parts(): jax.scipy.linalg.solve_triangular(unit_lower, right_side, lower=True, uni...]
  transfers between devices with their start and end apart: 9 -> 16, of which waited for: 8 -> 9; matrix products, arithmetic and copies ran while one was open for 20% -> 1% of each run, Pallas kernels for 0% -> 14%
where the time goes in v1:
time: 86 us; the launch traced here: 85.6 us
  Pallas kernels  36.9 us (43%)
  starting transfers between devices  24.8 us (29%)
  waiting for transfers between devices  15.1 us (18%)
  local copies, waits for them, and re-layouts  6.24 us (7%)
  other arithmetic  1.83 us (2%)
    pallas_call x10, Pallas kernels, call(): pl.pallas_call(body, out_shape=outs, scratch_shapes=[pltpu.VMEM(s, F32) f...  36.9 us
    ppermute x12, starting transfers between devices, swapped(): lax.ppermute(piece, 'seq', [(d, d ^ i) for d in range(count)])  15 us
    ppermute x12, waiting for transfers between devices, swapped(): lax.ppermute(piece, 'seq', [(d, d ^ i) for d in range(count)])  11.4 us
    unnamed x28, local copies, waits for them, and re-layouts  6.24 us
    ppermute x1, starting transfers between devices, local(): entry = lax.ppermute(total, 'seq', ahead)  4.83 us
    ppermute x1, starting transfers between devices, local(): other = lax.ppermute(total, 'seq', [(d, d ^ group) for d in range(count)])  3.44 us
    ppermute x1, waiting for transfers between devices, local(): other = lax.ppermute(total, 'seq', [(d, d ^ group) for d in range(count)])  2.64 us
  transfers between devices with their start and end apart: 16, of which 9 were waited for; matrix products, arithmetic and copies ran while one was open for 1% of the time, Pallas kernels for 14%

profile of v1, /device:TPU:0, one launch (start us, length us, event | category | flops | bytes accessed | tf_op | source)
XLA Modules:
  0.0 85.6 jit_solution(11854703494454064401)
XLA Ops:
  0.6 1.5 %copy.12 = f32[128,2,4]{2,1,0:T(2,128)} copy(f32[128,2,4]{0,2,1:T(4,128)} %param.9) | data formatting | bytes 8192 | tf_op args[3]
  2.1 6.0 %shard_map.109 = (f32[128,256]{1,0:T(8,128)}, f32[128,256]{1,0:T(8,128)}, f32[128,256]{1,0:T(8,128)}, f32[128,256]{1,0:T(8,128)}, f32[4,256,128]{2,1,0:T(8,128)}...) custom-call(bf16[1024,128]{1,0:T(8,128)(2,1)} %bitcast.17, bf16[1024,128]{1,0:T(8,128)(2,1)} %bitcast.21, ...), custom_call_target="tpu_custom_call" | custom-call | tf_op jit(solution)/shard_map/pallas_call | solution.py:366
  8.1 3.0 %collective-permute-start = (f32[128,256]{1,0:T(8,128)}, f32[128,256]{1,0:T(8,128)S(1)}, u32[]{:S(2)}, u32[]{:S(2)}) collective-permute-start(f32[128,256]{1,0:T(8,128)} %get-tuple-element.48), channel_id=1, source_target_pairs={{0,4},{4,0},{8,12},{12,8},{16,20},{20,16},{24,28},{28,24},{1,5},{5... | collective-permute-start | bytes 393224 | tf_op jit(solution)/shard_map/ppermute | solution.py:377
  11.0 1.6 %collective-permute-start.1 = (f32[128,256]{1,0:T(8,128)}, f32[128,256]{1,0:T(8,128)S(1)}, u32[]{:S(2)}, u32[]{:S(2)}) collective-permute-start(f32[128,256]{1,0:T(8,128)} %get-tuple-element.49), channel_id=1, source_target_pairs={{0,8},{4,12},{8,0},{12,4},{16,24},{20,28},{24,16},{28,20},{1,9},{5... | collective-permute-start | bytes 393224 | tf_op jit(solution)/shard_map/ppermute | solution.py:377
  12.6 0.0 collective-permute-start.2
  12.6 2.1 %collective-permute-done.p1 = f32[128,256]{1,0:T(8,128)S(1)} collective-permute-done((f32[128,256]{1,0:T(8,128)}, f32[128,256]{1,0:T(8,128)S(1)}, u32[]{:S(2)}, u32[]{:S(2)}) %collective-permute-start) | collective-permute-done | bytes 131104 | tf_op jit(solution)/shard_map/ppermute | solution.py:377
  14.7 2.9 %collective-permute-done.1.p2 = f32[128,256]{1,0:T(8,128)S(1)} collective-permute-done((f32[128,256]{1,0:T(8,128)}, f32[128,256]{1,0:T(8,128)S(1)}, u32[]{:S(2)}, u32[]{:S(2)}) %collective-permute-start.1) | collective-permute-done | bytes 131104 | tf_op jit(solution)/shard_map/ppermute | solution.py:377
  17.6 1.2 %collective-permute-done.2.p3 = f32[128,256]{1,0:T(8,128)S(1)} collective-permute-done((f32[128,256]{1,0:T(8,128)}, f32[128,256]{1,0:T(8,128)S(1)}, u32[]{:S(2)}, u32[]{:S(2)}) %collective-permute-start.2) | collective-permute-done | bytes 131104 | tf_op jit(solution)/shard_map/ppermute | solution.py:377
  18.8 0.6 copy-done.5
  19.5 2.5 %shard_map.110 = (f32[4,128,128]{2,1,0:T(8,128)}, f32[128,128]{1,0:T(8,128)}, f32[4,128,256]{2,1,0:T(8,128)}) custom-call(f32[128,256]{1,0:T(8,128)} %get-tuple-element.47.p0, f32[128,256]{1,0:T(8,128)} %copy-done.3, f32[128,256]{1,0:T(8,128)} %copy-done.4, f32[128,256]{1,0:T(8,128)} %copy-done.5), custom_call_target="tpu_custom_call" | custom-call | tf_op jit(solution)/shard_map/pallas_call | solution.py:366
  21.9 4.8 %collective-permute-start.3 = (f32[128,128]{1,0:T(8,128)}, f32[128,128]{1,0:T(8,128)S(1)}, u32[]{:S(2)}, u32[]{:S(2)}) collective-permute-start(f32[128,128]{1,0:T(8,128)} %get-tuple-element.51), channel_id=1, source_target_pairs={{0,16},{4,20},{8,24},{12,28},{1,17},{5,21},{9,25},{13,29},{2,18},{... | collective-permute-start | bytes 196616 | tf_op jit(solution)/shard_map/ppermute | solution.py:436
  26.8 2.4 %shard_map.111 = (f32[5,128,128]{2,1,0:T(8,128)}, f32[4,128,128]{2,1,0:T(8,128)}) custom-call(f32[4,128,256]{2,1,0:T(8,128)} %get-tuple-element.53.maps_ref), custom_call_target="tpu_custom_call" | custom-call | tf_op jit(solution)/shard_map/pallas_call | solution.py:366
  29.1 0.0 collective-permute-done.3.entry_ref
  29.1 0.6 copy-done.12
  29.8 2.0 %shard_map.112 = (f32[128,128]{1,0:T(8,128)}, f32[128,128]{1,0:T(8,128)}, f32[128,128]{1,0:T(8,128)}, f32[128,128]{1,0:T(8,128)}) custom-call(f32[128,128]{1,0:T(8,128)} %copy-done.12, f32[4,128,128]{2,1,0:T(8,128)} %get-tuple-element.52.starts_ref, f32[5,128,128]{2,1,0:T(8,128)} %get-tuple-element.54.maps_ref), custom_call_target="tpu_custom_call" | custom-call | tf_op jit(solution)/shard_map/pallas_call | solution.py:366
  31.8 1.5 %collective-permute-start.4 = (f32[128,128]{1,0:T(8,128)}, f32[128,128]{1,0:T(8,128)S(1)}, u32[]{:S(2)}, u32[]{:S(2)}) collective-permute-start(f32[128,128]{1,0:T(8,128)} %get-tuple-element.56), channel_id=1, source_target_pairs={{0,4},{4,0},{8,12},{12,8},{16,20},{20,16},{24,28},{28,24},{1,5},{5... | collective-permute-start | bytes 196616 | tf_op jit(solution)/shard_map/ppermute | solution.py:377
  33.3 1.7 %collective-permute-start.5 = (f32[128,128]{1,0:T(8,128)}, f32[128,128]{1,0:T(8,128)S(1)}, u32[]{:S(2)}, u32[]{:S(2)}) collective-permute-start(f32[128,128]{1,0:T(8,128)} %get-tuple-element.57), channel_id=1, source_target_pairs={{0,8},{4,12},{8,0},{12,4},{16,24},{20,28},{24,16},{28,20},{1,9},{5... | collective-permute-start | bytes 196616 | tf_op jit(solution)/shard_map/ppermute | solution.py:377
  35.0 0.3 collective-permute-start.6
  35.3 4.2 %shard_map.113 = (f32[4,128,128]{2,1,0:T(8,128)}, f32[4,128,256]{2,1,0:T(8,128)}, f32[4,128,128]{2,1,0:T(8,128)}, f32[4,128,128]{2,1,0:T(8,128)}, f32[4,256,128]{2,1,0:T(8,128)}) custom-call(bf16[512,128]{1,0:T(8,128)(2,1)} %bitcast.19, f32[256,4]{1,0:T(8,128)} %bitcast.14, f32[4,256,128]{2,1,0:T(8,128)} %get-tuple-element.59.ku_ref, ...), custom_call_target="tpu_custom_call" | custom-call | tf_op jit(solution)/shard_map/pallas_call | solution.py:366
  39.5 0.0 collective-permute-done.4.s1
  39.5 0.8 collective-permute-done.6.s3
  40.4 0.6 copy-done.2
  41.0 4.2 %shard_map.114 = (f32[136,128]{1,0:T(8,128)}, f32[136,128]{1,0:T(8,128)}, f32[136,128]{1,0:T(8,128)}, f32[136,128]{1,0:T(8,128)}, bf16[512,128]{1,0:T(8,128)(2,1...) custom-call(f32[128,128]{1,0:T(8,128)} %get-tuple-element.55.s0, f32[128,128]{1,0:T(8,128)} %copy-done, ...), custom_call_target="tpu_custom_call" | custom-call | tf_op jit(solution)/shard_map/pallas_call | solution.py:366
  45.2 0.7 collective-permute-start.7
  45.9 1.7 %collective-permute-start.8 = (f32[136,128]{1,0:T(8,128)}, f32[136,128]{1,0:T(8,128)S(1)}, u32[]{:S(2)}, u32[]{:S(2)}) collective-permute-start(f32[136,128]{1,0:T(8,128)} %get-tuple-element.73), channel_id=1, source_target_pairs={{0,8},{4,12},{8,0},{12,4},{16,24},{20,28},{24,16},{28,20},{1,9},{5... | collective-permute-start | bytes 208904 | tf_op jit(solution)/shard_map/ppermute | solution.py:377
  47.6 1.1 %collective-permute-start.9 = (f32[136,128]{1,0:T(8,128)}, f32[136,128]{1,0:T(8,128)S(1)}, u32[]{:S(2)}, u32[]{:S(2)}) collective-permute-start(f32[136,128]{1,0:T(8,128)} %get-tuple-element.74), channel_id=1, source_target_pairs={{0,12},{4,8},{8,4},{12,0},{16,28},{20,24},{24,20},{28,16},{1,13},{... | collective-permute-start | bytes 208904 | tf_op jit(solution)/shard_map/ppermute | solution.py:377
  48.7 1.0 %collective-permute-done.7.p1 = f32[136,128]{1,0:T(8,128)S(1)} collective-permute-done((f32[136,128]{1,0:T(8,128)}, f32[136,128]{1,0:T(8,128)S(1)}, u32[]{:S(2)}, u32[]{:S(2)}) %collective-permute-start.7) | collective-permute-done | bytes 69664 | tf_op jit(solution)/shard_map/ppermute | solution.py:377
  49.7 0.7 collective-permute-done.8.p2
  50.4 2.6 %collective-permute-done.9.p3 = f32[136,128]{1,0:T(8,128)S(1)} collective-permute-done((f32[136,128]{1,0:T(8,128)}, f32[136,128]{1,0:T(8,128)S(1)}, u32[]{:S(2)}, u32[]{:S(2)}) %collective-permute-start.9) | collective-permute-done | bytes 69664 | tf_op jit(solution)/shard_map/ppermute | solution.py:377
  53.0 0.6 copy-done.8
  53.6 2.4 %shard_map.116 = (f32[4,128,128]{2,1,0:T(8,128)}, f32[136,128]{1,0:T(8,128)}) custom-call(f32[136,128]{1,0:T(8,128)} %get-tuple-element.71.p0, f32[136,128]{1,0:T(8,128)} %copy-done.6, f32[136,128]{1,0:T(8,128)} %copy-done.7, f32[136,128]{1,0:T(8,128)} %copy-done.8, f32[4,128,256]{2,1,0:T(8,128)} %get-tuple-element.53.maps_ref), custom_call_target="tpu_custom_call" | custom-call | tf_op jit(solution)/shard_map/pallas_call | solution.py:366
  56.0 3.4 %collective-permute-start.10 = (f32[136,128]{1,0:T(8,128)}, f32[136,128]{1,0:T(8,128)S(1)}, u32[]{:S(2)}, u32[]{:S(2)}) collective-permute-start(f32[136,128]{1,0:T(8,128)} %get-tuple-element.75), channel_id=1, source_target_pairs={{0,16},{4,20},{8,24},{12,28},{16,0},{20,4},{24,8},{28,12},{1,17},{... | collective-permute-start | bytes 208904 | tf_op jit(solution)/shard_map/ppermute | solution.py:483
  59.5 2.6 %collective-permute-done.10 = f32[136,128]{1,0:T(8,128)S(1)} collective-permute-done((f32[136,128]{1,0:T(8,128)}, f32[136,128]{1,0:T(8,128)S(1)}, u32[]{:S(2)}, u32[]{:S(2)}) %collective-permute-start.10) | collective-permute-done | bytes 69664 | tf_op jit(solution)/shard_map/ppermute | solution.py:483
  62.1 0.6 slice_select_fusion.entry_ref
  62.7 2.1 %shard_map.117 = (f32[128,128]{1,0:T(8,128)}, f32[128,128]{1,0:T(8,128)}, f32[128,128]{1,0:T(8,128)}, f32[128,128]{1,0:T(8,128)}) custom-call(f32[128,128]{1,0:T(8,128)} %slice_select_fusion.entry_ref, f32[4,128,128]{2,1,0:T(8,128)} %get-tuple-element.76.starts_ref, f32[4,128,128]{2,1,0:T(8,128)} %get-tuple-element.77.maps_ref), custom_call_target="tpu_custom_call" | custom-call | tf_op jit(solution)/shard_map/pallas_call | solution.py:366
  64.8 0.9 %collective-permute-start.11 = (f32[128,128]{1,0:T(8,128)}, f32[128,128]{1,0:T(8,128)S(1)}, u32[]{:S(2)}, u32[]{:S(2)}) collective-permute-start(f32[128,128]{1,0:T(8,128)} %get-tuple-element.79), channel_id=1, source_target_pairs={{0,4},{4,0},{8,12},{12,8},{16,20},{20,16},{24,28},{28,24},{1,5},{5... | collective-permute-start | bytes 196616 | tf_op jit(solution)/shard_map/ppermute | solution.py:377
  65.7 0.5 collective-permute-start.12
  66.3 2.0 %collective-permute-start.13 = (f32[128,128]{1,0:T(8,128)}, f32[128,128]{1,0:T(8,128)S(1)}, u32[]{:S(2)}, u32[]{:S(2)}) collective-permute-start(f32[128,128]{1,0:T(8,128)} %get-tuple-element.81), channel_id=1, source_target_pairs={{0,12},{4,8},{8,4},{12,0},{16,28},{20,24},{24,20},{28,16},{1,13},{... | collective-permute-start | bytes 196616 | tf_op jit(solution)/shard_map/ppermute | solution.py:377
  68.3 0.7 fusion
  69.0 1.1 %collective-permute-done.14 = f32[128]{0:T(128)S(1)} collective-permute-done((f32[128]{0:T(128)S(1)}, f32[128]{0:T(128)S(1)}, u32[]{:S(2)}, u32[]{:S(2)}) %collective-permute-start.14) | collective-permute-done | bytes 544 | tf_op jit(solution)/shard_map/ppermute | solution.py:490
  70.1 1.5 %collective-permute-start.15 = (f32[128]{0:T(128)S(1)}, f32[128]{0:T(128)S(1)}, u32[]{:S(2)}, u32[]{:S(2)}) collective-permute-start(f32[128]{0:T(128)S(1)} %add.14), channel_id=1, source_target_pairs={{0,2},{1,3},{2,0},{3,1},{4,6},{5,7},{6,4},{7,5},{8,10},{9,11},{10,... | collective-permute-start | bytes 1544 | tf_op jit(solution)/shard_map/ppermute | solution.py:490
  71.6 5.6 %shard_map.115 = (bf16[512,128]{1,0:T(8,128)(2,1)}, f32[4,256,128]{2,1,0:T(8,128)}, f32[4,256,128]{2,1,0:T(8,128)}) custom-call(f32[128,128]{1,0:T(8,128)} %get-tuple-element.55.s0, f32[128,128]{1,0:T(8,128)} %copy-done, f32[128,128]{1,0:T(8,128)} %copy-done.1, f32[128,128]{1,0:T(8,128)} %copy-done.2, bf16[512,128]{1,0:T(8,128)(2,1)} %bitcast.20, ...), custom_call_target="tpu_custom_call" | custom-call | tf_op jit(solution)/shard_map/pallas_call | solution.py:366
  77.1 0.5 add.15
  77.7 0.6 copy-done.9
  78.3 0.0 copy-done.10
  78.3 0.0 copy-done.11
  78.3 5.7 %shard_map.118 = (bf16[1024,128]{1,0:T(8,128)(2,1)}, bf16[1024,128]{1,0:T(8,128)(2,1)}, f32[256,4]{1,0:T(8,128)}) custom-call(f32[128,128]{1,0:T(8,128)} %get-tuple-element.78.a0, f32[128,128]{1,0:T(8,128)} %copy-done.9, f32[128,128]{1,0:T(8,128)} %copy-done.10, f32[128,128]{1,0:T(8,128)} %copy-done.11, f32[128,128]{1,0:T(8,128)} %get-tuple-element.55.s0, ...), custom_call_target="tpu_custom_call" | custom-call | tf_op jit(solution)/shard_map/pallas_call | solution.py:366
  84.0 1.6 %copy.13 = f32[128,2,4]{0,2,1:T(4,128)} copy(f32[128,2,4]{2,1,0:T(2,128)} %bitcast.23) | data formatting | bytes 8192
  (26 shorter events, 0.1 us)
Async XLA Ops:
  8.1 6.7 %collective-permute-start = (f32[128,256]{1,0:T(8,128)}, f32[128,256]{1,0:T(8,128)S(1)}, u32[]{:S(2)}, u32[]{:S(2)}) collective-permute-start(f32[128,256]{1,0:T(8,128)} %get-tuple-element.48), channel_id=1, source_target_pairs={{0,4},{4,0},{8,12},{12,8},{16,20},{20,16},{24,28},{28,24},{1,5},{5... | collective-permute-start | bytes 393224 | tf_op jit(solution)/shard_map/ppermute | solution.py:377
  11.0 6.6 %collective-permute-start.1 = (f32[128,256]{1,0:T(8,128)}, f32[128,256]{1,0:T(8,128)S(1)}, u32[]{:S(2)}, u32[]{:S(2)}) collective-permute-start(f32[128,256]{1,0:T(8,128)} %get-tuple-element.49), channel_id=1, source_target_pairs={{0,8},{4,12},{8,0},{12,4},{16,24},{20,28},{24,16},{28,20},{1,9},{5... | collective-permute-start | bytes 393224 | tf_op jit(solution)/shard_map/ppermute | solution.py:377
  12.6 6.2 %collective-permute-start.2 = (f32[128,256]{1,0:T(8,128)}, f32[128,256]{1,0:T(8,128)S(1)}, u32[]{:S(2)}, u32[]{:S(2)}) collective-permute-start(f32[128,256]{1,0:T(8,128)} %get-tuple-element.50), channel_id=1, source_target_pairs={{0,12},{4,8},{8,4},{12,0},{16,28},{20,24},{24,20},{28,16},{1,13},{... | collective-permute-start | bytes 393224 | tf_op jit(solution)/shard_map/ppermute | solution.py:377
  14.7 4.1 %copy-start.3 = (f32[128,256]{1,0:T(8,128)}, f32[128,256]{1,0:T(8,128)S(1)}, u32[]{:S(2)}) copy-start(f32[128,256]{1,0:T(8,128)S(1)} %collective-permute-done.p1) | copy-start | bytes 393220
  17.6 1.2 %copy-start.4 = (f32[128,256]{1,0:T(8,128)}, f32[128,256]{1,0:T(8,128)S(1)}, u32[]{:S(2)}) copy-start(f32[128,256]{1,0:T(8,128)S(1)} %collective-permute-done.1.p2) | copy-start | bytes 393220
  18.8 0.7 copy-start.5
  21.9 7.2 %collective-permute-start.3 = (f32[128,128]{1,0:T(8,128)}, f32[128,128]{1,0:T(8,128)S(1)}, u32[]{:S(2)}, u32[]{:S(2)}) collective-permute-start(f32[128,128]{1,0:T(8,128)} %get-tuple-element.51), channel_id=1, source_target_pairs={{0,16},{4,20},{8,24},{12,28},{1,17},{5,21},{9,25},{13,29},{2,18},{... | collective-permute-start | bytes 196616 | tf_op jit(solution)/shard_map/ppermute | solution.py:436
  29.1 0.6 copy-start.12
  31.8 7.7 %collective-permute-start.4 = (f32[128,128]{1,0:T(8,128)}, f32[128,128]{1,0:T(8,128)S(1)}, u32[]{:S(2)}, u32[]{:S(2)}) collective-permute-start(f32[128,128]{1,0:T(8,128)} %get-tuple-element.56), channel_id=1, source_target_pairs={{0,4},{4,0},{8,12},{12,8},{16,20},{20,16},{24,28},{28,24},{1,5},{5... | collective-permute-start | bytes 196616 | tf_op jit(solution)/shard_map/ppermute | solution.py:377
  33.3 6.2 %collective-permute-start.5 = (f32[128,128]{1,0:T(8,128)}, f32[128,128]{1,0:T(8,128)S(1)}, u32[]{:S(2)}, u32[]{:S(2)}) collective-permute-start(f32[128,128]{1,0:T(8,128)} %get-tuple-element.57), channel_id=1, source_target_pairs={{0,8},{4,12},{8,0},{12,4},{16,24},{20,28},{24,16},{28,20},{1,9},{5... | collective-permute-start | bytes 196616 | tf_op jit(solution)/shard_map/ppermute | solution.py:377
  35.0 5.4 %collective-permute-start.6 = (f32[128,128]{1,0:T(8,128)}, f32[128,128]{1,0:T(8,128)S(1)}, u32[]{:S(2)}, u32[]{:S(2)}) collective-permute-start(f32[128,128]{1,0:T(8,128)} %get-tuple-element.58), channel_id=1, source_target_pairs={{0,12},{4,8},{8,4},{12,0},{16,28},{20,24},{24,20},{28,16},{1,13},{... | collective-permute-start | bytes 196616 | tf_op jit(solution)/shard_map/ppermute | solution.py:377
  39.5 0.9 copy-start
  39.5 0.8 copy-start.1
  40.4 0.6 copy-start.2
  45.2 4.5 %collective-permute-start.7 = (f32[136,128]{1,0:T(8,128)}, f32[136,128]{1,0:T(8,128)S(1)}, u32[]{:S(2)}, u32[]{:S(2)}) collective-permute-start(f32[136,128]{1,0:T(8,128)} %get-tuple-element.72), channel_id=1, source_target_pairs={{0,4},{4,0},{8,12},{12,8},{16,20},{20,16},{24,28},{28,24},{1,5},{5... | collective-permute-start | bytes 208904 | tf_op jit(solution)/shard_map/ppermute | solution.py:377
  45.9 4.5 %collective-permute-start.8 = (f32[136,128]{1,0:T(8,128)}, f32[136,128]{1,0:T(8,128)S(1)}, u32[]{:S(2)}, u32[]{:S(2)}) collective-permute-start(f32[136,128]{1,0:T(8,128)} %get-tuple-element.73), channel_id=1, source_target_pairs={{0,8},{4,12},{8,0},{12,4},{16,24},{20,28},{24,16},{28,20},{1,9},{5... | collective-permute-start | bytes 208904 | tf_op jit(solution)/shard_map/ppermute | solution.py:377
  47.6 5.4 %collective-permute-start.9 = (f32[136,128]{1,0:T(8,128)}, f32[136,128]{1,0:T(8,128)S(1)}, u32[]{:S(2)}, u32[]{:S(2)}) collective-permute-start(f32[136,128]{1,0:T(8,128)} %get-tuple-element.74), channel_id=1, source_target_pairs={{0,12},{4,8},{8,4},{12,0},{16,28},{20,24},{24,20},{28,16},{1,13},{... | collective-permute-start | bytes 208904 | tf_op jit(solution)/shard_map/ppermute | solution.py:377
  49.7 3.3 %copy-start.6 = (f32[136,128]{1,0:T(8,128)}, f32[136,128]{1,0:T(8,128)S(1)}, u32[]{:S(2)}) copy-start(f32[136,128]{1,0:T(8,128)S(1)} %collective-permute-done.7.p1) | copy-start | bytes 208900
  50.4 2.6 %copy-start.7 = (f32[136,128]{1,0:T(8,128)}, f32[136,128]{1,0:T(8,128)S(1)}, u32[]{:S(2)}) copy-start(f32[136,128]{1,0:T(8,128)S(1)} %collective-permute-done.8.p2) | copy-start | bytes 208900
  53.0 0.6 copy-start.8
  56.0 6.1 %collective-permute-start.10 = (f32[136,128]{1,0:T(8,128)}, f32[136,128]{1,0:T(8,128)S(1)}, u32[]{:S(2)}, u32[]{:S(2)}) collective-permute-start(f32[136,128]{1,0:T(8,128)} %get-tuple-element.75), channel_id=1, source_target_pairs={{0,16},{4,20},{8,24},{12,28},{16,0},{20,4},{24,8},{28,12},{1,17},{... | collective-permute-start | bytes 208904 | tf_op jit(solution)/shard_map/ppermute | solution.py:483
  64.8 12.9 %collective-permute-start.11 = (f32[128,128]{1,0:T(8,128)}, f32[128,128]{1,0:T(8,128)S(1)}, u32[]{:S(2)}, u32[]{:S(2)}) collective-permute-start(f32[128,128]{1,0:T(8,128)} %get-tuple-element.79), channel_id=1, source_target_pairs={{0,4},{4,0},{8,12},{12,8},{16,20},{20,16},{24,28},{28,24},{1,5},{5... | collective-permute-start | bytes 196616 | tf_op jit(solution)/shard_map/ppermute | solution.py:377
  65.7 11.9 %collective-permute-start.12 = (f32[128,128]{1,0:T(8,128)}, f32[128,128]{1,0:T(8,128)S(1)}, u32[]{:S(2)}, u32[]{:S(2)}) collective-permute-start(f32[128,128]{1,0:T(8,128)} %get-tuple-element.80), channel_id=1, source_target_pairs={{0,8},{4,12},{8,0},{12,4},{16,24},{20,28},{24,16},{28,20},{1,9},{5... | collective-permute-start | bytes 196616 | tf_op jit(solution)/shard_map/ppermute | solution.py:377
  66.3 11.4 %collective-permute-start.13 = (f32[128,128]{1,0:T(8,128)}, f32[128,128]{1,0:T(8,128)S(1)}, u32[]{:S(2)}, u32[]{:S(2)}) collective-permute-start(f32[128,128]{1,0:T(8,128)} %get-tuple-element.81), channel_id=1, source_target_pairs={{0,12},{4,8},{8,4},{12,0},{16,28},{20,24},{24,20},{28,16},{1,13},{... | collective-permute-start | bytes 196616 | tf_op jit(solution)/shard_map/ppermute | solution.py:377
  69.0 1.1 %collective-permute-start.14 = (f32[128]{0:T(128)S(1)}, f32[128]{0:T(128)S(1)}, u32[]{:S(2)}, u32[]{:S(2)}) collective-permute-start(f32[128]{0:T(128)S(1)} %fusion), channel_id=1, source_target_pairs={{0,1},{1,0},{2,3},{3,2},{4,5},{5,4},{6,7},{7,6},{8,9},{9,8},{10,11... | collective-permute-start | bytes 1544 | tf_op jit(solution)/shard_map/ppermute | solution.py:490
  70.1 7.1 %collective-permute-start.15 = (f32[128]{0:T(128)S(1)}, f32[128]{0:T(128)S(1)}, u32[]{:S(2)}, u32[]{:S(2)}) collective-permute-start(f32[128]{0:T(128)S(1)} %add.14), channel_id=1, source_target_pairs={{0,2},{1,3},{2,0},{3,1},{4,6},{5,7},{6,4},{7,5},{8,10},{9,11},{10,... | collective-permute-start | bytes 1544 | tf_op jit(solution)/shard_map/ppermute | solution.py:490
  77.7 0.6 copy-start.9
  77.7 0.6 copy-start.10
  77.7 0.6 copy-start.11

commit v2 on v1

--- a/solution.py
+++ b/solution.py
@@ -33,6 +33,18 @@
 def row_of(column):
     square = jnp.where(iota((HALF, HALF), 0) == iota((HALF, HALF), 1), column, 0.0)
     return jnp.sum(square, axis=0, keepdims=True)
+
+
+def places(steps, j):
+    shape = (steps, steps // 2)
+    return (iota(shape, 0) == 2 * iota(shape, 1) + j).astype(F32)
+
+
+def pick(a, b, ta=False, tb=False):
+    dims = (((0 if ta else 1,), (1 if tb else 0,)), ((), ()))
+    return lax.dot_general(
+        a, b, dims, precision=lax.Precision.HIGHEST, preferred_element_type=F32
+    )
 
 
 def rate_column(rates, head):
@@ -57,27 +69,54 @@
 
 
 def first_kernel(
-    group, k_ref, v_ref, rates_ref, ts0, ts1, ts2, ts3, ku_ref, n_ref, w_ref, e_ref, kf, vf
+    group,
+    k_ref,
+    v_ref,
+    packed_ref,
+    ts0,
+    ts1,
+    ts2,
+    ts3,
+    ku_ref,
+    n_ref,
+    w_ref,
+    e_ref,
+    rates_ref,
+    k16,
+    v16,
+    kf,
+    vf,
+    rows,
+    sems,
 ):
-    me = lax.rem(lax.axis_index("seq"), group)
-    kf[...] = k_ref[...].astype(F32)
-    vf[...] = v_ref[...].astype(F32)
+    copies = [
+        pltpu.make_async_copy(k_ref, k16, sems.at[0]),
+        pltpu.make_async_copy(v_ref, v16, sems.at[1]),
+    ]
+    for copy in copies:
+        copy.start()
+    me = lax.rem(lax.axis_index("seq"), group)
     heads = range(len((ts0, ts1, ts2, ts3)))
     steps = rates_ref.shape[0]
     stride = kf.shape[0] // steps
-    rates = rates_ref[...]
+    packed = packed_ref[...]
+    own, place = [packed[: len(heads)], packed[len(heads) :]], [places(steps, j) for j in range(2)]
+    rates = pick(place[0], own[0], tb=True) + pick(place[1], own[1], tb=True)
+    rates_ref[...] = rates
+    rows[...] = pick(own[0], place[0], tb=True) + pick(own[1], place[1], tb=True)
     strict = iota((HALF, HALF), 1) < iota((HALF, HALF), 0)
     unit, vals, rate, rate_rows, diag, cross = [], [], [], [], [], []
+    copies[0].wait()
+    kf[...] = k16[...].astype(F32)
     for i in heads:
         head = me ^ i
         raw = kf[pl.ds(head, steps, stride=stride), :]
         inv = lax.rsqrt(jnp.sum(raw * raw, axis=1, keepdims=True) + EPS)
-        column = rate_column(rates, head)
         unit.append(raw * inv)
         ku_ref[i] = unit[i]
-        vals.append(vf[pl.ds(head, steps, stride=stride), :])
-        rate.append(column)
-        rate_rows.append([row_of(column[:HALF]), row_of(column[HALF:])])
+        rate.append(rate_column(rates, head))
+        rate_row = rows[pl.ds(head, 1), :]
+        rate_rows.append([rate_row[:, :HALF], rate_row[:, HALF:]])
         inv_rows = [row_of(inv[:HALF]), row_of(inv[HALF:])]
         raw16 = raw.astype(BF16)
         halves = [raw16[:HALF], raw16[HALF:]]
@@ -114,7 +153,10 @@
     right = [cross[i] - mm(cross[i] * rate_rows[i][0], inverse[i, 0]) for i in heads]
     joined = [right[i] - mm(inverse[i, 1] * rate_rows[i][1], right[i]) for i in heads]
     solved = []
+    copies[1].wait()
+    vf[...] = v16[...].astype(F32)
     for i in heads:
+        vals.append(vf[pl.ds(me ^ i, steps, stride=stride), :])
         n_ref[i, :HALF, :HALF] = inverse[i, 0]
         n_ref[i, :HALF, HALF:] = jnp.zeros((HALF, HALF), F32)
         n_ref[i, HALF:, :HALF] = joined[i]
@@ -185,11 +227,19 @@
         after = step if after is None else mm(after, step)
 
 
-def spread_kernel(group, transposed, entry_ref, starts_ref, maps_ref, o0, o1, o2, o3):
-    me = lax.rem(lax.axis_index("seq"), group)
-    entry = entry_ref[...]
-    for i, out in enumerate((o0, o1, o2, o3)):
-        out[...] = starts_ref[me ^ i] + mm(maps_ref[me ^ i], entry, ta=transposed)
+def spread_kernel(group, side, transposed, other_ref, starts_ref, maps_ref, *outs):
+    me = lax.rem(lax.axis_index("seq"), group)
+    entry = other_ref[:HALF, :]
+    if side is not None:
+        entry = jnp.where(lax.axis_index("seq") // group == side, entry, 0.0)
+    for i, out in enumerate(outs):
+        out[:HALF, :] = starts_ref[me ^ i] + mm(maps_ref[me ^ i], entry, ta=transposed)
+
+
+def spread_back_kernel(group, side, other_ref, starts_ref, maps_ref, gain_ref, *outs):
+    spread_kernel(group, side, True, other_ref, starts_ref, maps_ref, *outs)
+    for out in outs:
+        out[HALF:, :] = gain_ref[...] + other_ref[HALF:, :]
 
 
 def read_kernel(
@@ -211,6 +261,7 @@
     out_ref,
     grad_ref,
     err_ref,
+    gain_part_ref,
     gf,
     of,
 ):
@@ -232,10 +283,9 @@
         scaled = given * gain
         grad = inv_rms * (scaled - normal * jnp.mean(scaled * normal, axis=1, keepdims=True))
         grad_ref[i] = grad
-        part[:HALF, :] = mm(qc_ref[i], grad, ta=True)
+        part[...] = mm(qc_ref[i], grad, ta=True)
         err_ref[i] = e_ref[i] - mm(w_ref[i], state)
-    for part in (p0, p1, p2, p3):
-        part[HALF:, :] = jnp.broadcast_to(gain_part, (8, HALF))
+    gain_part_ref[...] = jnp.broadcast_to(gain_part, (8, HALF))
     out_ref[...] = of[...].astype(BF16)
 
 
@@ -284,19 +334,17 @@
     dq_ref[...] = df[...].astype(BF16)
 
 
-def join_back_kernel(group, p0, p1, p2, p3, maps_ref, starts_ref, total_ref, parts):
-    me = lax.rem(lax.axis_index("seq"), group)
-    gain = jnp.zeros((8, HALF), F32)
+def join_back_kernel(group, p0, p1, p2, p3, maps_ref, gain_ref, starts_ref, total_ref, parts):
+    me = lax.rem(lax.axis_index("seq"), group)
     for i, piece in enumerate((p0, p1, p2, p3)):
-        parts[me ^ i] = piece[:HALF, :]
-        gain = gain + piece[HALF:, :]
+        parts[me ^ i] = piece[...]
     adjoint = jnp.zeros((HALF, HALF), F32)
     for j in reversed(range(group)):
         starts_ref[j] = adjoint
         own = parts[j]
         adjoint = own if j == group - 1 else mm(maps_ref[j, :, :HALF], adjoint, ta=True) + own
     total_ref[:HALF, :] = adjoint
-    total_ref[HALF:, :] = gain
+    total_ref[HALF:, :] = gain_ref[...]
 
 
 def last_kernel(
@@ -319,6 +367,7 @@
     dk_ref,
     dv_ref,
     db_ref,
+    gain_ref,
     kf,
     df,
     vf,
@@ -332,7 +381,7 @@
     d_rates = jnp.zeros(rates.shape, F32)
     for i, (adjoint_ref, state_ref) in enumerate(zip((a0, a1, a2, a3), (s0, s1, s2, s3))):
         head = me ^ i
-        adjoint, state = adjoint_ref[...], state_ref[...]
+        adjoint, state = adjoint_ref[:HALF, :], state_ref[...]
         rate = rate_column(rates, head)
         unit, err = ku_ref[i], err_ref[i]
         pseudo = rate * err
@@ -351,32 +400,35 @@
         )
     dk_ref[...] = df[...].astype(BF16)
     dv_ref[...] = vf[...].astype(BF16)
-    db_ref[...] = d_rates
+    for j in range(2):
+        db_ref[j * heads : (j + 1) * heads, :] = pick(d_rates, places(steps, j), ta=True)
+    gain_ref[...] = a0[HALF:, :] + a1[HALF:, :] + a2[HALF:, :] + a3[HALF:, :]
 
 
 def f32(*shape):
-    return jax.ShapeDtypeStruct(shape, F32)
-
-
-def b16(*shape):
-    return jax.ShapeDtypeStruct(shape, BF16)
-
-
-def call(body, outs, *args, scratch=()):
+    return pltpu.VMEM(shape, F32)
+
+
+def out(dtype, *shape):
+    return jax.ShapeDtypeStruct(shape, dtype)
+
+
+def call(body, outs, *args, scratch=(), specs=None):
     return pl.pallas_call(
         body,
         out_shape=outs,
-        scratch_shapes=[pltpu.VMEM(s, F32) for s in scratch],
-        compiler_params=pltpu.CompilerParams(vmem_limit_bytes=56 * 1024 * 1024),
+        in_specs=specs or [pl.BlockSpec(memory_space=pltpu.VMEM)] * len(args),
+        scratch_shapes=[pltpu.VMEM(s, F32) if isinstance(s, tuple) else s for s in scratch],
+        compiler_params=pltpu.CompilerParams(vmem_limit_bytes=16 * 1024 * 1024),
     )(*args)
 
 
-def swapped(pieces, group):
+def swapped(pieces, group, order=(3, 2, 1)):
     count = lax.axis_size("seq")
-    return [
-        piece if i == 0 else lax.ppermute(piece, "seq", [(d, d ^ i) for d in range(count)])
-        for i, piece in enumerate(pieces)
-    ]
+    got = list(pieces)
+    for i in order:
+        got[i] = lax.ppermute(pieces[i], "seq", [(d, d ^ i) for d in range(count)])
+    return got
 
 
 def local(queries, keys, values, betas, gain, out_grad):
@@ -391,10 +443,11 @@
     g2 = out_grad.reshape(tokens * heads, dim)
     k2 = keys.reshape(steps * heads, dim)
     v2 = values.reshape(steps * heads, dim)
-    rates = betas.reshape(steps, heads)
+    packed = betas.transpose(1, 2, 0).reshape(substeps * heads, tokens)
     gain2 = gain.reshape(1, dim)
-
-    *maps, ku, inverse, w, e = call(
+    in_hbm = pl.BlockSpec(memory_space=pltpu.HBM)
+
+    *maps, ku, inverse, w, e, rates = call(
         bind(first_kernel, group),
         [f32(dim, 2 * dim)] * heads
         + [
@@ -402,13 +455,17 @@
             f32(heads, steps, steps),
             f32(heads, steps, dim),
             f32(heads, steps, dim),
+            f32(steps, heads),
         ],
-        k2,
-        v2,
-        rates,
-        scratch=[(steps * heads, dim)] * 2,
-    )
-    got = swapped(maps, group)
+        pltpu.with_memory_space_constraint(k2, pltpu.HBM),
+        pltpu.with_memory_space_constraint(v2, pltpu.HBM),
+        packed,
+        specs=[in_hbm, in_hbm, pl.BlockSpec(memory_space=pltpu.VMEM)],
+        scratch=[pltpu.VMEM((steps * heads, dim), BF16)] * 2
+        + [(steps * heads, dim)] * 2
+        + [(heads, steps), pltpu.SemaphoreType.DMA((2,))],
+    )
+    got = swapped(maps, group, (1, 2, 3))
     qu, scores, qc, o_part, kx = call(
         bind(second_kernel, group),
         [
@@ -433,7 +490,9 @@
     )
     ahead = [(d, d + group) for d in range(count - group)]
     behind = [(d + group, d) for d in range(count - group)]
-    entry = lax.ppermute(total, "seq", ahead)
+    across = [(d, d ^ group) for d in range(count)]
+    two = groups == 2
+    entry = lax.ppermute(total, "seq", across if two else ahead)
     before, after = call(
         bind(products_kernel, group), [f32(group + 1, dim, dim), f32(group, dim, dim)], by_place
     )
@@ -441,13 +500,22 @@
         passed = jnp.dot(before[group], entry, precision=lax.Precision.HIGHEST) + total
         entry = lax.ppermute(passed, "seq", ahead)
     states = call(
-        bind(spread_kernel, group, False), [f32(dim, dim)] * heads, entry, starts, before
+        bind(spread_kernel, group, 1 if two else None, False),
+        [f32(dim, dim)] * heads,
+        entry,
+        starts,
+        before,
     )
     states = swapped(states, group)
-    *parts, normed, o_grad, err = call(
+    *parts, normed, o_grad, err, gain_part = call(
         bind(read_kernel, group),
-        [f32(dim + 8, dim)] * heads
-        + [b16(tokens * heads, dim), f32(heads, tokens, dim), f32(heads, steps, dim)],
+        [f32(dim, dim)] * heads
+        + [
+            out(BF16, tokens * heads, dim),
+            f32(heads, tokens, dim),
+            f32(heads, steps, dim),
+            f32(8, dim),
+        ],
         *states,
         g2,
         gain2,
@@ -458,9 +526,16 @@
         scratch=[(tokens * heads, dim)] * 2,
     )
     got_parts = swapped(parts, group)
+    head_count = lax.axis_size("head")
+    hops = 1
+    while two and hops < head_count:
+        gain_part = gain_part + lax.ppermute(
+            gain_part, "head", [(d, d ^ hops) for d in range(head_count)]
+        )
+        hops *= 2
     dq, dk0, z0 = call(
         bind(early_kernel, group),
-        [b16(tokens * heads, dim), f32(heads, steps, dim), f32(heads, steps, dim)],
+        [out(BF16, tokens * heads, dim), f32(heads, steps, dim), f32(heads, steps, dim)],
         *states,
         q2,
         rates,
@@ -477,35 +552,32 @@
         [f32(group, dim, dim), f32(dim + 8, dim)],
         *got_parts,
         by_place,
+        gain_part,
         scratch=[(group, dim, dim)],
     )
-    if groups == 2:
-        other = lax.ppermute(total, "seq", [(d, d ^ group) for d in range(count)])
-        here = lax.axis_index("seq") < group
-        entry = jnp.where(here, other[:dim], 0.0)
-        gain_sum = total[dim] + other[dim]
-        head_count = lax.axis_size("head")
-        hops = 1
-        while hops < head_count:
-            gain_sum = gain_sum + lax.ppermute(
-                gain_sum, "head", [(d, d ^ hops) for d in range(head_count)]
-            )
-            hops *= 2
-    else:
-        entry = lax.ppermute(total[:dim], "seq", behind)
-        gain_sum = lax.psum(parts[0][dim], ("seq", "head"))
+    entry = lax.ppermute(total, "seq", across if two else behind)
     for _ in range(groups - 2):
         passed = (
-            jnp.dot(before[group].T, entry, precision=lax.Precision.HIGHEST) + total[:dim]
+            jnp.dot(before[group].T, entry[:dim], precision=lax.Precision.HIGHEST) + total[:dim]
         )
-        entry = lax.ppermute(passed, "seq", behind)
+        entry = lax.ppermute(jnp.pad(passed, ((0, 8), (0, 0))), "seq", behind)
     adjoints = call(
-        bind(spread_kernel, group, True), [f32(dim, dim)] * heads, entry, starts, after
+        bind(spread_back_kernel, group, 0 if two else None),
+        [f32(dim + 8, dim)] * heads,
+        entry,
+        starts,
+        after,
+        gain_part,
     )
     adjoints = swapped(adjoints, group)
-    dk, dv, db = call(
+    dk, dv, db, gain_sum = call(
         bind(last_kernel, group),
-        [b16(steps * heads, dim), b16(steps * heads, dim), f32(steps, heads)],
+        [
+            out(BF16, steps * heads, dim),
+            out(BF16, steps * heads, dim),
+            out(F32, substeps * heads, tokens),
+            out(F32, 8, dim),
+        ],
         *adjoints,
         *states,
         k2,
@@ -517,12 +589,13 @@
         dk0,
         scratch=[(steps * heads, dim)] * 3,
     )
+    gain_sum = gain_sum[0] if two else lax.psum(gain_part[0], ("seq", "head"))
     return (
         normed.reshape(tokens, heads, dim),
         dq.reshape(tokens, heads, dim),
         dk.reshape(tokens, substeps, heads, dim),
         dv.reshape(tokens, substeps, heads, dim),
-        db.reshape(tokens, substeps, heads),
+        db.reshape(substeps, heads, tokens).transpose(2, 0, 1),
         gain_sum,
     )
 

time: 86 us -> 60.5 us (0.70)
  Pallas kernels: 36.9 us -> 17.7 us
  local copies, waits for them, and re-layouts: 6.24 us -> 1.86 us
  waiting for transfers between devices: 15.1 us -> 17.2 us
  starting transfers between devices: 24.8 us -> 22.8 us
  other arithmetic: 1.83 us -> 0.01 us
    pallas_call x10, Pallas kernels: 36.9 us -> 17.7 us  [call(): pl.pallas_call(body, out_shape=outs, in_specs=specs or [pl.BlockSpec(memo...]
    unnamed x28 -> x10, local copies, waits for them, and re-layouts: 6.24 us -> 1.34 us
    ppermute x16, waiting for transfers between devices: 15.1 us -> 17.2 us  [the longest x12 9.42 us: swapped(): got[i] = lax.ppermute(pieces[i], 'seq', [(d, d ^ i) for d in range(count)])]
    ppermute x16, starting transfers between devices: 24.8 us -> 22.8 us  [the longest x12 15.2 us: swapped(): got[i] = lax.ppermute(pieces[i], 'seq', [(d, d ^ i) for d in range(count)])]
    add x3 -> x2, other arithmetic: 1.2 us -> 0.01 us  [local(): gain_part + lax.ppermute(gain_part, 'head', [(d, d ^ hops) for d in range...]
  transfers between devices with their start and end apart: 16 -> 16, of which waited for: 9 -> 9; matrix products, arithmetic and copies ran while one was open for 1% -> 0% of each run, Pallas kernels for 14% -> 8%
where the time goes in v2:
time: 60.5 us; the launch traced here: 60.3 us
  starting transfers between devices  22.8 us (38%)
  Pallas kernels  17.7 us (29%)
  waiting for transfers between devices  17.2 us (28%)
  local copies, waits for them, and re-layouts  1.86 us (3%)
  between operations  0.75 us (1%)
    pallas_call x10, Pallas kernels, call(): pl.pallas_call(body, out_shape=outs, in_specs=specs or [pl.BlockSpec(memo...  17.7 us
    ppermute x12, starting transfers between devices, swapped(): got[i] = lax.ppermute(pieces[i], 'seq', [(d, d ^ i) for d in range(count)])  15.2 us
    ppermute x12, waiting for transfers between devices, swapped(): got[i] = lax.ppermute(pieces[i], 'seq', [(d, d ^ i) for d in range(count)])  9.42 us
    ppermute x2, waiting for transfers between devices, local(): lax.ppermute(gain_part, 'head', [(d, d ^ hops) for d in range(head_count)])  3.28 us
    ppermute x1, starting transfers between devices, local(): entry = lax.ppermute(total, 'seq', across if two else behind)  3.24 us
    ppermute x1, starting transfers between devices, local(): entry = lax.ppermute(total, 'seq', across if two else ahead)  2.81 us
    ppermute x1, waiting for transfers between devices, local(): entry = lax.ppermute(total, 'seq', across if two else behind)  2.66 us
    ppermute x1, waiting for transfers between devices, local(): entry = lax.ppermute(total, 'seq', across if two else ahead)  1.85 us
  transfers between devices with their start and end apart: 16, of which 9 were waited for; matrix products, arithmetic and copies ran while one was open for 0% of the time, Pallas kernels for 8%

profile of v2, /device:TPU:0, one launch (start us, length us, event | category | flops | bytes accessed | tf_op | source)
XLA Modules:
  0.0 60.3 jit_solution(4606853528804619790)
XLA Ops:
  0.6 0.0 copy-start.3
  0.6 0.7 %copy-done.3 = f32[128,2,4]{0,2,1:T(4,128)S(1)} copy-done((f32[128,2,4]{0,2,1:T(4,128)S(1)}, f32[128,2,4]{0,2,1:T(4,128)}, u32[]{:S(2)}) %copy-start.3) | copy-done | bytes 4120
  1.3 4.9 %shard_map.109 = (f32[128,256]{1,0:T(8,128)S(1)}, f32[128,256]{1,0:T(8,128)S(1)}, f32[128,256]{1,0:T(8,128)S(1)}, f32[128,256]{1,0:T(8,128)S(1)}, f32[4,256,128]...) custom-call(bf16[1024,128]{1,0:T(8,128)(2,1)} %bitcast.17, ...), custom_call_target="tpu_custom_call" | custom-call | tf_op jit(solution)/shard_map/pallas_call | solution.py:417
  6.2 3.0 %collective-permute-start = (f32[128,256]{1,0:T(8,128)S(1)}, f32[128,256]{1,0:T(8,128)S(1)}, u32[]{:S(2)}, u32[]{:S(2)}) collective-permute-start(f32[128,256]{1,0:T(8,128)S(1)} %get-tuple-element.51), channel_id=1, source_target_pairs={{0,4},{4,0},{8,12},{12,8},{16,20},{20,16},{24,28},{28,24},{1,5},{5... | collective-permute-start | bytes 393224 | tf_op jit(solution)/shard_map/ppermute | solution.py:430
  9.2 1.6 %collective-permute-start.1 = (f32[128,256]{1,0:T(8,128)S(1)}, f32[128,256]{1,0:T(8,128)S(1)}, u32[]{:S(2)}, u32[]{:S(2)}) collective-permute-start(f32[128,256]{1,0:T(8,128)S(1)} %get-tuple-element.52), channel_id=1, source_target_pairs={{0,8},{4,12},{8,0},{12,4},{16,24},{20,28},{24,16},{28,20},{1,9},{5... | collective-permute-start | bytes 393224 | tf_op jit(solution)/shard_map/ppermute | solution.py:430
  10.8 0.0 collective-permute-start.2
  10.8 1.9 %collective-permute-done.p1 = f32[128,256]{1,0:T(8,128)S(1)} collective-permute-done((f32[128,256]{1,0:T(8,128)S(1)}, f32[128,256]{1,0:T(8,128)S(1)}, u32[]{:S(2)}, u32[]{:S(2)}) %collective-permute-start) | collective-permute-done | bytes 131104 | tf_op jit(solution)/shard_map/ppermute | solution.py:430
  12.7 2.9 %collective-permute-done.1.p2 = f32[128,256]{1,0:T(8,128)S(1)} collective-permute-done((f32[128,256]{1,0:T(8,128)S(1)}, f32[128,256]{1,0:T(8,128)S(1)}, u32[]{:S(2)}, u32[]{:S(2)}) %collective-permute-start.1) | collective-permute-done | bytes 131104 | tf_op jit(solution)/shard_map/ppermute | solution.py:430
  15.6 1.2 %collective-permute-done.2.p3 = f32[128,256]{1,0:T(8,128)S(1)} collective-permute-done((f32[128,256]{1,0:T(8,128)S(1)}, f32[128,256]{1,0:T(8,128)S(1)}, u32[]{:S(2)}, u32[]{:S(2)}) %collective-permute-start.2) | collective-permute-done | bytes 131104 | tf_op jit(solution)/shard_map/ppermute | solution.py:430
  16.8 0.6 shard_map.110
  17.4 2.8 %collective-permute-start.3 = (f32[128,128]{1,0:T(8,128)S(1)}, f32[128,128]{1,0:T(8,128)S(1)}, u32[]{:S(2)}, u32[]{:S(2)}) collective-permute-start(f32[128,128]{1,0:T(8,128)S(1)} %get-tuple-element.54), channel_id=1, source_target_pairs={{0,16},{4,20},{8,24},{12,28},{16,0},{20,4},{24,8},{28,12},{1,17},{... | collective-permute-start | bytes 196616 | tf_op jit(solution)/shard_map/ppermute | solution.py:495
  20.2 0.6 shard_map.111
  20.7 1.9 %collective-permute-done.3.other_ref = f32[128,128]{1,0:T(8,128)S(1)} collective-permute-done((f32[128,128]{1,0:T(8,128)S(1)}, f32[128,128]{1,0:T(8,128)S(1)}, u32[]{:S(2)}, u32[]{:S(2)}) %collective-permute-start.3) | collective-permute-done | bytes 65568 | tf_op jit(solution)/shard_map/ppermute | solution.py:495
  22.6 0.3 shard_map.112
  22.9 1.7 %collective-permute-start.4 = (f32[128,128]{1,0:T(8,128)S(1)}, f32[128,128]{1,0:T(8,128)S(1)}, u32[]{:S(2)}, u32[]{:S(2)}) collective-permute-start(f32[128,128]{1,0:T(8,128)S(1)} %get-tuple-element.59), channel_id=1, source_target_pairs={{0,4},{4,0},{8,12},{12,8},{16,20},{20,16},{24,28},{28,24},{1,5},{5... | collective-permute-start | bytes 196616 | tf_op jit(solution)/shard_map/ppermute | solution.py:430
  24.6 1.6 %collective-permute-start.5 = (f32[128,128]{1,0:T(8,128)S(1)}, f32[128,128]{1,0:T(8,128)S(1)}, u32[]{:S(2)}, u32[]{:S(2)}) collective-permute-start(f32[128,128]{1,0:T(8,128)S(1)} %get-tuple-element.60), channel_id=1, source_target_pairs={{0,8},{4,12},{8,0},{12,4},{16,24},{20,28},{24,16},{28,20},{1,9},{5... | collective-permute-start | bytes 196616 | tf_op jit(solution)/shard_map/ppermute | solution.py:430
  26.2 0.2 collective-permute-start.6
  26.4 1.5 %shard_map.113 = (f32[4,128,128]{2,1,0:T(8,128)S(1)}, f32[4,128,256]{2,1,0:T(8,128)S(1)}, f32[4,128,128]{2,1,0:T(8,128)S(1)}, f32[4,128,128]{2,1,0:T(8,128)S(1)}, f32[4,256,128]{2,1,0:T(8,128)S(1)}) custom-call(bf16[512,128]{1,0:T(8,128)(2,1)S(1)} %bitcast.19, f32[256,4]{1,0:T(8,128)S(1)} %get-tuple-element.62.rates_ref, ...), custom_call_target="tpu_custom_call" | custom-call | tf_op jit(solution)/shard_map/pallas_call | solution.py:417
  27.9 0.0 collective-permute-done.4.s1
  27.9 0.9 %collective-permute-done.5.s2 = f32[128,128]{1,0:T(8,128)S(1)} collective-permute-done((f32[128,128]{1,0:T(8,128)S(1)}, f32[128,128]{1,0:T(8,128)S(1)}, u32[]{:S(2)}, u32[]{:S(2)}) %collective-permute-start.5) | collective-permute-done | bytes 65568 | tf_op jit(solution)/shard_map/ppermute | solution.py:430
  28.9 2.5 %collective-permute-done.6.s3 = f32[128,128]{1,0:T(8,128)S(1)} collective-permute-done((f32[128,128]{1,0:T(8,128)S(1)}, f32[128,128]{1,0:T(8,128)S(1)}, u32[]{:S(2)}, u32[]{:S(2)}) %collective-permute-start.6) | collective-permute-done | bytes 65568 | tf_op jit(solution)/shard_map/ppermute | solution.py:430
  31.3 0.0 copy-done.2
  31.3 0.7 %copy-done.4 = f32[128]{0:T(128)S(1)} copy-done((f32[128]{0:T(128)S(1)}, f32[128]{0:T(128)}, u32[]{:S(2)}) %copy-start.4) | copy-done | bytes 536
  32.0 2.4 %shard_map.114 = (f32[128,128]{1,0:T(8,128)S(1)}, f32[128,128]{1,0:T(8,128)S(1)}, f32[128,128]{1,0:T(8,128)S(1)}, f32[128,128]{1,0:T(8,128)S(1)}, bf16[512,128]{...) custom-call(f32[128,128]{1,0:T(8,128)S(1)} %get-tuple-element.58.s0, ...), custom_call_target="tpu_custom_call" | custom-call | tf_op jit(solution)/shard_map/pallas_call | solution.py:417
  34.4 0.5 collective-permute-start.7
  34.9 0.8 %collective-permute-start.8 = (f32[128,128]{1,0:T(8,128)S(1)}, f32[128,128]{1,0:T(8,128)S(1)}, u32[]{:S(2)}, u32[]{:S(2)}) collective-permute-start(f32[128,128]{1,0:T(8,128)S(1)} %get-tuple-element.77), channel_id=1, source_target_pairs={{0,8},{4,12},{8,0},{12,4},{16,24},{20,28},{24,16},{28,20},{1,9},{5... | collective-permute-start | bytes 196616 | tf_op jit(solution)/shard_map/ppermute | solution.py:430
  35.7 2.2 %collective-permute-start.9 = (f32[128,128]{1,0:T(8,128)S(1)}, f32[128,128]{1,0:T(8,128)S(1)}, u32[]{:S(2)}, u32[]{:S(2)}) collective-permute-start(f32[128,128]{1,0:T(8,128)S(1)} %get-tuple-element.78), channel_id=1, source_target_pairs={{0,12},{4,8},{8,4},{12,0},{16,28},{20,24},{24,20},{28,16},{1,13},{... | collective-permute-start | bytes 196616 | tf_op jit(solution)/shard_map/ppermute | solution.py:430
  37.9 0.0 collective-permute-start.10
  37.9 1.2 %collective-permute-done.10 = f32[8,128]{1,0:T(8,128)S(1)} collective-permute-done((f32[8,128]{1,0:T(8,128)S(1)}, f32[8,128]{1,0:T(8,128)S(1)}, u32[]{:S(2)}, u32[]{:S(2)}) %collective-permute-start.10) | collective-permute-done | bytes 4128 | tf_op jit(solution)/shard_map/ppermute | solution.py:532
  39.1 1.5 %collective-permute-start.11 = (f32[8,128]{1,0:T(8,128)S(1)}, f32[8,128]{1,0:T(8,128)S(1)}, u32[]{:S(2)}, u32[]{:S(2)}) collective-permute-start(f32[8,128]{1,0:T(8,128)S(1)} %add.6), channel_id=1, source_target_pairs={{0,2},{1,3},{2,0},{3,1},{4,6},{5,7},{6,4},{7,5},{8,10},{9,11},{10,... | collective-permute-start | bytes 12296 | tf_op jit(solution)/shard_map/ppermute | solution.py:532
  40.5 2.1 %collective-permute-done.11 = f32[8,128]{1,0:T(8,128)S(1)} collective-permute-done((f32[8,128]{1,0:T(8,128)S(1)}, f32[8,128]{1,0:T(8,128)S(1)}, u32[]{:S(2)}, u32[]{:S(2)}) %collective-permute-start.11) | collective-permute-done | bytes 4128 | tf_op jit(solution)/shard_map/ppermute | solution.py:532
  42.7 0.0 collective-permute-done.7.p1
  42.7 0.0 collective-permute-done.8.p2
  42.7 0.0 collective-permute-done.9.p3
  42.7 0.6 shard_map.116
  43.3 3.2 %collective-permute-start.12 = (f32[136,128]{1,0:T(8,128)S(1)}, f32[136,128]{1,0:T(8,128)S(1)}, u32[]{:S(2)}, u32[]{:S(2)}) collective-permute-start(f32[136,128]{1,0:T(8,128)S(1)} %get-tuple-element.80), channel_id=1, source_target_pairs={{0,16},{4,20},{8,24},{12,28},{16,0},{20,4},{24,8},{28,12},{1,17},{... | collective-permute-start | bytes 208904 | tf_op jit(solution)/shard_map/ppermute | solution.py:558
  46.5 2.7 %collective-permute-done.12.other_ref = f32[136,128]{1,0:T(8,128)S(1)} collective-permute-done((f32[136,128]{1,0:T(8,128)S(1)}, f32[136,128]{1,0:T(8,128)S(1)}, u32[]{:S(2)}, u32[]{:S(2)}) %collective-permute-start.12) | collective-permute-done | bytes 69664 | tf_op jit(solution)/shard_map/ppermute | solution.py:558
  49.2 0.3 shard_map.117
  49.5 1.0 %collective-permute-start.13 = (f32[136,128]{1,0:T(8,128)S(1)}, f32[136,128]{1,0:T(8,128)S(1)}, u32[]{:S(2)}, u32[]{:S(2)}) collective-permute-start(f32[136,128]{1,0:T(8,128)S(1)} %get-tuple-element.84), channel_id=1, source_target_pairs={{0,4},{4,0},{8,12},{12,8},{16,20},{20,16},{24,28},{28,24},{1,5},{5... | collective-permute-start | bytes 208904 | tf_op jit(solution)/shard_map/ppermute | solution.py:430
  50.4 0.1 collective-permute-start.14
  50.5 2.5 %collective-permute-start.15 = (f32[136,128]{1,0:T(8,128)S(1)}, f32[136,128]{1,0:T(8,128)S(1)}, u32[]{:S(2)}, u32[]{:S(2)}) collective-permute-start(f32[136,128]{1,0:T(8,128)S(1)} %get-tuple-element.86), channel_id=1, source_target_pairs={{0,12},{4,8},{8,4},{12,0},{16,28},{20,24},{24,20},{28,16},{1,13},{... | collective-permute-start | bytes 208904 | tf_op jit(solution)/shard_map/ppermute | solution.py:430
  53.0 3.0 %shard_map.115 = (bf16[512,128]{1,0:T(8,128)(2,1)}, f32[4,256,128]{2,1,0:T(8,128)S(1)}, f32[4,256,128]{2,1,0:T(8,128)S(1)}) custom-call(f32[128,128]{1,0:T(8,128)S(1)} %get-tuple-element.58.s0, f32[128,128]{1,0:T(8,128)S(1)} %collective-permute-done.4.s1, f32[128,128]{1,0:T(8,128)S(1)} %collective-permute-done.5.s2, ...), custom_call_target="tpu_custom_call" | custom-call | tf_op jit(solution)/shard_map/pallas_call | solution.py:417
  56.1 0.0 collective-permute-done.13.a1
  56.1 0.0 collective-permute-done.14.a2
  56.1 0.0 collective-permute-done.15.a3
  56.1 0.0 copy-done
  56.1 3.7 %shard_map.118 = (bf16[1024,128]{1,0:T(8,128)(2,1)}, bf16[1024,128]{1,0:T(8,128)(2,1)}, f32[8,128]{1,0:T(8,128)}, f32[8,128]{1,0:T(8,128)S(1)}) custom-call(f32[136,128]{1,0:T(8,128)S(1)} %get-tuple-element.83.a0, f32[136,128]{1,0:T(8,128)S(1)} %collective-permute-done.13.a1, f32[136,128]{1,0:T(8,128)S(1)} %collective-permute-done.14.a2, ...), custom_call_target="tpu_custom_call" | custom-call | tf_op jit(solution)/shard_map/pallas_call | solution.py:417
  59.8 0.5 slice_bitcast_fusion
  (7 shorter events, 0.0 us)
Async XLA Ops:
  0.6 0.7 %copy-start.3 = (f32[128,2,4]{0,2,1:T(4,128)S(1)}, f32[128,2,4]{0,2,1:T(4,128)}, u32[]{:S(2)}) copy-start(f32[128,2,4]{0,2,1:T(4,128)} %param.9) | copy-start | bytes 12292
  6.2 6.5 %collective-permute-start = (f32[128,256]{1,0:T(8,128)S(1)}, f32[128,256]{1,0:T(8,128)S(1)}, u32[]{:S(2)}, u32[]{:S(2)}) collective-permute-start(f32[128,256]{1,0:T(8,128)S(1)} %get-tuple-element.51), channel_id=1, source_target_pairs={{0,4},{4,0},{8,12},{12,8},{16,20},{20,16},{24,28},{28,24},{1,5},{5... | collective-permute-start | bytes 393224 | tf_op jit(solution)/shard_map/ppermute | solution.py:430
  9.2 6.4 %collective-permute-start.1 = (f32[128,256]{1,0:T(8,128)S(1)}, f32[128,256]{1,0:T(8,128)S(1)}, u32[]{:S(2)}, u32[]{:S(2)}) collective-permute-start(f32[128,256]{1,0:T(8,128)S(1)} %get-tuple-element.52), channel_id=1, source_target_pairs={{0,8},{4,12},{8,0},{12,4},{16,24},{20,28},{24,16},{28,20},{1,9},{5... | collective-permute-start | bytes 393224 | tf_op jit(solution)/shard_map/ppermute | solution.py:430
  10.8 6.0 %collective-permute-start.2 = (f32[128,256]{1,0:T(8,128)S(1)}, f32[128,256]{1,0:T(8,128)S(1)}, u32[]{:S(2)}, u32[]{:S(2)}) collective-permute-start(f32[128,256]{1,0:T(8,128)S(1)} %get-tuple-element.53), channel_id=1, source_target_pairs={{0,12},{4,8},{8,4},{12,0},{16,28},{20,24},{24,20},{28,16},{1,13},{... | collective-permute-start | bytes 393224 | tf_op jit(solution)/shard_map/ppermute | solution.py:430
  17.4 5.2 %collective-permute-start.3 = (f32[128,128]{1,0:T(8,128)S(1)}, f32[128,128]{1,0:T(8,128)S(1)}, u32[]{:S(2)}, u32[]{:S(2)}) collective-permute-start(f32[128,128]{1,0:T(8,128)S(1)} %get-tuple-element.54), channel_id=1, source_target_pairs={{0,16},{4,20},{8,24},{12,28},{16,0},{20,4},{24,8},{28,12},{1,17},{... | collective-permute-start | bytes 196616 | tf_op jit(solution)/shard_map/ppermute | solution.py:495
  22.6 3.8 %copy-start.1 = (bf16[128,4,128]{2,1,0:T(4,128)(2,1)S(1)}, bf16[128,4,128]{2,1,0:T(4,128)(2,1)}, u32[]{:S(2)}) copy-start(bf16[128,4,128]{2,1,0:T(4,128)(2,1)} %param.6) | copy-start | bytes 393220
  22.9 5.0 %collective-permute-start.4 = (f32[128,128]{1,0:T(8,128)S(1)}, f32[128,128]{1,0:T(8,128)S(1)}, u32[]{:S(2)}, u32[]{:S(2)}) collective-permute-start(f32[128,128]{1,0:T(8,128)S(1)} %get-tuple-element.59), channel_id=1, source_target_pairs={{0,4},{4,0},{8,12},{12,8},{16,20},{20,16},{24,28},{28,24},{1,5},{5... | collective-permute-start | bytes 196616 | tf_op jit(solution)/shard_map/ppermute | solution.py:430
  24.6 4.3 %collective-permute-start.5 = (f32[128,128]{1,0:T(8,128)S(1)}, f32[128,128]{1,0:T(8,128)S(1)}, u32[]{:S(2)}, u32[]{:S(2)}) collective-permute-start(f32[128,128]{1,0:T(8,128)S(1)} %get-tuple-element.60), channel_id=1, source_target_pairs={{0,8},{4,12},{8,0},{12,4},{16,24},{20,28},{24,16},{28,20},{1,9},{5... | collective-permute-start | bytes 196616 | tf_op jit(solution)/shard_map/ppermute | solution.py:430
  26.2 5.2 %collective-permute-start.6 = (f32[128,128]{1,0:T(8,128)S(1)}, f32[128,128]{1,0:T(8,128)S(1)}, u32[]{:S(2)}, u32[]{:S(2)}) collective-permute-start(f32[128,128]{1,0:T(8,128)S(1)} %get-tuple-element.61), channel_id=1, source_target_pairs={{0,12},{4,8},{8,4},{12,0},{16,28},{20,24},{24,20},{28,16},{1,13},{... | collective-permute-start | bytes 196616 | tf_op jit(solution)/shard_map/ppermute | solution.py:430
  26.4 4.9 %copy-start.2 = (bf16[128,4,128]{2,1,0:T(4,128)(2,1)S(1)}, bf16[128,4,128]{2,1,0:T(4,128)(2,1)}, u32[]{:S(2)}) copy-start(bf16[128,4,128]{2,1,0:T(4,128)(2,1)} %param.11) | copy-start | bytes 393220
  31.3 0.7 %copy-start.4 = (f32[128]{0:T(128)S(1)}, f32[128]{0:T(128)}, u32[]{:S(2)}) copy-start(f32[128]{0:T(128)} %param.10) | copy-start | bytes 1540
  34.4 8.3 %collective-permute-start.7 = (f32[128,128]{1,0:T(8,128)S(1)}, f32[128,128]{1,0:T(8,128)S(1)}, u32[]{:S(2)}, u32[]{:S(2)}) collective-permute-start(f32[128,128]{1,0:T(8,128)S(1)} %get-tuple-element.76), channel_id=1, source_target_pairs={{0,4},{4,0},{8,12},{12,8},{16,20},{20,16},{24,28},{28,24},{1,5},{5... | collective-permute-start | bytes 196616 | tf_op jit(solution)/shard_map/ppermute | solution.py:430
  34.9 7.8 %collective-permute-start.8 = (f32[128,128]{1,0:T(8,128)S(1)}, f32[128,128]{1,0:T(8,128)S(1)}, u32[]{:S(2)}, u32[]{:S(2)}) collective-permute-start(f32[128,128]{1,0:T(8,128)S(1)} %get-tuple-element.77), channel_id=1, source_target_pairs={{0,8},{4,12},{8,0},{12,4},{16,24},{20,28},{24,16},{28,20},{1,9},{5... | collective-permute-start | bytes 196616 | tf_op jit(solution)/shard_map/ppermute | solution.py:430
  35.7 7.0 %collective-permute-start.9 = (f32[128,128]{1,0:T(8,128)S(1)}, f32[128,128]{1,0:T(8,128)S(1)}, u32[]{:S(2)}, u32[]{:S(2)}) collective-permute-start(f32[128,128]{1,0:T(8,128)S(1)} %get-tuple-element.78), channel_id=1, source_target_pairs={{0,12},{4,8},{8,4},{12,0},{16,28},{20,24},{24,20},{28,16},{1,13},{... | collective-permute-start | bytes 196616 | tf_op jit(solution)/shard_map/ppermute | solution.py:430
  37.9 1.2 %collective-permute-start.10 = (f32[8,128]{1,0:T(8,128)S(1)}, f32[8,128]{1,0:T(8,128)S(1)}, u32[]{:S(2)}, u32[]{:S(2)}) collective-permute-start(f32[8,128]{1,0:T(8,128)S(1)} %get-tuple-element.79), channel_id=1, source_target_pairs={{0,1},{1,0},{2,3},{3,2},{4,5},{5,4},{6,7},{7,6},{8,9},{9,8},{10,11... | collective-permute-start | bytes 12296 | tf_op jit(solution)/shard_map/ppermute | solution.py:532
  39.1 3.6 %collective-permute-start.11 = (f32[8,128]{1,0:T(8,128)S(1)}, f32[8,128]{1,0:T(8,128)S(1)}, u32[]{:S(2)}, u32[]{:S(2)}) collective-permute-start(f32[8,128]{1,0:T(8,128)S(1)} %add.6), channel_id=1, source_target_pairs={{0,2},{1,3},{2,0},{3,1},{4,6},{5,7},{6,4},{7,5},{8,10},{9,11},{10,... | collective-permute-start | bytes 12296 | tf_op jit(solution)/shard_map/ppermute | solution.py:532
  43.3 5.9 %collective-permute-start.12 = (f32[136,128]{1,0:T(8,128)S(1)}, f32[136,128]{1,0:T(8,128)S(1)}, u32[]{:S(2)}, u32[]{:S(2)}) collective-permute-start(f32[136,128]{1,0:T(8,128)S(1)} %get-tuple-element.80), channel_id=1, source_target_pairs={{0,16},{4,20},{8,24},{12,28},{16,0},{20,4},{24,8},{28,12},{1,17},{... | collective-permute-start | bytes 208904 | tf_op jit(solution)/shard_map/ppermute | solution.py:558
  49.5 6.6 %collective-permute-start.13 = (f32[136,128]{1,0:T(8,128)S(1)}, f32[136,128]{1,0:T(8,128)S(1)}, u32[]{:S(2)}, u32[]{:S(2)}) collective-permute-start(f32[136,128]{1,0:T(8,128)S(1)} %get-tuple-element.84), channel_id=1, source_target_pairs={{0,4},{4,0},{8,12},{12,8},{16,20},{20,16},{24,28},{28,24},{1,5},{5... | collective-permute-start | bytes 208904 | tf_op jit(solution)/shard_map/ppermute | solution.py:430
  50.4 5.6 %collective-permute-start.14 = (f32[136,128]{1,0:T(8,128)S(1)}, f32[136,128]{1,0:T(8,128)S(1)}, u32[]{:S(2)}, u32[]{:S(2)}) collective-permute-start(f32[136,128]{1,0:T(8,128)S(1)} %get-tuple-element.85), channel_id=1, source_target_pairs={{0,8},{4,12},{8,0},{12,4},{16,24},{20,28},{24,16},{28,20},{1,9},{5... | collective-permute-start | bytes 208904 | tf_op jit(solution)/shard_map/ppermute | solution.py:430
  50.5 5.5 %collective-permute-start.15 = (f32[136,128]{1,0:T(8,128)S(1)}, f32[136,128]{1,0:T(8,128)S(1)}, u32[]{:S(2)}, u32[]{:S(2)}) collective-permute-start(f32[136,128]{1,0:T(8,128)S(1)} %get-tuple-element.86), channel_id=1, source_target_pairs={{0,12},{4,8},{8,4},{12,0},{16,28},{20,24},{24,20},{28,16},{1,13},{... | collective-permute-start | bytes 208904 | tf_op jit(solution)/shard_map/ppermute | solution.py:430
  53.0 3.1 %copy-start = (bf16[128,2,4,128]{3,2,1,0:T(4,128)(2,1)S(1)}, bf16[128,2,4,128]{3,2,1,0:T(4,128)(2,1)}, u32[]{:S(2)}) copy-start(bf16[128,2,4,128]{3,2,1,0:T(4,128)(2,1)} %param.7) | copy-start | bytes 786436

commit v3 on v0

v3 whole, which is shorter than its diff:
```python
import functools
import types

import jax
import jax.numpy as jnp
from jax import lax
from jax.experimental import pallas as pl
from jax.experimental.pallas import tpu as pltpu
from jax.sharding import PartitionSpec as P

EPS = 1e-06
GROUP = 4
HALF = 128
BASE = 16
F32 = jnp.float32
BF16 = jnp.bfloat16


def split(x):
    high = x.astype(BF16)
    return high, (x - high.astype(F32)).astype(BF16)


def mm(a, b, ta=False, tb=False):
    (ah, al), (bh, bl) = split(a), split(b)
    if ta:
        ah, al = ah.T, al.T
    dims = (((1,), (1 if tb else 0,)), ((), ()))
    if b.shape[0 if tb else 1] > 128:
        left = jnp.concatenate([ah, ah, al], axis=1)
        right = jnp.concatenate([bh, bl, bh], axis=1 if tb else 0)
        return lax.dot_general(left, right, dims, preferred_element_type=F32)
    left = jnp.concatenate([ah, al], axis=1)
    if tb:
        right = jnp.concatenate(
            [jnp.concatenate([bh, bh], axis=1), jnp.concatenate([bl, bl], axis=1)], axis=0
        )
        width = b.shape[0]
    else:
        right = jnp.concatenate([bh, bl], axis=1)
        right = jnp.concatenate([right, right], axis=0)
        width = b.shape[1]
    both = lax.dot_general(left, right, dims, preferred_element_type=F32)
    return both[:, :width] + both[:, width:]


def exact_nt(a, b):
    return lax.dot_general(a, b, (((1,), (1,)), ((), ())), preferred_element_type=F32)


def iota(shape, dim):
    return lax.broadcasted_iota(jnp.int32, shape, dim)


def row_of(column):
    square = jnp.where(iota((HALF, HALF), 0) == iota((HALF, HALF), 1), column, 0.0)
    return jnp.sum(square, axis=0, keepdims=True)


def places(steps, j):
    shape = (steps, steps // 2)
    return (iota(shape, 0) == 2 * iota(shape, 1) + j).astype(F32)


def pick(a, b, ta=False, tb=False):
    dims = (((0 if ta else 1,), (1 if tb else 0,)), ((), ()))
    return lax.dot_general(
        a, b, dims, precision=lax.Precision.HIGHEST, preferred_element_type=F32
    )


def rate_column(rates, head):
    return jnp.sum(jnp.where(iota(rates.shape, 1) == head, rates, 0.0), axis=1, keepdims=True)


def small_inverses(lowers, rate_rows):
    blocks = HALF // BASE
    lane = iota((BASE, HALF), 1)
    row = iota((BASE, HALF), 0)
    jobs = range(len(lowers))
    packed = []
    for lower in lowers:
        one = lower[:BASE]
        for b in range(1, blocks):
            one = jnp.where(lane // BASE == b, lower[b * BASE : (b + 1) * BASE], one)
        packed.append(one)
    scaled = [packed[n] * rate_rows[n] for n in jobs]
    for j in range(BASE - 1):
        index = lane // BASE * BASE + j
        factors = [
            jnp.take_along_axis(scaled[n], index, axis=1, mode="promise_in_bounds") for n in jobs
        ]
        packed = [
            packed[n] - jnp.where(row > j, factors[n], 0.0) * packed[n][j : j + 1] for n in jobs
        ]
    return [
        jnp.concatenate(
            [jnp.where(lane // BASE == b, one, 0.0) for b in range(blocks)], axis=0
        )
        for one in packed
    ]


def place_in(group):
    return lax.rem(lax.axis_index("seq"), group)


def strided(ref, head, rows):
    return ref[pl.ds(head, rows, stride=ref.shape[0] // rows), :]


def store_strided(ref, head, value):
    rows = value.shape[0]
    ref[pl.ds(head, rows, stride=ref.shape[0] // rows), :] = value


SOONER, LATER = (1, 2), (3, 0)


def take(pairs, heads):
    order = SOONER + LATER
    return [pairs[order.index(h) // 2][order.index(h) % 2] for h in heads]


def inverse_norm(rows):
    return lax.rsqrt(jnp.sum(rows * rows, axis=1, keepdims=True) + EPS)


def unit_grad(inv, unit, grad):
    return inv * (grad - unit * jnp.sum(unit * grad, axis=1, keepdims=True))


def chunk(me, heads, kf, vf, rates, rows, o, wait):
    steps = rates.shape[0]
    strict = iota((HALF, HALF), 1) < iota((HALF, HALF), 0)
    rate = [rate_column(rates, me ^ h) for h in heads]
    rate_rows = [rows[pl.ds(me ^ h, 1), :] for h in heads]
    sides = [slice(0, HALF), slice(HALF, 2 * HALF)]
    raws = [strided(kf, me ^ h, steps) for h in heads]
    heads = range(len(heads)) if wait is None else heads
    count = range(len(raws))
    invs = [inverse_norm(raw) for raw in raws]
    inv_rows = [[row_of(inv[side]) for side in sides] for inv in invs]
    units = [raw * inv for raw, inv in zip(raws, invs)]
    raw16 = [raw.astype(BF16) for raw in raws]
    jobs = [(i, b) for i in count for b in range(2)]
    diag = {
        (i, b): jnp.where(
            strict,
            exact_nt(raw16[i][sides[b]], raw16[i][sides[b]]) * invs[i][sides[b]] * inv_rows[i][b],
            0.0,
        )
        for i, b in jobs
    }
    cross = [
        exact_nt(raw16[i][sides[1]], raw16[i][sides[0]]) * invs[i][sides[1]] * inv_rows[i][0]
        for i in count
    ]
    across = {(i, b): rate_rows[i][:, sides[b]] for i, b in jobs}
    inverse = dict(zip(jobs, small_inverses([diag[n] for n in jobs], [across[n] for n in jobs])))
    size = BASE
    while size < HALF:
        r, c = iota((HALF, HALF), 0) // size, iota((HALF, HALF), 1) // size
        below = (r % 2 == 1) & (c == r - 1)
        part = {n: jnp.where(below, diag[n], 0.0) for n in jobs}
        right = {n: part[n] - mm(part[n] * across[n], inverse[n]) for n in jobs}
        inverse = {
            n: inverse[n] + right[n] - mm(inverse[n] * across[n], right[n]) for n in jobs
        }
        size *= 2
    right = [cross[i] - mm(cross[i] * across[i, 0], inverse[i, 0]) for i in count]
    joined = [right[i] - mm(inverse[i, 1] * across[i, 1], right[i]) for i in count]
    vals = vf()
    both = [jnp.concatenate([units[i], vals[i]], axis=1) for i in count]
    top = [both[i][:HALF] - mm(inverse[i, 0] * across[i, 0], both[i][:HALF]) for i in count]
    low = [
        jnp.concatenate([joined[i] * across[i, 0], inverse[i, 1] * across[i, 1]], axis=1)
        for i in count
    ]
    bottom = [both[i][HALF:] - mm(low[i], both[i]) for i in count]
    solved = [jnp.concatenate([top[i], bottom[i]], axis=0) for i in count]
    eye = (iota((HALF, 2 * HALF), 0) == iota((HALF, 2 * HALF), 1)).astype(F32)
    sign = jnp.where(iota((HALF, 2 * HALF), 1) < HALF, -1.0, 1.0)
    ends = [eye + sign * mm(units[i], rate[i] * solved[i], ta=True) for i in count]
    for i in count:
        o.maps[i][...] = ends[i]
        o.unit[i] = units[i]
        o.inverse[i, :HALF, :HALF] = inverse[i, 0]
        o.inverse[i, :HALF, HALF:] = jnp.zeros((HALF, HALF), F32)
        o.inverse[i, HALF:, :HALF] = joined[i]
        o.inverse[i, HALF:, HALF:] = inverse[i, 1]
        o.w[i] = solved[i][:, :HALF]
        o.e[i] = solved[i][:, HALF:]


def first_kernel(group, heads, n, o, k16, v16, p32, sems):
    copies = [
        pltpu.make_async_copy(src, dst, sems.at[c])
        for c, (src, dst) in enumerate(((n.packed, p32), (n.k, k16), (n.v, v16)))
    ]
    for copy in copies:
        copy.start()
    me = place_in(group)
    steps, count = o.rates.shape
    copies[0].wait()
    packed = p32[...]
    own, place = [packed[:count], packed[count:]], [places(steps, j) for j in range(2)]
    rates = pick(place[0], own[0], tb=True) + pick(place[1], own[1], tb=True)
    o.rates[...] = rates
    o.rows[...] = pick(own[0], place[0], tb=True) + pick(own[1], place[1], tb=True)
    copies[1].wait()
    o.kf[...] = k16[...].astype(F32)
    copies[2].wait()
    o.vf[...] = v16[...].astype(F32)
    vals = [strided(o.vf, me ^ h, steps) for h in heads]
    chunk(me, heads, o.kf, lambda: vals, rates, o.rows, o, None)


def next_kernel(group, heads, n, o):
    me = place_in(group)
    steps = n.rates.shape[0]
    vals = [strided(n.vf, me ^ h, steps) for h in heads]
    chunk(me, heads, n.kf, lambda: vals, n.rates[...], n.rows, o, None)


def second_kernel(group, n, o, qf):
    me = place_in(group)
    qf[...] = n.q[...].astype(F32)
    heads, tokens, steps = o.scores.shape
    heads = range(heads)
    rates = n.rates[...]
    seen = iota((tokens, steps), 1) <= 2 * iota((tokens, steps), 0) + 1
    raws = [strided(qf, me ^ i, tokens) for i in heads]
    keys, w, e, inverse = (take(x, heads) for x in (n.unit, n.w, n.e, n.inverse))
    rate = [rate_column(rates, me ^ i) for i in heads]
    weighted = [rate[i] * jnp.concatenate([w[i], e[i]], axis=1) for i in heads]
    units = [raw * inverse_norm(raw) for raw in raws]
    scores = [jnp.where(seen, mm(units[i], keys[i], tb=True), 0.0) for i in heads]
    rows = [mm(scores[i], weighted[i]) for i in heads]
    spread = [keys[i] - mm(inverse[i], rate[i] * keys[i], ta=True) for i in heads]
    for i in heads:
        o.q_unit[i] = units[i]
        o.scores[i] = scores[i]
        o.qc[i] = units[i] - rows[i][:, :HALF]
        o.part[i] = rows[i][:, HALF:]
        o.kx[i] = spread[i]
    o.gain[...] = n.gain[...]


def join_kernel(group, n, o):
    me = place_in(group)
    for i, piece in enumerate(n.maps):
        o.maps[me ^ i] = piece[...]
    state = jnp.zeros((HALF, HALF), F32)
    for j in range(group):
        o.starts[j] = state
        own = o.maps[j, :, HALF:]
        state = own if j == 0 else mm(o.maps[j, :, :HALF], state) + own
    o.total[...] = state


def products_kernel(group, n, o):
    eye = (iota((HALF, HALF), 0) == iota((HALF, HALF), 1)).astype(F32)
    steps = [n.maps[j, :, :HALF] for j in range(group)]
    before, after = [eye, steps[0]], [eye, steps[-1]]
    for j in range(1, group):
        before.append(mm(steps[j], before[-1]))
        after.append(mm(after[-1], steps[-1 - j]))
    for j in range(group + 1):
        o.before[j] = before[j]
    for j in range(group):
        o.after[j] = after[group - 1 - j]


def spread_kernel(group, side, transposed, n, o):
    me = place_in(group)
    entry = n.entry[:HALF, :]
    if side is not None:
        entry = jnp.where(lax.axis_index("seq") // group == side, entry, 0.0)
    starts = [n.starts[me ^ i] for i in range(group)]
    maps = [n.maps[me ^ i] for i in range(group)]
    values = [starts[i] + mm(maps[i], entry, ta=transposed) for i in range(group)]
    for i, out in enumerate(o.states):
        out[:HALF, :] = values[i]
        if transposed:
            out[HALF:, :] = n.gain[...] + n.entry[HALF:, :]


def read_kernel(group, heads, n, o, gf, *of):
    me = place_in(group)
    gf[...] = n.og[...].astype(F32)
    tokens = n.qc.shape[1]
    gain = n.gain[...]
    given = [strided(gf, me ^ h, tokens) for h in heads]
    query = [n.qc[h] for h in heads]
    count = range(len(heads))
    reads = [n.part[h] + mm(query[i], n.states[i][...]) for i, h in enumerate(heads)]
    inv_rms = [lax.rsqrt(jnp.mean(read * read, axis=1, keepdims=True) + EPS) for read in reads]
    normal = [reads[i] * inv_rms[i] for i in count]
    scaled = [given[i] * gain for i in count]
    grads = [
        inv_rms[i] * (scaled[i] - normal[i] * jnp.mean(scaled[i] * normal[i], axis=1, keepdims=True))
        for i in count
    ]
    parts = [mm(query[i], grads[i], ta=True) for i in count]
    gain_part = sum(jnp.sum(given[i] * normal[i], axis=0, keepdims=True) for i in count)
    for i in count:
        o.parts[i][...] = parts[i]
        o.grad[i] = grads[i]
    if of:
        for i, h in enumerate(heads):
            store_strided(of[0], me ^ h, gain * normal[i])
            store_strided(of[0], me ^ SOONER[i], n.normed[i])
        o.normed[...] = of[0][...].astype(BF16)
        o.gain_part[...] = n.gain_part[...] + gain_part
    else:
        for i in count:
            o.normed[i] = gain * normal[i]
        o.gain_part[...] = jnp.broadcast_to(gain_part, o.gain_part.shape)


def query_kernel(group, n, o, qf, df):
    me = place_in(group)
    qf[...] = n.q[...].astype(F32)
    heads, tokens, steps = o.d_scores.shape
    heads = range(heads)
    rates = n.rates[...]
    seen = iota((tokens, steps), 1) <= 2 * iota((tokens, steps), 0) + 1
    raws = [strided(qf, me ^ i, tokens) for i in heads]
    states = [ref[...] for ref in n.states]
    grads, keys, w, e = (take(x, heads) for x in (n.grad, n.unit, n.w, n.e))
    units = [n.q_unit[i] for i in heads]
    errs = [e[i] - mm(w[i], states[i]) for i in heads]
    pseudo = [rate_column(rates, me ^ i) * errs[i] for i in heads]
    d_scores = [jnp.where(seen, mm(grads[i], pseudo[i], tb=True), 0.0) for i in heads]
    d_units = [mm(grads[i], states[i], tb=True) + mm(d_scores[i], keys[i]) for i in heads]
    done = [unit_grad(inverse_norm(raws[i]), units[i], d_units[i]) for i in heads]
    for i in heads:
        o.err[i] = errs[i]
        o.d_scores[i] = d_scores[i]
        store_strided(df, me ^ i, done[i])
    o.dq[...] = df[...].astype(BF16)


def early_kernel(group, n, o):
    me = place_in(group)
    heads = range(o.dk.shape[0])
    rates = n.rates[...]
    rate = [rate_column(rates, me ^ i) for i in heads]
    grads, inverse = (take(x, heads) for x in (n.grad, n.inverse))
    units, scores, d_scores = ([x[i] for i in heads] for x in (n.q_unit, n.scores, n.d_scores))
    d_keys = [mm(d_scores[i], units[i], ta=True) for i in heads]
    d_pseudo = [mm(scores[i], grads[i], ta=True) for i in heads]
    z = [d_pseudo[i] - mm(inverse[i], rate[i] * d_pseudo[i], ta=True) for i in heads]
    for i in heads:
        o.dk[i] = d_keys[i]
        o.z[i] = z[i]


def join_back_kernel(group, n, o, parts):
    me = place_in(group)
    for i, piece in enumerate(n.parts):
        parts[me ^ i] = piece[...]
    maps = [n.maps[j, :, :HALF] for j in range(group)]
    adjoint = jnp.zeros((HALF, HALF), F32)
    for j in reversed(range(group)):
        o.starts[j] = adjoint
        own = parts[j]
        adjoint = own if j == group - 1 else mm(maps[j], adjoint, ta=True) + own
    o.total[:HALF, :] = adjoint
    gain = sum(ref[...] for ref in n.gains)
    o.total[HALF:, :] = gain
    o.gain[...] = gain


def last_kernel(group, heads, n, o, kf, *scratch):
    me = place_in(group)
    kf[...] = n.k[...].astype(F32)
    rates = n.rates[...]
    steps, every = rates.shape
    count = range(len(heads))
    rate = [rate_column(rates, me ^ h) for h in heads]
    raws = [strided(kf, me ^ h, steps) for h in heads]
    adjoints = [ref[:HALF, :] for ref in n.adjoints]
    states = [ref[...] for ref in n.states]
    units = take(n.unit, heads)
    errs, kx, z0, dk0 = ([x[h] for h in heads] for x in (n.err, n.kx, n.z, n.dk))
    z = [z0[i] + mm(kx[i], adjoints[i]) for i in count]
    invs = [inverse_norm(raw) for raw in raws]
    pseudo = [rate[i] * errs[i] for i in count]
    d_values = [rate[i] * z[i] for i in count]
    below = iota((steps, steps), 1) < iota((steps, steps), 0)
    above = iota((steps, steps), 1) > iota((steps, steps), 0)
    d_grams = [
        jnp.where(
            below,
            mm(d_values[i], pseudo[i], tb=True),
            jnp.where(above, mm(pseudo[i], d_values[i], tb=True), 0.0),
        )
        for i in count
    ]
    d_units = [
        dk0[i]
        + mm(pseudo[i], adjoints[i], tb=True)
        - mm(d_values[i], states[i], tb=True)
        - mm(d_grams[i], units[i])
        for i in count
    ]
    done = [unit_grad(invs[i], units[i], d_units[i]) for i in count]
    d_rates = n.d_rates[...] if scratch else jnp.zeros(rates.shape, F32)
    for i, h in enumerate(heads):
        d_rate = jnp.sum(z[i] * errs[i], axis=1, keepdims=True)
        d_rates = jnp.where(iota(rates.shape, 1) == me ^ h, d_rate, d_rates)
    if not scratch:
        for i in count:
            o.dk[i] = done[i]
            o.dv[i] = d_values[i]
        o.d_rates[...] = d_rates
        return
    df, vf = scratch
    for i, h in enumerate(heads):
        store_strided(vf, me ^ SOONER[i], n.dv[i])
        store_strided(vf, me ^ h, d_values[i])
        store_strided(df, me ^ SOONER[i], n.dk1[i])
        store_strided(df, me ^ h, done[i])
    o.dk[...] = df[...].astype(BF16)
    o.dv[...] = vf[...].astype(BF16)
    for j in range(2):
        o.db[j * every : (j + 1) * every, :] = pick(d_rates, places(steps, j), ta=True)
    o.gain[...] = sum(ref[HALF:, :] for ref in n.all_adjoints)[:1]


def f32(*shape):
    return pltpu.VMEM(shape, F32)


def out(dtype, *shape):
    return jax.ShapeDtypeStruct(shape, dtype)


def call(body, ins, outs, scratch=(), hbm=(), after=(), flops=1000):
    names = [name for name in ins]
    flat, tree = jax.tree.flatten([ins[name] for name in names])
    outs = dict(outs)
    flat_outs, out_tree = jax.tree.flatten(outs)
    specs = jax.tree.leaves(
        [
            jax.tree.map(
                lambda _: pl.BlockSpec(memory_space=pltpu.HBM if name in hbm else pltpu.VMEM),
                ins[name],
            )
            for name in names
        ]
    )
    after = list(after)

    def kernel(*refs):
        values = jax.tree.unflatten(tree, refs[: len(flat)])
        start = len(flat) + len(after)
        results = jax.tree.unflatten(out_tree, refs[start : start + len(flat_outs)])
        body(
            types.SimpleNamespace(**dict(zip(names, values))),
            types.SimpleNamespace(**results),
            *refs[start + len(flat_outs) :],
        )

    results = pl.pallas_call(
        kernel,
        out_shape=flat_outs,
        in_specs=specs + [pl.BlockSpec(memory_space=pl.ANY)] * len(after),
        scratch_shapes=[pltpu.VMEM(s, F32) if isinstance(s, tuple) else s for s in scratch],
        compiler_params=pltpu.CompilerParams(vmem_limit_bytes=16 * 1024 * 1024),
        cost_estimate=pl.CostEstimate(flops=flops, bytes_accessed=0, transcendentals=0),
    )(*flat, *after)
    return types.SimpleNamespace(**jax.tree.unflatten(out_tree, results))


def swap(piece, i):
    return lax.ppermute(piece, "seq", [(d, d ^ i) for d in range(lax.axis_size("seq"))])


def local(queries, keys, values, betas, gain, out_grad):
    tokens, heads, dim = queries.shape
    substeps = keys.shape[1]
    steps = tokens * substeps
    group = GROUP
    count = lax.axis_size("seq")
    groups = count // group
    two = groups == 2
    bind = functools.partial
    q2 = queries.reshape(tokens * heads, dim)
    g2 = out_grad.reshape(tokens * heads, dim)
    k2 = keys.reshape(steps * heads, dim)
    v2 = values.reshape(steps * heads, dim)
    packed = betas.transpose(1, 2, 0).reshape(substeps * heads, tokens)

    def chunk_outs():
        return dict(
            maps=[f32(dim, 2 * dim) for _ in SOONER],
            unit=f32(2, steps, dim),
            inverse=f32(2, steps, steps),
            w=f32(2, steps, dim),
            e=f32(2, steps, dim),
        )

    a = call(
        bind(first_kernel, group, SOONER),
        {
            name: pltpu.with_memory_space_constraint(x, pltpu.HBM)
            for name, x in (("k", k2), ("v", v2), ("packed", packed))
        },
        dict(
            chunk_outs(),
            rates=f32(steps, heads),
            rows=f32(heads, steps),
            kf=f32(steps * heads, dim),
            vf=f32(steps * heads, dim),
        ),
        scratch=[pltpu.VMEM((steps * heads, dim), BF16)] * 2
        + [(substeps * heads, tokens), pltpu.SemaphoreType.DMA((3,))],
        hbm=("k", "v", "packed"),
    )
    got = {h: swap(a.maps[i], h) for i, h in enumerate(SOONER)}
    b = call(
        bind(next_kernel, group, LATER),
        dict(kf=a.kf, vf=a.vf, rates=a.rates, rows=a.rows),
        chunk_outs(),
    )
    for i, h in enumerate(LATER):
        got[h] = swap(b.maps[i], h) if h else b.maps[i]
    unit, inverse, w, e = ([getattr(x, name) for x in (a, b)] for name in ("unit", "inverse", "w", "e"))
    rates = a.rates
    c = call(
        bind(second_kernel, group),
        dict(q=q2, gain=gain.reshape(1, dim), rates=rates, unit=unit, inverse=inverse, w=w, e=e),
        dict(
            q_unit=f32(heads, tokens, dim),
            scores=f32(heads, tokens, steps),
            qc=f32(heads, tokens, dim),
            part=f32(heads, tokens, dim),
            kx=f32(heads, steps, dim),
            gain=f32(1, dim),
        ),
        scratch=[(tokens * heads, dim)],
        after=[got[h] for h in SOONER],
        flops=10**9,
    )
    j = call(
        bind(join_kernel, group),
        dict(maps=[got[h] for h in range(heads)]),
        dict(
            starts=f32(group, dim, dim), total=f32(dim, dim), maps=f32(group, dim, 2 * dim)
        ),
        after=[c.gain],
    )
    ahead = [(d, d + group) for d in range(count - group)]
    behind = [(d + group, d) for d in range(count - group)]
    across = [(d, d ^ group) for d in range(count)]
    entry = lax.ppermute(j.total, "seq", across if two else ahead)
    p = call(
        bind(products_kernel, group),
        dict(maps=j.maps),
        dict(before=f32(group + 1, dim, dim), after=f32(group, dim, dim)),
    )
    for _ in range(groups - 2):
        passed = jnp.dot(p.before[group], entry, precision=lax.Precision.HIGHEST) + j.total
        entry = lax.ppermute(passed, "seq", ahead)
    states = call(
        bind(spread_kernel, group, 1 if two else None, False),
        dict(entry=entry, starts=j.starts, maps=p.before),
        dict(states=[f32(dim, dim)] * heads),
    ).states
    states = [states[0]] + [swap(states[h], h) for h in range(1, heads)]
    shared = dict(og=g2, gain=c.gain, qc=c.qc, part=c.part)
    r1 = call(
        bind(read_kernel, group, SOONER),
        dict(shared, states=[states[h] for h in SOONER]),
        dict(
            parts=[f32(dim, dim)] * 2,
            grad=f32(2, tokens, dim),
            normed=f32(2, tokens, dim),
            gain_part=f32(8, dim),
        ),
        scratch=[(tokens * heads, dim)],
    )
    got = {h: swap(r1.parts[i], h) for i, h in enumerate(SOONER)}
    r2 = call(
        bind(read_kernel, group, LATER),
        dict(
            shared,
            states=[states[h] for h in LATER],
            normed=r1.normed,
            gain_part=r1.gain_part,
        ),
        dict(
            parts=[f32(dim, dim)] * 2,
            grad=f32(2, tokens, dim),
            normed=out(BF16, tokens * heads, dim),
            gain_part=f32(8, dim),
        ),
        scratch=[(tokens * heads, dim)] * 2,
    )
    for i, h in enumerate(LATER):
        got[h] = swap(r2.parts[i], h) if h else r2.parts[i]
    grad = [r1.grad, r2.grad]
    gain_part = r2.gain_part
    gains = [gain_part]
    if two:
        size = lax.axis_size("head")
        if size > 1:
            gain_part = gain_part + lax.ppermute(
                gain_part, "head", [(d, d ^ 1) for d in range(size)]
            )
        gains = [gain_part] + [
            lax.ppermute(gain_part, "head", [(d, d ^ flip) for d in range(size)])
            for flip in range(2, size, 2)
        ]
    y = call(
        bind(query_kernel, group),
        dict(
            states=states,
            q=q2,
            rates=rates,
            grad=grad,
            w=w,
            e=e,
            q_unit=c.q_unit,
            unit=unit,
        ),
        dict(
            dq=out(BF16, tokens * heads, dim),
            err=f32(heads, steps, dim),
            d_scores=f32(heads, tokens, steps),
        ),
        scratch=[(tokens * heads, dim)] * 2,
        after=[got[h] for h in SOONER],
        flops=10**9,
    )
    jb = call(
        bind(join_back_kernel, group),
        dict(parts=[got[h] for h in range(heads)], maps=j.maps, gains=gains),
        dict(starts=f32(group, dim, dim), total=f32(dim + 8, dim), gain=f32(8, dim)),
        scratch=[(group, dim, dim)],
        after=[y.err],
    )
    entry = lax.ppermute(jb.total, "seq", across if two else behind)
    z = call(
        bind(early_kernel, group),
        dict(
            rates=rates,
            grad=grad,
            d_scores=y.d_scores,
            q_unit=c.q_unit,
            scores=c.scores,
            inverse=inverse,
        ),
        dict(dk=f32(heads, steps, dim), z=f32(heads, steps, dim)),
    )
    for _ in range(groups - 2):
        passed = jnp.dot(p.before[group].T, entry[:dim], precision=lax.Precision.HIGHEST)
        entry = lax.ppermute(jb.total.at[:dim].add(passed), "seq", behind)
    adjoints = call(
        bind(spread_kernel, group, 0 if two else None, True),
        dict(entry=entry, starts=jb.starts, maps=p.after, gain=jb.gain),
        dict(states=[f32(dim + 8, dim)] * heads),
        after=[z.dk],
    ).states
    adjoints = [adjoints[0]] + [swap(adjoints[h], h) for h in range(1, heads)]
    ins = dict(
        k=k2, rates=rates, unit=unit, err=y.err, kx=c.kx, z=z.z, dk=z.dk
    )
    l1 = call(
        bind(last_kernel, group, SOONER),
        dict(ins, adjoints=[adjoints[h] for h in SOONER], states=[states[h] for h in SOONER]),
        dict(dk=f32(2, steps, dim), dv=f32(2, steps, dim), d_rates=f32(steps, heads)),
        scratch=[(steps * heads, dim)],
    )
    l2 = call(
        bind(last_kernel, group, LATER),
        dict(
            ins,
            adjoints=[adjoints[h] for h in LATER],
            states=[states[h] for h in LATER],
            all_adjoints=adjoints,
            dk1=l1.dk,
            dv=l1.dv,
            d_rates=l1.d_rates,
        ),
        dict(
            dk=out(BF16, steps * heads, dim),
            dv=out(BF16, steps * heads, dim),
            db=out(F32, substeps * heads, tokens),
            gain=out(F32, 1, dim),
        ),
        scratch=[(steps * heads, dim)] * 3,
    )
    gain_sum = l2.gain[0] if two else lax.psum(gain_part[0], ("seq", "head"))
    return (
        r2.normed.reshape(tokens, heads, dim),
        y.dq.reshape(tokens, heads, dim),
        l2.dk.reshape(tokens, substeps, heads, dim),
        l2.dv.reshape(tokens, substeps, heads, dim),
        l2.db.reshape(substeps, heads, tokens).transpose(2, 0, 1),
        gain_sum,
    )


def solution(mesh):
    return jax.shard_map(
        local,
        mesh=mesh,
        in_specs=(
            P("seq", "head", None),
            P("seq", None, "head", None),
            P("seq", None, "head", None),
            P("seq", None, "head"),
            P(),
            P("seq", "head", None),
        ),
        out_specs=(
            P("seq", "head", None),
            P("seq", "head", None),
            P("seq", None, "head", None),
            P("seq", None, "head", None),
            P("seq", None, "head"),
            P(),
        ),
        check_vma=False,
    )
```

time: 473 us -> 54.1 us (0.11)
  other arithmetic: 252 us -> 0.01 us
  matrix products: 55.6 us -> 0 us
  blocking collectives: 44.8 us -> 0 us
  waiting for transfers between devices: 46.2 us -> 13.5 us
  starting transfers between devices: 46.7 us -> 22.4 us
  Pallas kernels: 0 us -> 16.6 us
  between operations: 14.4 us -> 0.74 us
  local copies, waits for them, and re-layouts: 11 us -> 0.66 us
    another operation x20 -> x0, other arithmetic: 240 us -> none  [group_parts(): jax.scipy.linalg.solve_triangular(unit_lower, right_side, lower=True, uni...]
    dot_general x76 -> x0, matrix products: 49 us -> none  [the longest x8 11.4 us: compose(): jnp.einsum('hij,hjk->hik', trans_late, state_early, precision=HIGH_ACCURACY)]
    psum x1 -> x0, blocking collectives: 44.8 us -> none  [local(): gain_grad = lax.psum(gain_part, ('seq', 'head'))]
    ppermute x7 -> x16, starting transfers between devices: 46.5 us -> 22.4 us  [the longest x12 15.3 us: swap(): lax.ppermute(piece, 'seq', [(d, d ^ i) for d in range(lax.axis_size('seq'...]
    ppermute x7 -> x16, waiting for transfers between devices: 37.1 us -> 13.5 us  [the longest x12 7.54 us: swap(): lax.ppermute(piece, 'seq', [(d, d ^ i) for d in range(lax.axis_size('seq'...]
    pallas_call x0 -> x14, Pallas kernels: none -> 16.6 us  [call(): pl.pallas_call(kernel, out_shape=flat_outs, in_specs=specs + [pl.BlockSpe...]
    all_gather x2 -> x0, waiting for transfers between devices: 9.09 us -> none  [prefix(): everything = jax.tree.map(lambda part: lax.all_gather(part, axis), array)]
    another operation x10 -> x0, matrix products: 6.52 us -> none  [group_parts(): jax.scipy.linalg.solve_triangular(unit_lower, right_side, lower=True, uni...]
  transfers between devices with their start and end apart: 9 -> 16, of which waited for: 8 -> 9; matrix products, arithmetic and copies ran while one was open for 20% -> 0% of each run, Pallas kernels for 0% -> 17%
where the time goes in v3:
time: 54.1 us; the launch traced here: 53.9 us
  starting transfers between devices  22.4 us (41%)
  Pallas kernels  16.6 us (31%)
  waiting for transfers between devices  13.5 us (25%)
  between operations  0.74 us (1%)
  local copies, waits for them, and re-layouts  0.66 us (1%)
    pallas_call x14, Pallas kernels, call(): pl.pallas_call(kernel, out_shape=flat_outs, in_specs=specs + [pl.BlockSpe...  16.6 us
    ppermute x12, starting transfers between devices, swap(): lax.ppermute(piece, 'seq', [(d, d ^ i) for d in range(lax.axis_size('seq'...  15.3 us
    ppermute x12, waiting for transfers between devices, swap(): lax.ppermute(piece, 'seq', [(d, d ^ i) for d in range(lax.axis_size('seq'...  7.54 us
    ppermute x1, waiting for transfers between devices, local(): entry = lax.ppermute(jb.total, 'seq', across if two else behind)  2.97 us
    ppermute x1, starting transfers between devices, local(): entry = lax.ppermute(jb.total, 'seq', across if two else behind)  2.83 us
    ppermute x1, waiting for transfers between devices, local(): entry = lax.ppermute(j.total, 'seq', across if two else ahead)  2.65 us
    ppermute x1, starting transfers between devices, local(): entry = lax.ppermute(j.total, 'seq', across if two else ahead)  2.65 us
    ppermute x1, starting transfers between devices, local(): lax.ppermute(gain_part, 'head', [(d, d ^ flip) for d in range(size)])  1.55 us
  transfers between devices with their start and end apart: 16, of which 9 were waited for; matrix products, arithmetic and copies ran while one was open for 0% of the time, Pallas kernels for 17%

profile of v3, /device:TPU:0, one launch (start us, length us, event | category | flops | bytes accessed | tf_op | source)
XLA Modules:
  0.0 53.9 jit_solution(7644044633658830999)
XLA Ops:
  0.6 3.7 %shard_map.109 = (f32[2,256,128]{2,1,0:T(8,128)S(1)}, f32[2,256,256]{2,1,0:T(8,128)S(1)}, f32[1024,128]{1,0:T(8,128)S(1)}, f32[128,256]{1,0:T(8,128)S(1)}, f32[1...) custom-call(bf16[1024,128]{1,0:T(8,128)(2,1)} %bitcast.16, ...), custom_call_target="tpu_custom_call" | custom-call | flops 1000 | tf_op jit(solution)/shard_map/pallas_call | solution.py:467
  4.4 3.0 %collective-permute-start = (f32[128,256]{1,0:T(8,128)S(1)}, f32[128,256]{1,0:T(8,128)S(1)}, u32[]{:S(2)}, u32[]{:S(2)}) collective-permute-start(f32[128,256]{1,0:T(8,128)S(1)} %get-tuple-element.78), channel_id=1, source_target_pairs={{0,4},{4,0},{8,12},{12,8},{16,20},{20,16},{24,28},{28,24},{1,5},{5... | collective-permute-start | bytes 393224 | tf_op jit(solution)/shard_map/ppermute | solution.py:479
  7.4 1.6 %collective-permute-start.1 = (f32[128,256]{1,0:T(8,128)S(1)}, f32[128,256]{1,0:T(8,128)S(1)}, u32[]{:S(2)}, u32[]{:S(2)}) collective-permute-start(f32[128,256]{1,0:T(8,128)S(1)} %get-tuple-element.79), channel_id=1, source_target_pairs={{0,8},{4,12},{8,0},{12,4},{16,24},{20,28},{24,16},{28,20},{1,9},{5... | collective-permute-start | bytes 393224 | tf_op jit(solution)/shard_map/ppermute | solution.py:479
  9.0 2.4 %shard_map.110 = (f32[2,256,128]{2,1,0:T(8,128)S(1)}, f32[2,256,256]{2,1,0:T(8,128)S(1)}, f32[128,256]{1,0:T(8,128)S(1)}, f32[128,256]{1,0:T(8,128)S(1)}, f32[2,...) custom-call(f32[1024,128]{1,0:T(8,128)S(1)} %get-tuple-element.68.refs_0_, f32[1024,128]{1,0:T(8,128)S(1)} %get-tuple-element.69.refs_1_, ...), custom_call_target="tpu_custom_call" | custom-call | flops 1000 | tf_op jit(solution)/shard_map/pallas_call | solution.py:467
  11.4 0.1 collective-permute-start.2
  11.5 0.0 collective-permute-done.refs_11_.refs_1_
  11.5 0.9 %collective-permute-done.1.refs_12_.refs_2_ = f32[128,256]{1,0:T(8,128)S(1)} collective-permute-done((f32[128,256]{1,0:T(8,128)S(1)}, f32[128,256]{1,0:T(8,128)S(1)}, u32[]{:S(2)}, u32[]{:S(2)}) %collective-permute-start.1) | collective-permute-done | bytes 131104 | tf_op jit(solution)/shard_map/ppermute | solution.py:479
  12.4 0.7 %copy-done.3 = f32[128]{0:T(128)S(1)} copy-done((f32[128]{0:T(128)S(1)}, f32[128]{0:T(128)}, u32[]{:S(2)}) %copy-start.3) | copy-done | bytes 536
  13.0 1.1 %shard_map.111 = (f32[1,128]{1,0:T(1,128)S(1)}, f32[4,256,128]{2,1,0:T(8,128)S(1)}, f32[4,128,128]{2,1,0:T(8,128)S(1)}, f32[4,128,128]{2,1,0:T(8,128)S(1)}, f32[...) custom-call(bf16[512,128]{1,0:T(8,128)(2,1)S(1)} %bitcast.21, f32[1,128]{1,0:T(1,128)S(1)} %bitcast.23, ...), custom_call_target="tpu_custom_call" | custom-call | flops 1000000000 | tf_op jit(solution)/shard_map/pallas_call | solution.py:467
  14.1 3.2 %collective-permute-done.2.refs_3_ = f32[128,256]{1,0:T(8,128)S(1)} collective-permute-done((f32[128,256]{1,0:T(8,128)S(1)}, f32[128,256]{1,0:T(8,128)S(1)}, u32[]{:S(2)}, u32[]{:S(2)}) %collective-permute-start.2) | collective-permute-done | bytes 131104 | tf_op jit(solution)/shard_map/ppermute | solution.py:479
  17.3 0.6 %shard_map.112 = (f32[4,128,256]{2,1,0:T(8,128)S(1)}, f32[4,128,128]{2,1,0:T(8,128)S(1)}, f32[128,128]{1,0:T(8,128)S(1)}) custom-call(f32[128,256]{1,0:T(8,128)S(1)} %get-tuple-element.83.refs_0_, f32[128,256]{1,0:T(8,128)S(1)} %collective-permute-done.refs_11_.refs_1_, f32[128,256]{1,0:T(8,128)S(1)} %collective-permute-done.1.refs_12_.refs_2_, ...), custom_call_target="tpu_custom_call" | custom-call | flops 1000 | tf_op jit(solution)/shard_map/pallas_call | solution.py:467
  17.9 2.6 %collective-permute-start.3 = (f32[128,128]{1,0:T(8,128)S(1)}, f32[128,128]{1,0:T(8,128)S(1)}, u32[]{:S(2)}, u32[]{:S(2)}) collective-permute-start(f32[128,128]{1,0:T(8,128)S(1)} %get-tuple-element.85), channel_id=1, source_target_pairs={{0,16},{4,20},{8,24},{12,28},{16,0},{20,4},{24,8},{28,12},{1,17},{... | collective-permute-start | bytes 196616 | tf_op jit(solution)/shard_map/ppermute | solution.py:559
  20.5 0.5 shard_map.113
  21.1 2.6 %collective-permute-done.3.refs_0_ = f32[128,128]{1,0:T(8,128)S(1)} collective-permute-done((f32[128,128]{1,0:T(8,128)S(1)}, f32[128,128]{1,0:T(8,128)S(1)}, u32[]{:S(2)}, u32[]{:S(2)}) %collective-permute-start.3) | collective-permute-done | bytes 65568 | tf_op jit(solution)/shard_map/ppermute | solution.py:559
  23.7 0.2 shard_map.114
  24.0 0.5 collective-permute-start.5
  24.5 0.0 collective-permute-start.6
  24.5 3.1 %collective-permute-start.4 = (f32[128,128]{1,0:T(8,128)S(1)}, f32[128,128]{1,0:T(8,128)S(1)}, u32[]{:S(2)}, u32[]{:S(2)}) collective-permute-start(f32[128,128]{1,0:T(8,128)S(1)} %get-tuple-element.89), channel_id=1, source_target_pairs={{0,12},{4,8},{8,4},{12,0},{16,28},{20,24},{24,20},{28,16},{1,13},{... | collective-permute-start | bytes 196616 | tf_op jit(solution)/shard_map/ppermute | solution.py:479
  27.5 1.3 %collective-permute-done.5.refs_4_.refs_1_.refs_10_ = f32[128,128]{1,0:T(8,128)S(1)} collective-permute-done((f32[128,128]{1,0:T(8,128)S(1)}, f32[128,128]{1,0:T(8,128)S(1)}, u32[]{:S(2)}, u32[]{:S(2)}) %collective-permute-start.5) | collective-permute-done | bytes 65568 | tf_op jit(solution)/shard_map/ppermute | solution.py:479
  28.9 0.0 collective-permute-done.6.refs_5_.refs_2_.refs_11_
  28.9 0.5 %shard_map.115 = (f32[8,128]{1,0:T(8,128)S(1)}, f32[2,128,128]{2,1,0:T(8,128)S(1)}, f32[2,128,128]{2,1,0:T(8,128)S(1)}, f32[128,128]{1,0:T(8,128)S(1)}, f32[128,128]{1,0:T(8,128)S(1)}) custom-call(bf16[512,128]{1,0:T(8,128)(2,1)S(1)} %bitcast.19, f32[1,128]{1,0:T(1,128)S(1)} %get-tuple-element.80.refs_4_.refs_1_, ...), custom_call_target="tpu_custom_call" | custom-call | flops 1000 | tf_op jit(solution)/shard_map/pallas_call | solution.py:467
  29.4 1.8 %collective-permute-start.7 = (f32[128,128]{1,0:T(8,128)S(1)}, f32[128,128]{1,0:T(8,128)S(1)}, u32[]{:S(2)}, u32[]{:S(2)}) collective-permute-start(f32[128,128]{1,0:T(8,128)S(1)} %get-tuple-element.99), channel_id=1, source_target_pairs={{0,4},{4,0},{8,12},{12,8},{16,20},{20,16},{24,28},{28,24},{1,5},{5... | collective-permute-start | bytes 196616 | tf_op jit(solution)/shard_map/ppermute | solution.py:479
  31.2 0.0 collective-permute-start.8
  31.2 0.0 collective-permute-done.4.refs_4_.refs_3_.refs_10_
  31.2 1.0 %shard_map.116 = (f32[8,128]{1,0:T(8,128)S(1)}, f32[2,128,128]{2,1,0:T(8,128)S(1)}, bf16[512,128]{1,0:T(8,128)(2,1)}, f32[128,128]{1,0:T(8,128)S(1)}, f32[128,128]{1,0:T(8,128)S(1)}) custom-call(bf16[512,128]{1,0:T(8,128)(2,1)S(1)} %bitcast.20, f32[1,128]{1,0:T(1,128)S(1)} %get-tuple-element.80.refs_4_.refs_1_, ...), custom_call_target="tpu_custom_call" | custom-call | flops 1000 | tf_op jit(solution)/shard_map/pallas_call | solution.py:467
  32.3 0.0 collective-permute-start.10
  32.3 1.7 %collective-permute-start.9 = (f32[128,128]{1,0:T(8,128)S(1)}, f32[128,128]{1,0:T(8,128)S(1)}, u32[]{:S(2)}, u32[]{:S(2)}) collective-permute-start(f32[128,128]{1,0:T(8,128)S(1)} %get-tuple-element.109), channel_id=1, source_target_pairs={{0,12},{4,8},{8,4},{12,0},{16,28},{20,24},{24,20},{28,16},{1,13},{... | collective-permute-start | bytes 196616 | tf_op jit(solution)/shard_map/ppermute | solution.py:479
  34.0 0.0 collective-permute-done.10
  34.0 1.5 %collective-permute-start.11 = (f32[8,128]{1,0:T(8,128)S(1)}, f32[8,128]{1,0:T(8,128)S(1)}, u32[]{:S(2)}, u32[]{:S(2)}) collective-permute-start(f32[8,128]{1,0:T(8,128)S(1)} %add.3.refs_5_), channel_id=1, source_target_pairs={{0,2},{1,3},{2,0},{3,1},{4,6},{5,7},{6,4},{7,5},{8,10},{9,11},{10,... | collective-permute-start | bytes 12296 | tf_op jit(solution)/shard_map/ppermute | solution.py:615
  35.6 0.0 collective-permute-done.7.refs_15_.refs_1_
  35.6 0.0 collective-permute-done.8.refs_16_.refs_2_
  35.6 1.7 %shard_map.117 = (f32[4,128,256]{2,1,0:T(8,128)S(1)}, bf16[512,128]{1,0:T(8,128)(2,1)}, f32[4,256,128]{2,1,0:T(8,128)S(1)}) custom-call(f32[128,128]{1,0:T(8,128)S(1)} %get-tuple-element.90.refs_5_.refs_0_.refs_11_, f32[128,128]{1,0:T(8,128)S(1)} %collective-permute-done.5.refs_4_.refs_1_.refs_10_, ...), custom_call_target="tpu_custom_call" | custom-call | flops 1000000000 | tf_op jit(solution)/shard_map/pallas_call | solution.py:467
  37.2 0.4 collective-permute-done.11.refs_6_
  37.6 0.1 collective-permute-done.9.refs_3_
  37.7 0.5 %shard_map.119 = (f32[8,128]{1,0:T(8,128)S(1)}, f32[4,128,128]{2,1,0:T(8,128)S(1)}, f32[136,128]{1,0:T(8,128)S(1)}) custom-call(f32[128,128]{1,0:T(8,128)S(1)} %get-tuple-element.108.refs_0_, f32[128,128]{1,0:T(8,128)S(1)} %collective-permute-done.7.refs_15_.refs_1_, f32[128,128]{1,0:T(8,128)S(1)} %collective-permute-done.8.refs_16_.refs_2_, ...), custom_call_target="tpu_custom_call" | custom-call | flops 1000 | tf_op jit(solution)/shard_map/pallas_call | solution.py:467
  38.2 2.8 %collective-permute-start.12 = (f32[136,128]{1,0:T(8,128)S(1)}, f32[136,128]{1,0:T(8,128)S(1)}, u32[]{:S(2)}, u32[]{:S(2)}) collective-permute-start(f32[136,128]{1,0:T(8,128)S(1)} %get-tuple-element.111), channel_id=1, source_target_pairs={{0,16},{4,20},{8,24},{12,28},{16,0},{20,4},{24,8},{28,12},{1,17},{... | collective-permute-start | bytes 208904 | tf_op jit(solution)/shard_map/ppermute | solution.py:646
  41.0 1.0 %shard_map.118 = (f32[4,256,128]{2,1,0:T(8,128)S(1)}, f32[4,256,128]{2,1,0:T(8,128)S(1)}) custom-call(f32[256,4]{1,0:T(8,128)S(1)} %get-tuple-element.66.refs_2_.refs_5_.refs_0_.refs_1_, f32[2,128,128]{2,1,0:T(8,128)S(1)} %get-tuple-element.96.refs_6_.refs_1_, f32[2,128,128]{2,1,0:T(8,128)S(1)} %get-tuple-element.97.refs_7_.refs_2_, ...), custom_call_target="tpu_custom_call" | custom-call | flops 1000 | tf_op jit(solution)/shard_map/pallas_call | solution.py:467
  42.0 3.0 %collective-permute-done.12.refs_0_ = f32[136,128]{1,0:T(8,128)S(1)} collective-permute-done((f32[136,128]{1,0:T(8,128)S(1)}, f32[136,128]{1,0:T(8,128)S(1)}, u32[]{:S(2)}, u32[]{:S(2)}) %collective-permute-start.12) | collective-permute-done | bytes 69664 | tf_op jit(solution)/shard_map/ppermute | solution.py:646
  45.0 0.3 shard_map.120
  45.3 1.3 %collective-permute-start.14 = (f32[136,128]{1,0:T(8,128)S(1)}, f32[136,128]{1,0:T(8,128)S(1)}, u32[]{:S(2)}, u32[]{:S(2)}) collective-permute-start(f32[136,128]{1,0:T(8,128)S(1)} %get-tuple-element.117), channel_id=1, source_target_pairs={{0,4},{4,0},{8,12},{12,8},{16,20},{20,16},{24,28},{28,24},{1,5},{5... | collective-permute-start | bytes 208904 | tf_op jit(solution)/shard_map/ppermute | solution.py:479
  46.6 0.0 collective-permute-start.15
  46.6 2.3 %collective-permute-start.13 = (f32[136,128]{1,0:T(8,128)S(1)}, f32[136,128]{1,0:T(8,128)S(1)}, u32[]{:S(2)}, u32[]{:S(2)}) collective-permute-start(f32[136,128]{1,0:T(8,128)S(1)} %get-tuple-element.115), channel_id=1, source_target_pairs={{0,12},{4,8},{8,4},{12,0},{16,28},{20,24},{24,20},{28,16},{1,13},{... | collective-permute-start | bytes 208904 | tf_op jit(solution)/shard_map/ppermute | solution.py:479
  48.8 1.6 %collective-permute-done.14.refs_8_.refs_13_ = f32[136,128]{1,0:T(8,128)S(1)} collective-permute-done((f32[136,128]{1,0:T(8,128)S(1)}, f32[136,128]{1,0:T(8,128)S(1)}, u32[]{:S(2)}, u32[]{:S(2)}) %collective-permute-start.14) | collective-permute-done | bytes 69664 | tf_op jit(solution)/shard_map/ppermute | solution.py:479
  50.4 0.5 collective-permute-done.15.refs_9_.refs_14_
  50.9 0.0 copy-done
  50.9 1.0 %shard_map.121 = (f32[256,4]{1,0:T(8,128)S(1)}, f32[2,256,128]{2,1,0:T(8,128)S(1)}, f32[2,256,128]{2,1,0:T(8,128)S(1)}) custom-call(bf16[1024,128]{1,0:T(8,128)(2,1)S(1)} %bitcast.17, f32[256,4]{1,0:T(8,128)S(1)} %get-tuple-element.66.refs_2_.refs_5_.refs_0_.refs_1_, f32[2,256,128]{2,1,0:T(8,128)S(1)} %get-tuple-element.67.refs_3_.refs_13_.refs_2_, ...), custom_call_target="tpu_custom_call" | custom-call | flops 1000 | tf_op jit(solution)/shard_map/pallas_call | solution.py:467
  51.8 0.0 collective-permute-done.13.refs_8_.refs_15_
  51.9 2.0 %shard_map.122 = (f32[8,128]{1,0:T(8,128)}, bf16[1024,128]{1,0:T(8,128)(2,1)}, bf16[1024,128]{1,0:T(8,128)(2,1)}, f32[1,128]{1,0:T(1,128)}) custom-call(bf16[1024,128]{1,0:T(8,128)(2,1)S(1)} %bitcast.18, f32[256,4]{1,0:T(8,128)S(1)} %get-tuple-element.66.refs_2_.refs_5_.refs_0_.refs_1_, f32[2,256,128]{2,1,0:T(8,128)S(1)} %get-tuple-element.67.refs_3_.refs_13_.refs_2_, ...), custom_call_target="tpu_custom_call" | custom-call | flops 1000 | tf_op jit(solution)/shard_map/pallas_call | solution.py:467
  (7 shorter events, 0.0 us)
Async XLA Ops:
  4.4 7.1 %collective-permute-start = (f32[128,256]{1,0:T(8,128)S(1)}, f32[128,256]{1,0:T(8,128)S(1)}, u32[]{:S(2)}, u32[]{:S(2)}) collective-permute-start(f32[128,256]{1,0:T(8,128)S(1)} %get-tuple-element.78), channel_id=1, source_target_pairs={{0,4},{4,0},{8,12},{12,8},{16,20},{20,16},{24,28},{28,24},{1,5},{5... | collective-permute-start | bytes 393224 | tf_op jit(solution)/shard_map/ppermute | solution.py:479
  7.4 5.0 %collective-permute-start.1 = (f32[128,256]{1,0:T(8,128)S(1)}, f32[128,256]{1,0:T(8,128)S(1)}, u32[]{:S(2)}, u32[]{:S(2)}) collective-permute-start(f32[128,256]{1,0:T(8,128)S(1)} %get-tuple-element.79), channel_id=1, source_target_pairs={{0,8},{4,12},{8,0},{12,4},{16,24},{20,28},{24,16},{28,20},{1,9},{5... | collective-permute-start | bytes 393224 | tf_op jit(solution)/shard_map/ppermute | solution.py:479
  9.0 3.4 %copy-start.2 = (bf16[128,4,128]{2,1,0:T(4,128)(2,1)S(1)}, bf16[128,4,128]{2,1,0:T(4,128)(2,1)}, u32[]{:S(2)}) copy-start(bf16[128,4,128]{2,1,0:T(4,128)(2,1)} %param.6) | copy-start | bytes 393220
  11.4 5.9 %collective-permute-start.2 = (f32[128,256]{1,0:T(8,128)S(1)}, f32[128,256]{1,0:T(8,128)S(1)}, u32[]{:S(2)}, u32[]{:S(2)}) collective-permute-start(f32[128,256]{1,0:T(8,128)S(1)} %get-tuple-element.84), channel_id=1, source_target_pairs={{0,12},{4,8},{8,4},{12,0},{16,28},{20,24},{24,20},{28,16},{1,13},{... | collective-permute-start | bytes 393224 | tf_op jit(solution)/shard_map/ppermute | solution.py:479
  12.4 0.7 %copy-start.3 = (f32[128]{0:T(128)S(1)}, f32[128]{0:T(128)}, u32[]{:S(2)}) copy-start(f32[128]{0:T(128)} %param.10) | copy-start | bytes 1540
  17.9 5.8 %collective-permute-start.3 = (f32[128,128]{1,0:T(8,128)S(1)}, f32[128,128]{1,0:T(8,128)S(1)}, u32[]{:S(2)}, u32[]{:S(2)}) collective-permute-start(f32[128,128]{1,0:T(8,128)S(1)} %get-tuple-element.85), channel_id=1, source_target_pairs={{0,16},{4,20},{8,24},{12,28},{16,0},{20,4},{24,8},{28,12},{1,17},{... | collective-permute-start | bytes 196616 | tf_op jit(solution)/shard_map/ppermute | solution.py:559
  23.7 5.1 %copy-start.1 = (bf16[128,4,128]{2,1,0:T(4,128)(2,1)S(1)}, bf16[128,4,128]{2,1,0:T(4,128)(2,1)}, u32[]{:S(2)}) copy-start(bf16[128,4,128]{2,1,0:T(4,128)(2,1)} %param.11) | copy-start | bytes 393220
  24.0 4.9 %collective-permute-start.5 = (f32[128,128]{1,0:T(8,128)S(1)}, f32[128,128]{1,0:T(8,128)S(1)}, u32[]{:S(2)}, u32[]{:S(2)}) collective-permute-start(f32[128,128]{1,0:T(8,128)S(1)} %get-tuple-element.91), channel_id=1, source_target_pairs={{0,4},{4,0},{8,12},{12,8},{16,20},{20,16},{24,28},{28,24},{1,5},{5... | collective-permute-start | bytes 196616 | tf_op jit(solution)/shard_map/ppermute | solution.py:479
  24.5 4.4 %collective-permute-start.6 = (f32[128,128]{1,0:T(8,128)S(1)}, f32[128,128]{1,0:T(8,128)S(1)}, u32[]{:S(2)}, u32[]{:S(2)}) collective-permute-start(f32[128,128]{1,0:T(8,128)S(1)} %get-tuple-element.92), channel_id=1, source_target_pairs={{0,8},{4,12},{8,0},{12,4},{16,24},{20,28},{24,16},{28,20},{1,9},{5... | collective-permute-start | bytes 196616 | tf_op jit(solution)/shard_map/ppermute | solution.py:479
  24.5 6.8 %collective-permute-start.4 = (f32[128,128]{1,0:T(8,128)S(1)}, f32[128,128]{1,0:T(8,128)S(1)}, u32[]{:S(2)}, u32[]{:S(2)}) collective-permute-start(f32[128,128]{1,0:T(8,128)S(1)} %get-tuple-element.89), channel_id=1, source_target_pairs={{0,12},{4,8},{8,4},{12,0},{16,28},{20,24},{24,20},{28,16},{1,13},{... | collective-permute-start | bytes 196616 | tf_op jit(solution)/shard_map/ppermute | solution.py:479
  29.4 6.1 %collective-permute-start.7 = (f32[128,128]{1,0:T(8,128)S(1)}, f32[128,128]{1,0:T(8,128)S(1)}, u32[]{:S(2)}, u32[]{:S(2)}) collective-permute-start(f32[128,128]{1,0:T(8,128)S(1)} %get-tuple-element.99), channel_id=1, source_target_pairs={{0,4},{4,0},{8,12},{12,8},{16,20},{20,16},{24,28},{28,24},{1,5},{5... | collective-permute-start | bytes 196616 | tf_op jit(solution)/shard_map/ppermute | solution.py:479
  31.2 4.3 %collective-permute-start.8 = (f32[128,128]{1,0:T(8,128)S(1)}, f32[128,128]{1,0:T(8,128)S(1)}, u32[]{:S(2)}, u32[]{:S(2)}) collective-permute-start(f32[128,128]{1,0:T(8,128)S(1)} %get-tuple-element.100), channel_id=1, source_target_pairs={{0,8},{4,12},{8,0},{12,4},{16,24},{20,28},{24,16},{28,20},{1,9},{5... | collective-permute-start | bytes 196616 | tf_op jit(solution)/shard_map/ppermute | solution.py:479
  32.3 1.7 %collective-permute-start.10 = (f32[8,128]{1,0:T(8,128)S(1)}, f32[8,128]{1,0:T(8,128)S(1)}, u32[]{:S(2)}, u32[]{:S(2)}) collective-permute-start(f32[8,128]{1,0:T(8,128)S(1)} %get-tuple-element.110), channel_id=1, source_target_pairs={{0,1},{1,0},{2,3},{3,2},{4,5},{5,4},{6,7},{7,6},{8,9},{9,8},{10,11... | collective-permute-start | bytes 12296 | tf_op jit(solution)/shard_map/ppermute | solution.py:611
  32.3 5.4 %collective-permute-start.9 = (f32[128,128]{1,0:T(8,128)S(1)}, f32[128,128]{1,0:T(8,128)S(1)}, u32[]{:S(2)}, u32[]{:S(2)}) collective-permute-start(f32[128,128]{1,0:T(8,128)S(1)} %get-tuple-element.109), channel_id=1, source_target_pairs={{0,12},{4,8},{8,4},{12,0},{16,28},{20,24},{24,20},{28,16},{1,13},{... | collective-permute-start | bytes 196616 | tf_op jit(solution)/shard_map/ppermute | solution.py:479
  34.0 3.6 %collective-permute-start.11 = (f32[8,128]{1,0:T(8,128)S(1)}, f32[8,128]{1,0:T(8,128)S(1)}, u32[]{:S(2)}, u32[]{:S(2)}) collective-permute-start(f32[8,128]{1,0:T(8,128)S(1)} %add.3.refs_5_), channel_id=1, source_target_pairs={{0,2},{1,3},{2,0},{3,1},{4,6},{5,7},{6,4},{7,5},{8,10},{9,11},{10,... | collective-permute-start | bytes 12296 | tf_op jit(solution)/shard_map/ppermute | solution.py:615
  38.2 6.8 %collective-permute-start.12 = (f32[136,128]{1,0:T(8,128)S(1)}, f32[136,128]{1,0:T(8,128)S(1)}, u32[]{:S(2)}, u32[]{:S(2)}) collective-permute-start(f32[136,128]{1,0:T(8,128)S(1)} %get-tuple-element.111), channel_id=1, source_target_pairs={{0,16},{4,20},{8,24},{12,28},{16,0},{20,4},{24,8},{28,12},{1,17},{... | collective-permute-start | bytes 208904 | tf_op jit(solution)/shard_map/ppermute | solution.py:646
  45.0 5.9 %copy-start = (bf16[128,2,4,128]{3,2,1,0:T(4,128)(2,1)S(1)}, bf16[128,2,4,128]{3,2,1,0:T(4,128)(2,1)}, u32[]{:S(2)}) copy-start(bf16[128,2,4,128]{3,2,1,0:T(4,128)(2,1)} %param.7) | copy-start | bytes 786436
  45.3 5.1 %collective-permute-start.14 = (f32[136,128]{1,0:T(8,128)S(1)}, f32[136,128]{1,0:T(8,128)S(1)}, u32[]{:S(2)}, u32[]{:S(2)}) collective-permute-start(f32[136,128]{1,0:T(8,128)S(1)} %get-tuple-element.117), channel_id=1, source_target_pairs={{0,4},{4,0},{8,12},{12,8},{16,20},{20,16},{24,28},{28,24},{1,5},{5... | collective-permute-start | bytes 208904 | tf_op jit(solution)/shard_map/ppermute | solution.py:479
  46.6 4.3 %collective-permute-start.15 = (f32[136,128]{1,0:T(8,128)S(1)}, f32[136,128]{1,0:T(8,128)S(1)}, u32[]{:S(2)}, u32[]{:S(2)}) collective-permute-start(f32[136,128]{1,0:T(8,128)S(1)} %get-tuple-element.118), channel_id=1, source_target_pairs={{0,8},{4,12},{8,0},{12,4},{16,24},{20,28},{24,16},{28,20},{1,9},{5... | collective-permute-start | bytes 208904 | tf_op jit(solution)/shard_map/ppermute | solution.py:479
  46.6 5.3 %collective-permute-start.13 = (f32[136,128]{1,0:T(8,128)S(1)}, f32[136,128]{1,0:T(8,128)S(1)}, u32[]{:S(2)}, u32[]{:S(2)}) collective-permute-start(f32[136,128]{1,0:T(8,128)S(1)} %get-tuple-element.115), channel_id=1, source_target_pairs={{0,12},{4,8},{8,4},{12,0},{16,28},{20,24},{24,20},{28,16},{1,13},{... | collective-permute-start | bytes 208904 | tf_op jit(solution)/shard_map/ppermute | solution.py:479

commit v4 on v3

v4 whole, which is shorter than its diff:
```python
import functools
import types

import jax
import jax.numpy as jnp
from jax import lax
from jax.experimental import pallas as pl
from jax.experimental.pallas import tpu as pltpu
from jax.sharding import PartitionSpec as P

EPS = 1e-06
GROUP = 4
HALF = 128
BASE = 16
F32 = jnp.float32
BF16 = jnp.bfloat16


def split(x):
    high = x.astype(BF16)
    return high, (x - high.astype(F32)).astype(BF16)


def mm(a, b, ta=False, tb=False):
    (ah, al), (bh, bl) = split(a), split(b)
    if ta:
        ah, al = ah.T, al.T
    dims = (((1,), (1 if tb else 0,)), ((), ()))
    if b.shape[0 if tb else 1] > 128:
        left = jnp.concatenate([ah, ah, al], axis=1)
        right = jnp.concatenate([bh, bl, bh], axis=1 if tb else 0)
        return lax.dot_general(left, right, dims, preferred_element_type=F32)
    left = jnp.concatenate([ah, al], axis=1)
    if tb:
        right = jnp.concatenate(
            [jnp.concatenate([bh, bh], axis=1), jnp.concatenate([bl, bl], axis=1)], axis=0
        )
        width = b.shape[0]
    else:
        right = jnp.concatenate([bh, bl], axis=1)
        right = jnp.concatenate([right, right], axis=0)
        width = b.shape[1]
    both = lax.dot_general(left, right, dims, preferred_element_type=F32)
    return both[:, :width] + both[:, width:]


def exact_nt(a, b):
    return lax.dot_general(a, b, (((1,), (1,)), ((), ())), preferred_element_type=F32)


def iota(shape, dim):
    return lax.broadcasted_iota(jnp.int32, shape, dim)


def row_of(column):
    square = jnp.where(iota((HALF, HALF), 0) == iota((HALF, HALF), 1), column, 0.0)
    return jnp.sum(square, axis=0, keepdims=True)


def places(steps, j):
    shape = (steps, steps // 2)
    return (iota(shape, 0) == 2 * iota(shape, 1) + j).astype(F32)


def pick(a, b, ta=False, tb=False):
    dims = (((0 if ta else 1,), (1 if tb else 0,)), ((), ()))
    return lax.dot_general(
        a, b, dims, precision=lax.Precision.HIGHEST, preferred_element_type=F32
    )


def rate_column(rates, head):
    return jnp.sum(jnp.where(iota(rates.shape, 1) == head, rates, 0.0), axis=1, keepdims=True)


def small_inverses(lowers, rate_rows):
    blocks = HALF // BASE
    lane = iota((BASE, HALF), 1)
    row = iota((BASE, HALF), 0)
    jobs = range(len(lowers))
    packed = []
    for lower in lowers:
        one = lower[:BASE]
        for b in range(1, blocks):
            one = jnp.where(lane // BASE == b, lower[b * BASE : (b + 1) * BASE], one)
        packed.append(one)
    scaled = [packed[n] * rate_rows[n] for n in jobs]
    for j in range(BASE - 1):
        index = lane // BASE * BASE + j
        factors = [
            jnp.take_along_axis(scaled[n], index, axis=1, mode="promise_in_bounds") for n in jobs
        ]
        packed = [
            packed[n] - jnp.where(row > j, factors[n], 0.0) * packed[n][j : j + 1] for n in jobs
        ]
    return [
        jnp.concatenate(
            [jnp.where(lane // BASE == b, one, 0.0) for b in range(blocks)], axis=0
        )
        for one in packed
    ]


def place_in(group):
    return lax.rem(lax.axis_index("seq"), group)


def strided(ref, head, rows):
    return ref[pl.ds(head, rows, stride=ref.shape[0] // rows), :]


def store_strided(ref, head, value):
    rows = value.shape[0]
    ref[pl.ds(head, rows, stride=ref.shape[0] // rows), :] = value


SOONER, LATER = (1, 2), (3, 0)


def take(pairs, heads):
    order = SOONER + LATER
    return [pairs[order.index(h) // 2][order.index(h) % 2] for h in heads]


def inverse_norm(rows):
    return lax.rsqrt(jnp.sum(rows * rows, axis=1, keepdims=True) + EPS)


def unit_grad(inv, unit, grad):
    return inv * (grad - unit * jnp.sum(unit * grad, axis=1, keepdims=True))


def chunk(me, heads, kf, vf, rates, rows, o, wait):
    steps = rates.shape[0]
    strict = iota((HALF, HALF), 1) < iota((HALF, HALF), 0)
    rate = [rate_column(rates, me ^ h) for h in heads]
    rate_rows = [rows[pl.ds(me ^ h, 1), :] for h in heads]
    sides = [slice(0, HALF), slice(HALF, 2 * HALF)]
    raws = [strided(kf, me ^ h, steps) for h in heads]
    heads = range(len(heads)) if wait is None else heads
    count = range(len(raws))
    invs = [inverse_norm(raw) for raw in raws]
    inv_rows = [[row_of(inv[side]) for side in sides] for inv in invs]
    units = [raw * inv for raw, inv in zip(raws, invs)]
    raw16 = [raw.astype(BF16) for raw in raws]
    jobs = [(i, b) for i in count for b in range(2)]
    diag = {
        (i, b): jnp.where(
            strict,
            exact_nt(raw16[i][sides[b]], raw16[i][sides[b]]) * invs[i][sides[b]] * inv_rows[i][b],
            0.0,
        )
        for i, b in jobs
    }
    cross = [
        exact_nt(raw16[i][sides[1]], raw16[i][sides[0]]) * invs[i][sides[1]] * inv_rows[i][0]
        for i in count
    ]
    across = {(i, b): rate_rows[i][:, sides[b]] for i, b in jobs}
    inverse = dict(zip(jobs, small_inverses([diag[n] for n in jobs], [across[n] for n in jobs])))
    size = BASE
    while size < HALF:
        r, c = iota((HALF, HALF), 0) // size, iota((HALF, HALF), 1) // size
        below = (r % 2 == 1) & (c == r - 1)
        part = {n: jnp.where(below, diag[n], 0.0) for n in jobs}
        right = {n: part[n] - mm(part[n] * across[n], inverse[n]) for n in jobs}
        inverse = {
            n: inverse[n] + right[n] - mm(inverse[n] * across[n], right[n]) for n in jobs
        }
        size *= 2
    right = [cross[i] - mm(cross[i] * across[i, 0], inverse[i, 0]) for i in count]
    joined = [right[i] - mm(inverse[i, 1] * across[i, 1], right[i]) for i in count]
    vals = vf()
    both = [jnp.concatenate([units[i], vals[i]], axis=1) for i in count]
    top = [both[i][:HALF] - mm(inverse[i, 0] * across[i, 0], both[i][:HALF]) for i in count]
    low = [
        jnp.concatenate([joined[i] * across[i, 0], inverse[i, 1] * across[i, 1]], axis=1)
        for i in count
    ]
    bottom = [both[i][HALF:] - mm(low[i], both[i]) for i in count]
    solved = [jnp.concatenate([top[i], bottom[i]], axis=0) for i in count]
    eye = (iota((HALF, 2 * HALF), 0) == iota((HALF, 2 * HALF), 1)).astype(F32)
    sign = jnp.where(iota((HALF, 2 * HALF), 1) < HALF, -1.0, 1.0)
    ends = [eye + sign * mm(units[i], rate[i] * solved[i], ta=True) for i in count]
    for i in count:
        o.maps[i][:, : 2 * HALF] = ends[i]
        o.unit[i] = units[i]
        o.inverse[i, :HALF, :HALF] = inverse[i, 0]
        o.inverse[i, :HALF, HALF:] = jnp.zeros((HALF, HALF), F32)
        o.inverse[i, HALF:, :HALF] = joined[i]
        o.inverse[i, HALF:, HALF:] = inverse[i, 1]
        o.w[i] = solved[i][:, :HALF]
        o.e[i] = solved[i][:, HALF:]
    return units, [x[:, :HALF] for x in solved], [x[:, HALF:] for x in solved]


def first_kernel(group, heads, n, o, k16, v16, q16, g16, p32, sems):
    copies = [
        pltpu.make_async_copy(src, dst, sems.at[c])
        for c, (src, dst) in enumerate(
            (
                (n.packed, p32),
                (n.k, k16),
                (n.v, v16),
                (n.q, q16),
                (n.og, g16),
                (n.gain, o.gain),
            )
        )
    ]
    for copy in copies:
        copy.start()
    me = place_in(group)
    steps, count = o.rates.shape
    copies[0].wait()
    packed = p32[...]
    own, place = [packed[:count], packed[count:]], [places(steps, j) for j in range(2)]
    rates = pick(place[0], own[0], tb=True) + pick(place[1], own[1], tb=True)
    o.rates[...] = rates
    o.rows[...] = pick(own[0], place[0], tb=True) + pick(own[1], place[1], tb=True)
    copies[1].wait()
    o.kf[...] = k16[...].astype(F32)
    copies[2].wait()
    o.vf[...] = v16[...].astype(F32)
    for copy in copies[3:]:
        copy.wait()
    o.qf[...] = q16[...].astype(F32)
    o.gf[...] = g16[...].astype(F32)
    tokens = steps // 2
    vals = [strided(o.vf, me ^ h, steps) for h in heads]
    qs = [strided(o.qf, me ^ h, tokens) for h in heads]
    given = [strided(o.gf, me ^ h, tokens) for h in heads]
    solved = chunk(me, heads, o.kf, lambda: vals, rates, o.rows, o, None)
    reads(heads, qs, given, rates, *solved, me, o)


def next_kernel(group, heads, n, o):
    me = place_in(group)
    steps = n.rates.shape[0]
    vals = [strided(n.vf, me ^ h, steps) for h in heads]
    chunk(me, heads, n.kf, lambda: vals, n.rates[...], n.rows, o, None)


def reads(heads, qs, given, rates, keys, w, e, me, o):
    tokens = qs[0].shape[0]
    steps = 2 * tokens
    count = range(len(heads))
    seen = iota((tokens, steps), 1) <= 2 * iota((tokens, steps), 0) + 1
    rate = [rate_column(rates, me ^ h) for h in heads]
    weighted = [rate[i] * jnp.concatenate([w[i], e[i]], axis=1) for i in count]
    units = [q * inverse_norm(q) for q in qs]
    scores = [jnp.where(seen, mm(units[i], keys[i], tb=True), 0.0) for i in count]
    rows = [mm(scores[i], weighted[i]) for i in count]
    for i in count:
        o.q_unit[i] = units[i]
        o.scores[i] = scores[i]
        out = o.reads[i]
        skip = out.shape[1] - 3 * HALF
        out[:, skip : skip + HALF] = units[i] - rows[i][:, :HALF]
        out[:, skip + HALF : skip + 2 * HALF] = rows[i][:, HALF:]
        out[:, skip + 2 * HALF :] = given[i]


def second_kernel(group, heads, n, o):
    me = place_in(group)
    tokens = o.scores.shape[1]
    rates = n.rates[...]
    qs = [strided(n.qf, me ^ h, tokens) for h in heads]
    given = [strided(n.gf, me ^ h, tokens) for h in heads]
    keys, w, e = (take(x, heads) for x in (n.unit, n.w, n.e))
    every = range(o.kx.shape[0])
    rate = [rate_column(rates, me ^ i) for i in every]
    units, inverse = (take(x, every) for x in (n.unit, n.inverse))
    spread = [units[i] - mm(inverse[i], rate[i] * units[i], ta=True) for i in every]
    reads(heads, qs, given, rates, keys, w, e, me, o)
    for i in every:
        o.kx[i] = spread[i]


def join_kernel(group, n, o):
    me = place_in(group)
    for i, piece in enumerate(n.maps):
        o.maps[me ^ i] = piece[:, : 2 * HALF]
    state = jnp.zeros((HALF, HALF), F32)
    for j in range(group):
        o.starts[j] = state
        own = o.maps[j, :, HALF:]
        state = own if j == 0 else mm(o.maps[j, :, :HALF], state) + own
    o.total[...] = state


def products_kernel(group, n, o):
    eye = (iota((HALF, HALF), 0) == iota((HALF, HALF), 1)).astype(F32)
    steps = [n.maps[j, :, :HALF] for j in range(group)]
    before, after = [eye, steps[0]], [eye, steps[-1]]
    for j in range(1, group):
        before.append(mm(steps[j], before[-1]))
        after.append(mm(after[-1], steps[-1 - j]))
    for j in range(group + 1):
        o.before[j] = before[j]
    for j in range(group):
        o.after[j] = after[group - 1 - j]


def spread_kernel(group, side, n, o):
    me = place_in(group)
    entry = n.entry[:HALF, :]
    if side is not None:
        entry = jnp.where(lax.axis_index("seq") // group == side, entry, 0.0)
    starts = [n.starts[me ^ i] for i in range(group)]
    maps = [n.maps[me ^ i] for i in range(group)]
    values = [starts[i] + mm(maps[i], entry, ta=True) for i in range(group)]
    for i, out in enumerate(o.adjoints):
        out[:HALF, :] = values[i]
        out[HALF:, :] = n.entry[HALF:, :]


def normed_and_grads(queries, parts, states, given, gain):
    count = range(len(queries))
    reads = [parts[i] + mm(queries[i], states[i]) for i in count]
    inv_rms = [lax.rsqrt(jnp.mean(read * read, axis=1, keepdims=True) + EPS) for read in reads]
    normal = [reads[i] * inv_rms[i] for i in count]
    scaled = [given[i] * gain for i in count]
    grads = [
        inv_rms[i] * (scaled[i] - normal[i] * jnp.mean(scaled[i] * normal[i], axis=1, keepdims=True))
        for i in count
    ]
    return normal, grads, sum(jnp.sum(given[i] * normal[i], axis=0, keepdims=True) for i in count)


def owner_kernel(group, side, n, o, packed):
    me = place_in(group)
    entry = n.entry[...]
    if side is not None:
        entry = jnp.where(lax.axis_index("seq") // group == side, entry, 0.0)
    for i, piece in enumerate(n.reads):
        packed[me ^ i] = piece[:, piece.shape[1] - 3 * HALF :]
    gain = n.gain[...]
    places_ = range(group)
    maps = [n.maps[j, :, :HALF] for j in places_]
    before = [n.before[j] for j in places_]
    starts = [n.starts[j] for j in places_]
    queries, parts, given = (
        [packed[j, :, c * HALF : (c + 1) * HALF] for j in places_] for c in range(3)
    )
    states = [starts[j] + mm(before[j], entry) if j else starts[j] + entry for j in places_]
    _, grads, gain_part = normed_and_grads(queries, parts, states, given, gain)
    adjoints = [mm(queries[j], grads[j], ta=True) for j in places_]
    chain = [jnp.zeros((HALF, HALF), F32), adjoints[-1]]
    for j in reversed(range(group - 1)):
        chain.append(mm(maps[j], chain[-1], ta=True) + adjoints[j])
    for j in places_:
        o.starts[j] = chain[group - 1 - j]
        o.entries[j] = states[j]
    o.total[:HALF, :] = chain[-1]
    for i in places_:
        o.states[i][:HALF, :] = o.entries[me ^ i]
        o.states[i][HALF:, :] = jnp.broadcast_to(gain_part, (8, HALF))
    o.total[HALF:, :] = jnp.broadcast_to(gain_part, (8, HALF))


def tokens_kernel(group, n, o, of, df):
    me = place_in(group)
    heads, tokens, steps = range(len(n.reads)), n.reads[0].shape[0], n.rates.shape[0]
    gain = n.gain[...]
    rates = n.rates[...]
    queries, parts, given = (
        [
            ref[:, ref.shape[1] - (3 - c) * HALF : ref.shape[1] - (2 - c) * HALF]
            for ref in n.reads
        ]
        for c in range(3)
    )
    states = [ref[:HALF, :] for ref in n.states]
    seen = iota((tokens, steps), 1) <= 2 * iota((tokens, steps), 0) + 1
    raws = [strided(n.qf, me ^ i, tokens) for i in heads]
    keys, w, e, units, inverse, scores = (
        take(x, heads) for x in (n.unit, n.w, n.e, n.q_unit, n.inverse, n.scores)
    )
    rate = [rate_column(rates, me ^ i) for i in heads]
    invs = [inverse_norm(raw) for raw in raws]
    errs = [e[i] - mm(w[i], states[i]) for i in heads]
    normal, grads, _ = normed_and_grads(queries, parts, states, given, gain)
    pseudo = [rate[i] * errs[i] for i in heads]
    d_scores = [jnp.where(seen, mm(grads[i], pseudo[i], tb=True), 0.0) for i in heads]
    d_pseudo = [mm(scores[i], grads[i], ta=True) for i in heads]
    d_units = [mm(grads[i], states[i], tb=True) + mm(d_scores[i], keys[i]) for i in heads]
    z = [d_pseudo[i] - mm(inverse[i], rate[i] * d_pseudo[i], ta=True) for i in heads]
    d_keys = [mm(d_scores[i], units[i], ta=True) for i in heads]
    done = [unit_grad(invs[i], units[i], d_units[i]) for i in heads]
    for i in heads:
        o.err[i] = errs[i]
        o.dk[i] = d_keys[i]
        o.z[i] = z[i]
        store_strided(of, me ^ i, gain * normal[i])
        store_strided(df, me ^ i, done[i])
    o.normed[...] = of[...].astype(BF16)
    o.dq[...] = df[...].astype(BF16)


def gain_kernel(n, o):
    o.gain[...] = sum(ref[HALF : HALF + 1, :] for ref in n.states + n.adjoints)


def last_kernel(group, n, o, df, vf):
    me = place_in(group)
    rates = n.rates[...]
    steps, count = rates.shape
    heads = range(count)
    rate = [rate_column(rates, me ^ i) for i in heads]
    raws = [strided(n.kf, me ^ i, steps) for i in heads]
    adjoints = [ref[:HALF, :] for ref in n.adjoints]
    states = [ref[:HALF, :] for ref in n.states]
    units = take(n.unit, heads)
    errs, kx, z0, dk0 = ([x[i] for i in heads] for x in (n.err, n.kx, n.z, n.dk))
    z = [z0[i] + mm(kx[i], adjoints[i]) for i in heads]
    invs = [inverse_norm(raw) for raw in raws]
    pseudo = [rate[i] * errs[i] for i in heads]
    d_values = [rate[i] * z[i] for i in heads]
    below = iota((steps, steps), 1) < iota((steps, steps), 0)
    above = iota((steps, steps), 1) > iota((steps, steps), 0)
    d_grams = [
        jnp.where(
            below,
            mm(d_values[i], pseudo[i], tb=True),
            jnp.where(above, mm(pseudo[i], d_values[i], tb=True), 0.0),
        )
        for i in heads
    ]
    d_units = [
        dk0[i]
        + mm(pseudo[i], adjoints[i], tb=True)
        - mm(d_values[i], states[i], tb=True)
        - mm(d_grams[i], units[i])
        for i in heads
    ]
    done = [unit_grad(invs[i], units[i], d_units[i]) for i in heads]
    d_rates = jnp.zeros(rates.shape, F32)
    for i in heads:
        d_rate = jnp.sum(z[i] * errs[i], axis=1, keepdims=True)
        d_rates = jnp.where(iota(rates.shape, 1) == me ^ i, d_rate, d_rates)
        store_strided(vf, me ^ i, d_values[i])
        store_strided(df, me ^ i, done[i])
    o.dk[...] = df[...].astype(BF16)
    o.dv[...] = vf[...].astype(BF16)
    for j in range(2):
        o.db[j * count : (j + 1) * count, :] = pick(d_rates, places(steps, j), ta=True)


def f32(*shape):
    return pltpu.VMEM(shape, F32)


def out(dtype, *shape):
    return jax.ShapeDtypeStruct(shape, dtype)


def call(body, ins, outs, scratch=(), hbm=(), after=(), flops=1000, shared={}):
    names = [name for name in ins]
    flat, tree = jax.tree.flatten([ins[name] for name in names])
    outs = dict(outs)
    flat_outs, out_tree = jax.tree.flatten(outs)
    specs = jax.tree.leaves(
        [
            jax.tree.map(
                lambda _: pl.BlockSpec(memory_space=pltpu.HBM if name in hbm else pltpu.VMEM),
                ins[name],
            )
            for name in names
        ]
    )
    after = list(after)

    def kernel(*refs):
        values = jax.tree.unflatten(tree, refs[: len(flat)])
        start = len(flat) + len(after)
        results = jax.tree.unflatten(out_tree, refs[start : start + len(flat_outs)])
        results.update({name: results[old] for name, old in shared.items()})
        body(
            types.SimpleNamespace(**dict(zip(names, values))),
            types.SimpleNamespace(**results),
            *refs[start + len(flat_outs) :],
        )

    results = pl.pallas_call(
        kernel,
        out_shape=flat_outs,
        in_specs=specs + [pl.BlockSpec(memory_space=pl.ANY)] * len(after),
        scratch_shapes=[pltpu.VMEM(s, F32) if isinstance(s, tuple) else s for s in scratch],
        compiler_params=pltpu.CompilerParams(vmem_limit_bytes=16 * 1024 * 1024),
        cost_estimate=pl.CostEstimate(flops=flops, bytes_accessed=0, transcendentals=0),
    )(*flat, *after)
    return types.SimpleNamespace(**jax.tree.unflatten(out_tree, results))


def swap(piece, i):
    return lax.ppermute(piece, "seq", [(d, d ^ i) for d in range(lax.axis_size("seq"))])


def local(queries, keys, values, betas, gain, out_grad):
    tokens, heads, dim = queries.shape
    substeps = keys.shape[1]
    steps = tokens * substeps
    group = GROUP
    count = lax.axis_size("seq")
    groups = count // group
    two = groups == 2
    bind = functools.partial
    q2 = queries.reshape(tokens * heads, dim)
    g2 = out_grad.reshape(tokens * heads, dim)
    k2 = keys.reshape(steps * heads, dim)
    v2 = values.reshape(steps * heads, dim)
    packed = betas.transpose(1, 2, 0).reshape(substeps * heads, tokens)

    def chunk_outs(width):
        return dict(
            maps=[f32(dim, width) for _ in SOONER],
            unit=f32(2, steps, dim),
            inverse=f32(2, steps, steps),
            w=f32(2, steps, dim),
            e=f32(2, steps, dim),
        )

    read_outs = dict(q_unit=f32(2, tokens, dim), scores=f32(2, tokens, steps))
    a = call(
        bind(first_kernel, group, SOONER),
        {
            name: pltpu.with_memory_space_constraint(x, pltpu.HBM)
            for name, x in (
                ("k", k2),
                ("v", v2),
                ("q", q2),
                ("og", g2),
                ("packed", packed),
                ("gain", gain.reshape(1, dim)),
            )
        },
        dict(
            chunk_outs(5 * dim),
            **read_outs,
            rates=f32(steps, heads),
            rows=f32(heads, steps),
            kf=f32(steps * heads, dim),
            vf=f32(steps * heads, dim),
            qf=f32(tokens * heads, dim),
            gf=f32(tokens * heads, dim),
            gain=f32(1, dim),
        ),
        scratch=[pltpu.VMEM((steps * heads, dim), BF16)] * 2
        + [pltpu.VMEM((tokens * heads, dim), BF16)] * 2
        + [(substeps * heads, tokens), pltpu.SemaphoreType.DMA((6,))],
        hbm=("k", "v", "q", "og", "packed", "gain"),
        shared=dict(reads="maps"),
    )
    got = {h: swap(a.maps[i], h) for i, h in enumerate(SOONER)}
    b = call(
        bind(next_kernel, group, LATER),
        dict(kf=a.kf, vf=a.vf, rates=a.rates, rows=a.rows),
        chunk_outs(2 * dim),
    )
    for i, h in enumerate(LATER):
        got[h] = swap(b.maps[i], h) if h else b.maps[i]
    unit, inverse, w, e = (
        [getattr(x, name) for x in (a, b)] for name in ("unit", "inverse", "w", "e")
    )
    rates = a.rates
    c = call(
        bind(second_kernel, group, LATER),
        dict(qf=a.qf, gf=a.gf, rates=rates, unit=unit, inverse=inverse, w=w, e=e),
        dict(read_outs, reads=[f32(tokens, 3 * dim)] * 2, kx=f32(heads, steps, dim)),
        after=[got[SOONER[0]]],
        flops=10**9,
    )
    q_unit, scores = [a.q_unit, c.q_unit], [a.scores, c.scores]
    own_reads, got_reads = {}, {}
    for i in range(2):
        own_reads[SOONER[i]], own_reads[LATER[i]] = a.maps[i], c.reads[i]
        got_reads[SOONER[i]] = got[SOONER[i]]
        got_reads[LATER[i]] = swap(c.reads[i], LATER[i]) if LATER[i] else c.reads[i]
    own_reads, got_reads = ([x[h] for h in range(heads)] for x in (own_reads, got_reads))
    j = call(
        bind(join_kernel, group),
        dict(maps=[got[h] for h in range(heads)]),
        dict(
            starts=f32(group, dim, dim), total=f32(dim, dim), maps=f32(group, dim, 2 * dim)
        ),
        after=[c.kx],
    )
    ahead = [(d, d + group) for d in range(count - group)]
    behind = [(d + group, d) for d in range(count - group)]
    across = [(d, d ^ group) for d in range(count)]
    entry = lax.ppermute(j.total, "seq", across if two else ahead)
    p = call(
        bind(products_kernel, group),
        dict(maps=j.maps),
        dict(before=f32(group + 1, dim, dim), after=f32(group, dim, dim)),
    )
    for _ in range(groups - 2):
        passed = jnp.dot(p.before[group], entry, precision=lax.Precision.HIGHEST) + j.total
        entry = lax.ppermute(passed, "seq", ahead)
    own = call(
        bind(owner_kernel, group, 1 if two else None),
        dict(
            entry=entry,
            reads=got_reads,
            gain=a.gain,
            maps=j.maps,
            before=p.before,
            starts=j.starts,
        ),
        dict(
            starts=f32(group, dim, dim),
            entries=f32(group, dim, dim),
            total=f32(dim + 8, dim),
            states=[f32(dim + 8, dim)] * heads,
        ),
        scratch=[(group, tokens, 3 * dim)],
    )
    entry = lax.ppermute(own.total, "seq", across if two else behind)
    for _ in range(groups - 2):
        passed = jnp.dot(p.before[group].T, entry[:dim], precision=lax.Precision.HIGHEST)
        entry = lax.ppermute(own.total.at[:dim].add(passed), "seq", behind)
    states = [own.states[0]] + [swap(own.states[h], h) for h in range(1, heads)]
    adjoints = call(
        bind(spread_kernel, group, 0 if two else None),
        dict(entry=entry, starts=own.starts, maps=p.after),
        dict(adjoints=[f32(dim + 8, dim)] * heads),
    ).adjoints
    first_adjoint = adjoints[0]
    adjoints = [adjoints[0]] + [swap(adjoints[h], h) for h in range(1, heads)]
    t = call(
        bind(tokens_kernel, group),
        dict(
            states=states,
            reads=own_reads,
            gain=a.gain,
            qf=a.qf,
            rates=rates,
            w=w,
            e=e,
            q_unit=q_unit,
            unit=unit,
            scores=scores,
            inverse=inverse,
        ),
        dict(
            normed=out(BF16, tokens * heads, dim),
            dq=out(BF16, tokens * heads, dim),
            err=f32(heads, steps, dim),
            dk=f32(heads, steps, dim),
            z=f32(heads, steps, dim),
        ),
        scratch=[(tokens * heads, dim)] * 2,
        after=[first_adjoint],
    )
    sums = call(
        gain_kernel, dict(states=states, adjoints=adjoints), dict(gain=f32(1, dim)), after=[t.err]
    ).gain
    size = lax.axis_size("head")
    last = call(
        bind(last_kernel, group),
        dict(
            kf=a.kf,
            rates=rates,
            unit=unit,
            err=t.err,
            kx=c.kx,
            z=t.z,
            dk=t.dk,
            adjoints=adjoints,
            states=states,
        ),
        dict(
            dk=out(BF16, steps * heads, dim),
            dv=out(BF16, steps * heads, dim),
            db=out(F32, substeps * heads, tokens),
        ),
        scratch=[(steps * heads, dim)] * 2,
        after=[sums],
    )
    if two:
        gain_sum = sums + sum(
            lax.ppermute(sums, "head", [(d, d ^ flip) for d in range(size)])
            for flip in range(1, size)
        )
    else:
        gain_sum = lax.psum(own.total[dim:][:1], ("seq", "head"))
    return (
        t.normed.reshape(tokens, heads, dim),
        t.dq.reshape(tokens, heads, dim),
        last.dk.reshape(tokens, substeps, heads, dim),
        last.dv.reshape(tokens, substeps, heads, dim),
        last.db.reshape(substeps, heads, tokens).transpose(2, 0, 1),
        gain_sum.reshape(dim),
    )


def solution(mesh):
    return jax.shard_map(
        local,
        mesh=mesh,
        in_specs=(
            P("seq", "head", None),
            P("seq", None, "head", None),
            P("seq", None, "head", None),
            P("seq", None, "head"),
            P(),
            P("seq", "head", None),
        ),
        out_specs=(
            P("seq", "head", None),
            P("seq", "head", None),
            P("seq", None, "head", None),
            P("seq", None, "head", None),
            P("seq", None, "head"),
            P(),
        ),
        check_vma=False,
    )
```

time: 54.1 us -> 48 us (0.89)
  waiting for transfers between devices: 13.5 us -> 8.63 us
  Pallas kernels: 16.6 us -> 15.3 us
  local copies, waits for them, and re-layouts: 0.66 us -> 0 us
    ppermute x3 -> x4, waiting for transfers between devices: 3.35 us -> 0.01 us  [the longest x3 0.01 us: local(): lax.ppermute(sums, 'head', [(d, d ^ flip) for d in range(size)])]
    pallas_call x14 -> x10, Pallas kernels: 16.6 us -> 15.3 us  [call(): pl.pallas_call(kernel, out_shape=flat_outs, in_specs=specs + [pl.BlockSpe...]
    ppermute x12 -> x10, waiting for transfers between devices: 7.54 us -> 6.57 us  [swap(): lax.ppermute(piece, 'seq', [(d, d ^ i) for d in range(lax.axis_size('seq'...]
    unnamed x8 -> x0, local copies, waits for them, and re-layouts: 0.66 us -> none
    ppermute x1, waiting for transfers between devices: 2.65 us -> 2.05 us  [local(): entry = lax.ppermute(j.total, 'seq', across if two else ahead)]
    ppermute x12 -> x10, starting transfers between devices: 15.3 us -> 15 us  [swap(): lax.ppermute(piece, 'seq', [(d, d ^ i) for d in range(lax.axis_size('seq'...]
    ppermute x3 -> x4, starting transfers between devices: 4.38 us -> 4.64 us  [the longest x1 2.72 us: local(): entry = lax.ppermute(own.total, 'seq', across if two else behind)]
  transfers between devices with their start and end apart: 16 -> 15, of which waited for: 9 -> 5; matrix products, arithmetic and copies ran while one was open for 0% -> 0% of each run, Pallas kernels for 17% -> 20%
where the time goes in v4:
time: 48 us; the launch traced here: 47.9 us
  starting transfers between devices  22.6 us (47%)
  Pallas kernels  15.3 us (32%)
  waiting for transfers between devices  8.63 us (18%)
  between operations  0.71 us (1%)
  other arithmetic  0.52 us (1%)
    pallas_call x10, Pallas kernels, call(): pl.pallas_call(kernel, out_shape=flat_outs, in_specs=specs + [pl.BlockSpe...  15.3 us
    ppermute x10, starting transfers between devices, swap(): lax.ppermute(piece, 'seq', [(d, d ^ i) for d in range(lax.axis_size('seq'...  15 us
    ppermute x10, waiting for transfers between devices, swap(): lax.ppermute(piece, 'seq', [(d, d ^ i) for d in range(lax.axis_size('seq'...  6.57 us
    ppermute x1, starting transfers between devices, local(): entry = lax.ppermute(j.total, 'seq', across if two else ahead)  3.06 us
    ppermute x1, starting transfers between devices, local(): entry = lax.ppermute(own.total, 'seq', across if two else behind)  2.72 us
    ppermute x1, waiting for transfers between devices, local(): entry = lax.ppermute(j.total, 'seq', across if two else ahead)  2.05 us
    ppermute x3, starting transfers between devices, local(): lax.ppermute(sums, 'head', [(d, d ^ flip) for d in range(size)])  1.92 us
  transfers between devices with their start and end apart: 15, of which 5 were waited for; matrix products, arithmetic and copies ran while one was open for 0% of the time, Pallas kernels for 20%

profile of v4, /device:TPU:0, one launch (start us, length us, event | category | flops | bytes accessed | tf_op | source)
XLA Modules:
  0.0 47.9 jit_solution(4941888974730024244)
XLA Ops:
  0.6 4.2 %shard_map.109 = (f32[2,256,128]{2,1,0:T(8,128)S(1)}, f32[1,128]{1,0:T(1,128)S(1)}, f32[512,128]{1,0:T(8,128)S(1)}, f32[2,256,256]{2,1,0:T(8,128)S(1)}, f32[1024...) custom-call(bf16[1024,128]{1,0:T(8,128)(2,1)} %bitcast.17, ...), custom_call_target="tpu_custom_call" | custom-call | flops 1000 | tf_op jit(solution)/shard_map/pallas_call | solution.py:485
  4.8 3.0 %collective-permute-start = (f32[128,640]{1,0:T(8,128)S(1)}, f32[128,640]{1,0:T(8,128)S(1)}, u32[]{:S(2)}, u32[]{:S(2)}) collective-permute-start(f32[128,640]{1,0:T(8,128)S(1)} %get-tuple-element.60.refs_5_), channel_id=1, source_target_pairs={{0,4},{4,0},{8,12},{12,8},{16,20},{20,16},{24,28},{28,24},{1,5},{5... | collective-permute-start | bytes 983048 | tf_op jit(solution)/shard_map/ppermute | solution.py:497
  7.8 1.6 %collective-permute-start.1 = (f32[128,640]{1,0:T(8,128)S(1)}, f32[128,640]{1,0:T(8,128)S(1)}, u32[]{:S(2)}, u32[]{:S(2)}) collective-permute-start(f32[128,640]{1,0:T(8,128)S(1)} %get-tuple-element.61.refs_6_), channel_id=1, source_target_pairs={{0,8},{4,12},{8,0},{12,4},{16,24},{20,28},{24,16},{28,20},{1,9},{5... | collective-permute-start | bytes 983048 | tf_op jit(solution)/shard_map/ppermute | solution.py:497
  9.4 2.4 %shard_map.110 = (f32[2,256,128]{2,1,0:T(8,128)S(1)}, f32[2,256,256]{2,1,0:T(8,128)S(1)}, f32[128,256]{1,0:T(8,128)S(1)}, f32[128,256]{1,0:T(8,128)S(1)}, f32[2,...) custom-call(f32[1024,128]{1,0:T(8,128)S(1)} %get-tuple-element.55.refs_0_, f32[1024,128]{1,0:T(8,128)S(1)} %get-tuple-element.56.refs_1_, ...), custom_call_target="tpu_custom_call" | custom-call | flops 1000 | tf_op jit(solution)/shard_map/pallas_call | solution.py:485
  11.8 0.1 collective-permute-start.2
  11.9 3.6 %collective-permute-done.refs_11_.refs_1_.refs_2_ = f32[128,640]{1,0:T(8,128)S(1)} collective-permute-done((f32[128,640]{1,0:T(8,128)S(1)}, f32[128,640]{1,0:T(8,128)S(1)}, u32[]{:S(2)}, u32[]{:S(2)}) %collective-permute-start) | collective-permute-done | bytes 327712 | tf_op jit(solution)/shard_map/ppermute | solution.py:497
  15.5 1.0 %shard_map.111 = (f32[4,256,128]{2,1,0:T(8,128)S(1)}, f32[2,128,128]{2,1,0:T(8,128)S(1)}, f32[128,384]{1,0:T(8,128)S(1)}, f32[128,384]{1,0:T(8,128)S(1)}, f32[2,128,256]{2,1,0:T(8,128)S(1)}) custom-call(f32[512,128]{1,0:T(8,128)S(1)} %get-tuple-element.63.refs_0_.refs_9_, f32[512,128]{1,0:T(8,128)S(1)} %get-tuple-element.64.refs_1_, ...), custom_call_target="tpu_custom_call" | custom-call | flops 1000000000 | tf_op jit(solution)/shard_map/pallas_call | solution.py:485
  16.5 3.1 %collective-permute-start.4 = (f32[128,384]{1,0:T(8,128)S(1)}, f32[128,384]{1,0:T(8,128)S(1)}, u32[]{:S(2)}, u32[]{:S(2)}) collective-permute-start(f32[128,384]{1,0:T(8,128)S(1)} %get-tuple-element.76.refs_7_), channel_id=1, source_target_pairs={{0,12},{4,8},{8,4},{12,0},{16,28},{20,24},{24,20},{28,16},{1,13},{... | collective-permute-start | bytes 589832 | tf_op jit(solution)/shard_map/ppermute | solution.py:497
  19.6 0.1 collective-permute-done.2.refs_3_
  19.8 0.0 collective-permute-done.1.refs_2_.refs_3_
  19.8 0.6 %shard_map.112 = (f32[4,128,256]{2,1,0:T(8,128)S(1)}, f32[4,128,128]{2,1,0:T(8,128)S(1)}, f32[128,128]{1,0:T(8,128)S(1)}) custom-call(f32[128,256]{1,0:T(8,128)S(1)} %get-tuple-element.59.refs_0_, f32[128,640]{1,0:T(8,128)S(1)} %collective-permute-done.refs_11_.refs_1_.refs_2_, f32[128,640]{1,0:T(8,128)S(1)} %collective-permute-done.1.refs_2_.refs_3_, ...), custom_call_target="tpu_custom_call" | custom-call | flops 1000 | tf_op jit(solution)/shard_map/pallas_call | solution.py:485
  20.3 3.1 %collective-permute-start.3 = (f32[128,128]{1,0:T(8,128)S(1)}, f32[128,128]{1,0:T(8,128)S(1)}, u32[]{:S(2)}, u32[]{:S(2)}) collective-permute-start(f32[128,128]{1,0:T(8,128)S(1)} %get-tuple-element.74), channel_id=1, source_target_pairs={{0,16},{4,20},{8,24},{12,28},{16,0},{20,4},{24,8},{28,12},{1,17},{... | collective-permute-start | bytes 196616 | tf_op jit(solution)/shard_map/ppermute | solution.py:592
  23.4 0.5 %shard_map.113 = (f32[4,128,128]{2,1,0:T(8,128)S(1)}, f32[5,128,128]{2,1,0:T(8,128)S(1)}) custom-call(f32[4,128,256]{2,1,0:T(8,128)S(1)} %get-tuple-element.78.refs_0_.refs_6_), custom_call_target="tpu_custom_call" | custom-call | flops 1000 | tf_op jit(solution)/shard_map/pallas_call | solution.py:485
  23.9 2.0 %collective-permute-done.3.refs_0_ = f32[128,128]{1,0:T(8,128)S(1)} collective-permute-done((f32[128,128]{1,0:T(8,128)S(1)}, f32[128,128]{1,0:T(8,128)S(1)}, u32[]{:S(2)}, u32[]{:S(2)}) %collective-permute-start.3) | collective-permute-done | bytes 65568 | tf_op jit(solution)/shard_map/ppermute | solution.py:592
  25.9 0.0 collective-permute-done.4.refs_4_
  26.0 1.4 %shard_map.114 = (f32[4,128,128]{2,1,0:T(8,128)}, f32[4,128,128]{2,1,0:T(8,128)S(1)}, f32[136,128]{1,0:T(8,128)S(1)}, f32[136,128]{1,0:T(8,128)S(1)}, f32[136,12...) custom-call(f32[128,128]{1,0:T(8,128)S(1)} %collective-permute-done.3.refs_0_, ...), custom_call_target="tpu_custom_call" | custom-call | flops 1000 | tf_op jit(solution)/shard_map/pallas_call | solution.py:485
  27.4 2.7 %collective-permute-start.8 = (f32[136,128]{1,0:T(8,128)S(1)}, f32[136,128]{1,0:T(8,128)S(1)}, u32[]{:S(2)}, u32[]{:S(2)}) collective-permute-start(f32[136,128]{1,0:T(8,128)S(1)} %get-tuple-element.89), channel_id=1, source_target_pairs={{0,16},{4,20},{8,24},{12,28},{16,0},{20,4},{24,8},{28,12},{1,17},{... | collective-permute-start | bytes 208904 | tf_op jit(solution)/shard_map/ppermute | solution.py:619
  30.1 1.5 %collective-permute-start.5 = (f32[136,128]{1,0:T(8,128)S(1)}, f32[136,128]{1,0:T(8,128)S(1)}, u32[]{:S(2)}, u32[]{:S(2)}) collective-permute-start(f32[136,128]{1,0:T(8,128)S(1)} %get-tuple-element.82), channel_id=1, source_target_pairs={{0,4},{4,0},{8,12},{12,8},{16,20},{20,16},{24,28},{28,24},{1,5},{5... | collective-permute-start | bytes 208904 | tf_op jit(solution)/shard_map/ppermute | solution.py:497
  31.6 2.1 %collective-permute-start.6 = (f32[136,128]{1,0:T(8,128)S(1)}, f32[136,128]{1,0:T(8,128)S(1)}, u32[]{:S(2)}, u32[]{:S(2)}) collective-permute-start(f32[136,128]{1,0:T(8,128)S(1)} %get-tuple-element.83), channel_id=1, source_target_pairs={{0,8},{4,12},{8,0},{12,4},{16,24},{20,28},{24,16},{28,20},{1,9},{5... | collective-permute-start | bytes 208904 | tf_op jit(solution)/shard_map/ppermute | solution.py:497
  33.7 0.0 collective-permute-start.7
  33.7 0.0 collective-permute-done.8.refs_0_
  33.7 0.3 shard_map.115
  34.0 1.5 %collective-permute-start.9 = (f32[136,128]{1,0:T(8,128)S(1)}, f32[136,128]{1,0:T(8,128)S(1)}, u32[]{:S(2)}, u32[]{:S(2)}) collective-permute-start(f32[136,128]{1,0:T(8,128)S(1)} %get-tuple-element.98), channel_id=1, source_target_pairs={{0,4},{4,0},{8,12},{12,8},{16,20},{20,16},{24,28},{28,24},{1,5},{5... | collective-permute-start | bytes 208904 | tf_op jit(solution)/shard_map/ppermute | solution.py:497
  35.5 2.0 %collective-permute-start.10 = (f32[136,128]{1,0:T(8,128)S(1)}, f32[136,128]{1,0:T(8,128)S(1)}, u32[]{:S(2)}, u32[]{:S(2)}) collective-permute-start(f32[136,128]{1,0:T(8,128)S(1)} %get-tuple-element.99), channel_id=1, source_target_pairs={{0,8},{4,12},{8,0},{12,4},{16,24},{20,28},{24,16},{28,20},{1,9},{5... | collective-permute-start | bytes 208904 | tf_op jit(solution)/shard_map/ppermute | solution.py:497
  37.6 0.0 collective-permute-done.5.refs_1_.refs_13_
  37.6 0.0 collective-permute-start.11
  37.6 0.0 collective-permute-done.6.refs_2_.refs_14_
  37.6 1.5 %collective-permute-done.7.refs_3_.refs_15_ = f32[136,128]{1,0:T(8,128)S(1)} collective-permute-done((f32[136,128]{1,0:T(8,128)S(1)}, f32[136,128]{1,0:T(8,128)S(1)}, u32[]{:S(2)}, u32[]{:S(2)}) %collective-permute-start.7) | collective-permute-done | bytes 69664 | tf_op jit(solution)/shard_map/ppermute | solution.py:497
  39.0 2.4 %shard_map.116 = (f32[4,256,128]{2,1,0:T(8,128)S(1)}, bf16[512,128]{1,0:T(8,128)(2,1)}, f32[4,256,128]{2,1,0:T(8,128)S(1)}, bf16[512,128]{1,0:T(8,128)(2,1)}, f32[4,256,128]{2,1,0:T(8,128)S(1)}) custom-call(f32[136,128]{1,0:T(8,128)S(1)} %get-tuple-element.81.refs_0_.refs_12_, f32[136,128]{1,0:T(8,128)S(1)} %collective-permute-done.5.refs_1_.refs_13_, ...), custom_call_target="tpu_custom_call" | custom-call | flops 1000 | tf_op jit(solution)/shard_map/pallas_call | solution.py:485
  41.4 0.0 collective-permute-done.9.refs_5_.refs_9_
  41.4 0.0 collective-permute-done.10.refs_6_.refs_10_
  41.4 1.4 %collective-permute-done.11.refs_7_.refs_11_ = f32[136,128]{1,0:T(8,128)S(1)} collective-permute-done((f32[136,128]{1,0:T(8,128)S(1)}, f32[136,128]{1,0:T(8,128)S(1)}, u32[]{:S(2)}, u32[]{:S(2)}) %collective-permute-start.11) | collective-permute-done | bytes 69664 | tf_op jit(solution)/shard_map/ppermute | solution.py:497
  42.8 0.1 collective-permute-start.14
  42.9 1.6 %collective-permute-start.13 = (f32[1,128]{1,0:T(1,128)S(1)}, f32[1,128]{1,0:T(1,128)S(1)}, u32[]{:S(2)}, u32[]{:S(2)}) collective-permute-start(f32[1,128]{1,0:T(1,128)S(1)} %shard_map.117.refs_16_), channel_id=1, source_target_pairs={{0,2},{1,3},{2,0},{3,1},{4,6},{5,7},{6,4},{7,5},{8,10},{9,11},{10,... | collective-permute-start | bytes 1544 | tf_op jit(solution)/shard_map/ppermute | solution.py:683
  44.4 0.3 collective-permute-start.12
  44.7 2.6 %shard_map.118 = (f32[8,128]{1,0:T(8,128)}, bf16[1024,128]{1,0:T(8,128)(2,1)}, bf16[1024,128]{1,0:T(8,128)(2,1)}) custom-call(f32[1024,128]{1,0:T(8,128)S(1)} %get-tuple-element.55.refs_0_, f32[256,4]{1,0:T(8,128)S(1)} %get-tuple-element.57.refs_2_.refs_10_.refs_1_, f32[2,256,128]{2,1,0:T(8,128)S(1)} %get-tuple-element.65.refs_3_.refs_17_.refs_2_, ...), custom_call_target="tpu_custom_call" | custom-call | flops 1000 | tf_op jit(solution)/shard_map/pallas_call | solution.py:485
  47.3 0.0 collective-permute-done.14
  47.3 0.0 collective-permute-done.13
  47.3 0.0 collective-permute-done.12
  47.3 0.5 %add_bitcast_fusion = f32[128]{0:T(128)} fusion(f32[1,128]{1,0:T(1,128)S(1)} %shard_map.117.refs_16_, f32[1,128]{1,0:T(1,128)S(1)} %collective-permute-done.14, f32[1,128]{1,0:T(1,128)S(1)} %collective-permute-done.12, f32[1,128]{1,0:T(1,128)S(1)} %collective-permute-done.13), kind=kLoop, calls=%fused_computation | loop fusion | flops 384 | bytes 2560 | tf_op jit(solution)/shard_map/reshape | solution.py:694
  (1 shorter events, 0.0 us)
Async XLA Ops:
  4.8 10.7 %collective-permute-start = (f32[128,640]{1,0:T(8,128)S(1)}, f32[128,640]{1,0:T(8,128)S(1)}, u32[]{:S(2)}, u32[]{:S(2)}) collective-permute-start(f32[128,640]{1,0:T(8,128)S(1)} %get-tuple-element.60.refs_5_), channel_id=1, source_target_pairs={{0,4},{4,0},{8,12},{12,8},{16,20},{20,16},{24,28},{28,24},{1,5},{5... | collective-permute-start | bytes 983048 | tf_op jit(solution)/shard_map/ppermute | solution.py:497
  7.8 11.9 %collective-permute-start.1 = (f32[128,640]{1,0:T(8,128)S(1)}, f32[128,640]{1,0:T(8,128)S(1)}, u32[]{:S(2)}, u32[]{:S(2)}) collective-permute-start(f32[128,640]{1,0:T(8,128)S(1)} %get-tuple-element.61.refs_6_), channel_id=1, source_target_pairs={{0,8},{4,12},{8,0},{12,4},{16,24},{20,28},{24,16},{28,20},{1,9},{5... | collective-permute-start | bytes 983048 | tf_op jit(solution)/shard_map/ppermute | solution.py:497
  11.8 7.9 %collective-permute-start.2 = (f32[128,256]{1,0:T(8,128)S(1)}, f32[128,256]{1,0:T(8,128)S(1)}, u32[]{:S(2)}, u32[]{:S(2)}) collective-permute-start(f32[128,256]{1,0:T(8,128)S(1)} %get-tuple-element.62), channel_id=1, source_target_pairs={{0,12},{4,8},{8,4},{12,0},{16,28},{20,24},{24,20},{28,16},{1,13},{... | collective-permute-start | bytes 393224 | tf_op jit(solution)/shard_map/ppermute | solution.py:497
  16.5 9.4 %collective-permute-start.4 = (f32[128,384]{1,0:T(8,128)S(1)}, f32[128,384]{1,0:T(8,128)S(1)}, u32[]{:S(2)}, u32[]{:S(2)}) collective-permute-start(f32[128,384]{1,0:T(8,128)S(1)} %get-tuple-element.76.refs_7_), channel_id=1, source_target_pairs={{0,12},{4,8},{8,4},{12,0},{16,28},{20,24},{24,20},{28,16},{1,13},{... | collective-permute-start | bytes 589832 | tf_op jit(solution)/shard_map/ppermute | solution.py:497
  20.3 5.6 %collective-permute-start.3 = (f32[128,128]{1,0:T(8,128)S(1)}, f32[128,128]{1,0:T(8,128)S(1)}, u32[]{:S(2)}, u32[]{:S(2)}) collective-permute-start(f32[128,128]{1,0:T(8,128)S(1)} %get-tuple-element.74), channel_id=1, source_target_pairs={{0,16},{4,20},{8,24},{12,28},{16,0},{20,4},{24,8},{28,12},{1,17},{... | collective-permute-start | bytes 196616 | tf_op jit(solution)/shard_map/ppermute | solution.py:592
  27.4 6.3 %collective-permute-start.8 = (f32[136,128]{1,0:T(8,128)S(1)}, f32[136,128]{1,0:T(8,128)S(1)}, u32[]{:S(2)}, u32[]{:S(2)}) collective-permute-start(f32[136,128]{1,0:T(8,128)S(1)} %get-tuple-element.89), channel_id=1, source_target_pairs={{0,16},{4,20},{8,24},{12,28},{16,0},{20,4},{24,8},{28,12},{1,17},{... | collective-permute-start | bytes 208904 | tf_op jit(solution)/shard_map/ppermute | solution.py:619
  30.1 7.5 %collective-permute-start.5 = (f32[136,128]{1,0:T(8,128)S(1)}, f32[136,128]{1,0:T(8,128)S(1)}, u32[]{:S(2)}, u32[]{:S(2)}) collective-permute-start(f32[136,128]{1,0:T(8,128)S(1)} %get-tuple-element.82), channel_id=1, source_target_pairs={{0,4},{4,0},{8,12},{12,8},{16,20},{20,16},{24,28},{28,24},{1,5},{5... | collective-permute-start | bytes 208904 | tf_op jit(solution)/shard_map/ppermute | solution.py:497
  31.6 6.0 %collective-permute-start.6 = (f32[136,128]{1,0:T(8,128)S(1)}, f32[136,128]{1,0:T(8,128)S(1)}, u32[]{:S(2)}, u32[]{:S(2)}) collective-permute-start(f32[136,128]{1,0:T(8,128)S(1)} %get-tuple-element.83), channel_id=1, source_target_pairs={{0,8},{4,12},{8,0},{12,4},{16,24},{20,28},{24,16},{28,20},{1,9},{5... | collective-permute-start | bytes 208904 | tf_op jit(solution)/shard_map/ppermute | solution.py:497
  33.7 5.3 %collective-permute-start.7 = (f32[136,128]{1,0:T(8,128)S(1)}, f32[136,128]{1,0:T(8,128)S(1)}, u32[]{:S(2)}, u32[]{:S(2)}) collective-permute-start(f32[136,128]{1,0:T(8,128)S(1)} %get-tuple-element.84), channel_id=1, source_target_pairs={{0,12},{4,8},{8,4},{12,0},{16,28},{20,24},{24,20},{28,16},{1,13},{... | collective-permute-start | bytes 208904 | tf_op jit(solution)/shard_map/ppermute | solution.py:497
  34.0 7.4 %collective-permute-start.9 = (f32[136,128]{1,0:T(8,128)S(1)}, f32[136,128]{1,0:T(8,128)S(1)}, u32[]{:S(2)}, u32[]{:S(2)}) collective-permute-start(f32[136,128]{1,0:T(8,128)S(1)} %get-tuple-element.98), channel_id=1, source_target_pairs={{0,4},{4,0},{8,12},{12,8},{16,20},{20,16},{24,28},{28,24},{1,5},{5... | collective-permute-start | bytes 208904 | tf_op jit(solution)/shard_map/ppermute | solution.py:497
  35.5 5.9 %collective-permute-start.10 = (f32[136,128]{1,0:T(8,128)S(1)}, f32[136,128]{1,0:T(8,128)S(1)}, u32[]{:S(2)}, u32[]{:S(2)}) collective-permute-start(f32[136,128]{1,0:T(8,128)S(1)} %get-tuple-element.99), channel_id=1, source_target_pairs={{0,8},{4,12},{8,0},{12,4},{16,24},{20,28},{24,16},{28,20},{1,9},{5... | collective-permute-start | bytes 208904 | tf_op jit(solution)/shard_map/ppermute | solution.py:497
  37.6 5.2 %collective-permute-start.11 = (f32[136,128]{1,0:T(8,128)S(1)}, f32[136,128]{1,0:T(8,128)S(1)}, u32[]{:S(2)}, u32[]{:S(2)}) collective-permute-start(f32[136,128]{1,0:T(8,128)S(1)} %get-tuple-element.100), channel_id=1, source_target_pairs={{0,12},{4,8},{8,4},{12,0},{16,28},{20,24},{24,20},{28,16},{1,13},{... | collective-permute-start | bytes 208904 | tf_op jit(solution)/shard_map/ppermute | solution.py:497
  42.8 4.5 %collective-permute-start.14 = (f32[1,128]{1,0:T(1,128)S(1)}, f32[1,128]{1,0:T(1,128)S(1)}, u32[]{:S(2)}, u32[]{:S(2)}) collective-permute-start(f32[1,128]{1,0:T(1,128)S(1)} %shard_map.117.refs_16_), channel_id=1, source_target_pairs={{0,3},{1,2},{2,1},{3,0},{4,7},{5,6},{6,5},{7,4},{8,11},{9,10},{10,... | collective-permute-start | bytes 1544 | tf_op jit(solution)/shard_map/ppermute | solution.py:683
  42.9 4.5 %collective-permute-start.13 = (f32[1,128]{1,0:T(1,128)S(1)}, f32[1,128]{1,0:T(1,128)S(1)}, u32[]{:S(2)}, u32[]{:S(2)}) collective-permute-start(f32[1,128]{1,0:T(1,128)S(1)} %shard_map.117.refs_16_), channel_id=1, source_target_pairs={{0,2},{1,3},{2,0},{3,1},{4,6},{5,7},{6,4},{7,5},{8,10},{9,11},{10,... | collective-permute-start | bytes 1544 | tf_op jit(solution)/shard_map/ppermute | solution.py:683
  44.4 2.9 %collective-permute-start.12 = (f32[1,128]{1,0:T(1,128)S(1)}, f32[1,128]{1,0:T(1,128)S(1)}, u32[]{:S(2)}, u32[]{:S(2)}) collective-permute-start(f32[1,128]{1,0:T(1,128)S(1)} %shard_map.117.refs_16_), channel_id=1, source_target_pairs={{0,1},{1,0},{2,3},{3,2},{4,5},{5,4},{6,7},{7,6},{8,9},{9,8},{10,11... | collective-permute-start | bytes 1544 | tf_op jit(solution)/shard_map/ppermute | solution.py:683

commit v5 on v4

--- a/solution.py
+++ b/solution.py
@@ -296,6 +296,7 @@
     for j in range(1, group):
         before.append(mm(steps[j], before[-1]))
         after.append(mm(after[-1], steps[-1 - j]))
+    o.middle[...] = mm(steps[2], steps[1])
     for j in range(group + 1):
         o.before[j] = before[j]
     for j in range(group):
@@ -346,13 +347,17 @@
     states = [starts[j] + mm(before[j], entry) if j else starts[j] + entry for j in places_]
     _, grads, gain_part = normed_and_grads(queries, parts, states, given, gain)
     adjoints = [mm(queries[j], grads[j], ta=True) for j in places_]
-    chain = [jnp.zeros((HALF, HALF), F32), adjoints[-1]]
-    for j in reversed(range(group - 1)):
-        chain.append(mm(maps[j], chain[-1], ta=True) + adjoints[j])
+    chain = [
+        adjoints[1] + mm(maps[1], adjoints[2], ta=True) + mm(n.middle[...], adjoints[3], ta=True),
+        adjoints[2] + mm(maps[2], adjoints[3], ta=True),
+        adjoints[3],
+        jnp.zeros((HALF, HALF), F32),
+    ]
+    total = adjoints[0] + sum(mm(before[j], adjoints[j], ta=True) for j in range(1, group))
     for j in places_:
-        o.starts[j] = chain[group - 1 - j]
+        o.starts[j] = chain[j]
         o.entries[j] = states[j]
-    o.total[:HALF, :] = chain[-1]
+    o.total[:HALF, :] = total
     for i in places_:
         o.states[i][:HALF, :] = o.entries[me ^ i]
         o.states[i][HALF:, :] = jnp.broadcast_to(gain_part, (8, HALF))
@@ -417,21 +422,31 @@
     invs = [inverse_norm(raw) for raw in raws]
     pseudo = [rate[i] * errs[i] for i in heads]
     d_values = [rate[i] * z[i] for i in heads]
-    below = iota((steps, steps), 1) < iota((steps, steps), 0)
-    above = iota((steps, steps), 1) > iota((steps, steps), 0)
-    d_grams = [
-        jnp.where(
-            below,
-            mm(d_values[i], pseudo[i], tb=True),
-            jnp.where(above, mm(pseudo[i], d_values[i], tb=True), 0.0),
-        )
-        for i in heads
-    ]
+    half = steps // 2
+    below = iota((half, half), 1) < iota((half, half), 0)
+    d_grams = []
+    for i in heads:
+        later = mm(d_values[i][half:], pseudo[i], tb=True)
+        corners = [
+            jnp.where(below, corner, 0.0)
+            for corner in (mm(d_values[i][:half], pseudo[i][:half], tb=True), later[:, half:])
+        ]
+        corners = [corner + corner.T for corner in corners]
+        d_grams.append(
+            jnp.concatenate(
+                [
+                    jnp.concatenate([corners[0], later[:, :half].T], axis=1),
+                    jnp.concatenate([later[:, :half], corners[1]], axis=1),
+                ],
+                axis=0,
+            )
+        )
     d_units = [
         dk0[i]
-        + mm(pseudo[i], adjoints[i], tb=True)
-        - mm(d_values[i], states[i], tb=True)
-        - mm(d_grams[i], units[i])
+        + mm(
+            jnp.concatenate([pseudo[i], d_values[i], d_grams[i]], axis=1),
+            jnp.concatenate([adjoints[i].T, -states[i].T, -units[i]], axis=0),
+        )
         for i in heads
     ]
     done = [unit_grad(invs[i], units[i], d_units[i]) for i in heads]
@@ -593,7 +608,11 @@
     p = call(
         bind(products_kernel, group),
         dict(maps=j.maps),
-        dict(before=f32(group + 1, dim, dim), after=f32(group, dim, dim)),
+        dict(
+            before=f32(group + 1, dim, dim),
+            after=f32(group, dim, dim),
+            middle=f32(dim, dim),
+        ),
     )
     for _ in range(groups - 2):
         passed = jnp.dot(p.before[group], entry, precision=lax.Precision.HIGHEST) + j.total
@@ -606,6 +625,7 @@
             gain=a.gain,
             maps=j.maps,
             before=p.before,
+            middle=p.middle,
             starts=j.starts,
         ),
         dict(

time: 48 us -> 47.6 us (level)
  no operation moved by 1% of the time
where the time goes in v5:
time: 47.6 us; the launch traced here: 47.4 us
  starting transfers between devices  22.6 us (47%)
  Pallas kernels  15 us (32%)
  waiting for transfers between devices  8.6 us (18%)
  between operations  0.71 us (1%)
  other arithmetic  0.52 us (1%)
    pallas_call x10, Pallas kernels, call(): pl.pallas_call(kernel, out_shape=flat_outs, in_specs=specs + [pl.BlockSpe...  15 us
    ppermute x10, starting transfers between devices, swap(): lax.ppermute(piece, 'seq', [(d, d ^ i) for d in range(lax.axis_size('seq'...  15 us
    ppermute x10, waiting for transfers between devices, swap(): lax.ppermute(piece, 'seq', [(d, d ^ i) for d in range(lax.axis_size('seq'...  6.56 us
    ppermute x1, starting transfers between devices, local(): entry = lax.ppermute(j.total, 'seq', across if two else ahead)  3.05 us
    ppermute x1, starting transfers between devices, local(): entry = lax.ppermute(own.total, 'seq', across if two else behind)  2.65 us
    ppermute x1, waiting for transfers between devices, local(): entry = lax.ppermute(j.total, 'seq', across if two else ahead)  2.03 us
    ppermute x3, starting transfers between devices, local(): lax.ppermute(sums, 'head', [(d, d ^ flip) for d in range(size)])  1.92 us
  transfers between devices with their start and end apart: 15, of which 5 were waited for; matrix products, arithmetic and copies ran while one was open for 0% of the time, Pallas kernels for 20%

profile of v5, /device:TPU:0, one launch (start us, length us, event | category | flops | bytes accessed | tf_op | source)
XLA Modules:
  0.0 47.4 jit_solution(10986448811394749972)
XLA Ops:
  0.6 4.2 %shard_map.109 = (f32[2,256,128]{2,1,0:T(8,128)S(1)}, f32[1,128]{1,0:T(1,128)S(1)}, f32[512,128]{1,0:T(8,128)S(1)}, f32[2,256,256]{2,1,0:T(8,128)S(1)}, f32[1024...) custom-call(bf16[1024,128]{1,0:T(8,128)(2,1)} %bitcast.17, ...), custom_call_target="tpu_custom_call" | custom-call | flops 1000 | tf_op jit(solution)/shard_map/pallas_call | solution.py:500
  4.8 3.0 %collective-permute-start = (f32[128,640]{1,0:T(8,128)S(1)}, f32[128,640]{1,0:T(8,128)S(1)}, u32[]{:S(2)}, u32[]{:S(2)}) collective-permute-start(f32[128,640]{1,0:T(8,128)S(1)} %get-tuple-element.61.refs_5_), channel_id=1, source_target_pairs={{0,4},{4,0},{8,12},{12,8},{16,20},{20,16},{24,28},{28,24},{1,5},{5... | collective-permute-start | bytes 983048 | tf_op jit(solution)/shard_map/ppermute | solution.py:512
  7.8 1.6 %collective-permute-start.1 = (f32[128,640]{1,0:T(8,128)S(1)}, f32[128,640]{1,0:T(8,128)S(1)}, u32[]{:S(2)}, u32[]{:S(2)}) collective-permute-start(f32[128,640]{1,0:T(8,128)S(1)} %get-tuple-element.62.refs_6_), channel_id=1, source_target_pairs={{0,8},{4,12},{8,0},{12,4},{16,24},{20,28},{24,16},{28,20},{1,9},{5... | collective-permute-start | bytes 983048 | tf_op jit(solution)/shard_map/ppermute | solution.py:512
  9.4 2.4 %shard_map.110 = (f32[2,256,128]{2,1,0:T(8,128)S(1)}, f32[2,256,256]{2,1,0:T(8,128)S(1)}, f32[128,256]{1,0:T(8,128)S(1)}, f32[128,256]{1,0:T(8,128)S(1)}, f32[2,...) custom-call(f32[1024,128]{1,0:T(8,128)S(1)} %get-tuple-element.56.refs_0_, f32[1024,128]{1,0:T(8,128)S(1)} %get-tuple-element.57.refs_1_, ...), custom_call_target="tpu_custom_call" | custom-call | flops 1000 | tf_op jit(solution)/shard_map/pallas_call | solution.py:500
  11.8 0.1 collective-permute-start.2
  11.9 3.6 %collective-permute-done.refs_11_.refs_1_.refs_2_ = f32[128,640]{1,0:T(8,128)S(1)} collective-permute-done((f32[128,640]{1,0:T(8,128)S(1)}, f32[128,640]{1,0:T(8,128)S(1)}, u32[]{:S(2)}, u32[]{:S(2)}) %collective-permute-start) | collective-permute-done | bytes 327712 | tf_op jit(solution)/shard_map/ppermute | solution.py:512
  15.5 1.0 %shard_map.111 = (f32[4,256,128]{2,1,0:T(8,128)S(1)}, f32[2,128,128]{2,1,0:T(8,128)S(1)}, f32[128,384]{1,0:T(8,128)S(1)}, f32[128,384]{1,0:T(8,128)S(1)}, f32[2,128,256]{2,1,0:T(8,128)S(1)}) custom-call(f32[512,128]{1,0:T(8,128)S(1)} %get-tuple-element.64.refs_0_.refs_9_, f32[512,128]{1,0:T(8,128)S(1)} %get-tuple-element.65.refs_1_, ...), custom_call_target="tpu_custom_call" | custom-call | flops 1000000000 | tf_op jit(solution)/shard_map/pallas_call | solution.py:500
  16.5 3.1 %collective-permute-start.4 = (f32[128,384]{1,0:T(8,128)S(1)}, f32[128,384]{1,0:T(8,128)S(1)}, u32[]{:S(2)}, u32[]{:S(2)}) collective-permute-start(f32[128,384]{1,0:T(8,128)S(1)} %get-tuple-element.77.refs_7_), channel_id=1, source_target_pairs={{0,12},{4,8},{8,4},{12,0},{16,28},{20,24},{24,20},{28,16},{1,13},{... | collective-permute-start | bytes 589832 | tf_op jit(solution)/shard_map/ppermute | solution.py:512
  19.6 0.1 collective-permute-done.2.refs_3_
  19.8 0.0 collective-permute-done.1.refs_2_.refs_3_
  19.8 0.6 %shard_map.112 = (f32[4,128,256]{2,1,0:T(8,128)S(1)}, f32[4,128,128]{2,1,0:T(8,128)S(1)}, f32[128,128]{1,0:T(8,128)S(1)}) custom-call(f32[128,256]{1,0:T(8,128)S(1)} %get-tuple-element.60.refs_0_, f32[128,640]{1,0:T(8,128)S(1)} %collective-permute-done.refs_11_.refs_1_.refs_2_, f32[128,640]{1,0:T(8,128)S(1)} %collective-permute-done.1.refs_2_.refs_3_, ...), custom_call_target="tpu_custom_call" | custom-call | flops 1000 | tf_op jit(solution)/shard_map/pallas_call | solution.py:500
  20.3 3.1 %collective-permute-start.3 = (f32[128,128]{1,0:T(8,128)S(1)}, f32[128,128]{1,0:T(8,128)S(1)}, u32[]{:S(2)}, u32[]{:S(2)}) collective-permute-start(f32[128,128]{1,0:T(8,128)S(1)} %get-tuple-element.75), channel_id=1, source_target_pairs={{0,16},{4,20},{8,24},{12,28},{16,0},{20,4},{24,8},{28,12},{1,17},{... | collective-permute-start | bytes 196616 | tf_op jit(solution)/shard_map/ppermute | solution.py:607
  23.4 0.5 %shard_map.113 = (f32[4,128,128]{2,1,0:T(8,128)S(1)}, f32[5,128,128]{2,1,0:T(8,128)S(1)}, f32[128,128]{1,0:T(8,128)S(1)}) custom-call(f32[4,128,256]{2,1,0:T(8,128)S(1)} %get-tuple-element.79.refs_0_.refs_6_), custom_call_target="tpu_custom_call" | custom-call | flops 1000 | tf_op jit(solution)/shard_map/pallas_call | solution.py:500
  23.9 2.0 %collective-permute-done.3.refs_0_ = f32[128,128]{1,0:T(8,128)S(1)} collective-permute-done((f32[128,128]{1,0:T(8,128)S(1)}, f32[128,128]{1,0:T(8,128)S(1)}, u32[]{:S(2)}, u32[]{:S(2)}) %collective-permute-start.3) | collective-permute-done | bytes 65568 | tf_op jit(solution)/shard_map/ppermute | solution.py:607
  25.9 0.0 collective-permute-done.4.refs_4_
  26.0 1.3 %shard_map.114 = (f32[4,128,128]{2,1,0:T(8,128)}, f32[4,128,128]{2,1,0:T(8,128)S(1)}, f32[136,128]{1,0:T(8,128)S(1)}, f32[136,128]{1,0:T(8,128)S(1)}, f32[136,12...) custom-call(f32[128,128]{1,0:T(8,128)S(1)} %collective-permute-done.3.refs_0_, ...), custom_call_target="tpu_custom_call" | custom-call | flops 1000 | tf_op jit(solution)/shard_map/pallas_call | solution.py:500
  27.3 2.7 %collective-permute-start.8 = (f32[136,128]{1,0:T(8,128)S(1)}, f32[136,128]{1,0:T(8,128)S(1)}, u32[]{:S(2)}, u32[]{:S(2)}) collective-permute-start(f32[136,128]{1,0:T(8,128)S(1)} %get-tuple-element.91), channel_id=1, source_target_pairs={{0,16},{4,20},{8,24},{12,28},{16,0},{20,4},{24,8},{28,12},{1,17},{... | collective-permute-start | bytes 208904 | tf_op jit(solution)/shard_map/ppermute | solution.py:639
  29.9 1.5 %collective-permute-start.5 = (f32[136,128]{1,0:T(8,128)S(1)}, f32[136,128]{1,0:T(8,128)S(1)}, u32[]{:S(2)}, u32[]{:S(2)}) collective-permute-start(f32[136,128]{1,0:T(8,128)S(1)} %get-tuple-element.84), channel_id=1, source_target_pairs={{0,4},{4,0},{8,12},{12,8},{16,20},{20,16},{24,28},{28,24},{1,5},{5... | collective-permute-start | bytes 208904 | tf_op jit(solution)/shard_map/ppermute | solution.py:512
  31.4 2.1 %collective-permute-start.6 = (f32[136,128]{1,0:T(8,128)S(1)}, f32[136,128]{1,0:T(8,128)S(1)}, u32[]{:S(2)}, u32[]{:S(2)}) collective-permute-start(f32[136,128]{1,0:T(8,128)S(1)} %get-tuple-element.85), channel_id=1, source_target_pairs={{0,8},{4,12},{8,0},{12,4},{16,24},{20,28},{24,16},{28,20},{1,9},{5... | collective-permute-start | bytes 208904 | tf_op jit(solution)/shard_map/ppermute | solution.py:512
  33.5 0.0 collective-permute-start.7
  33.5 0.0 collective-permute-done.8.refs_0_
  33.5 0.3 shard_map.115
  33.8 1.5 %collective-permute-start.9 = (f32[136,128]{1,0:T(8,128)S(1)}, f32[136,128]{1,0:T(8,128)S(1)}, u32[]{:S(2)}, u32[]{:S(2)}) collective-permute-start(f32[136,128]{1,0:T(8,128)S(1)} %get-tuple-element.100), channel_id=1, source_target_pairs={{0,4},{4,0},{8,12},{12,8},{16,20},{20,16},{24,28},{28,24},{1,5},{5... | collective-permute-start | bytes 208904 | tf_op jit(solution)/shard_map/ppermute | solution.py:512
  35.4 2.0 %collective-permute-start.10 = (f32[136,128]{1,0:T(8,128)S(1)}, f32[136,128]{1,0:T(8,128)S(1)}, u32[]{:S(2)}, u32[]{:S(2)}) collective-permute-start(f32[136,128]{1,0:T(8,128)S(1)} %get-tuple-element.101), channel_id=1, source_target_pairs={{0,8},{4,12},{8,0},{12,4},{16,24},{20,28},{24,16},{28,20},{1,9},{5... | collective-permute-start | bytes 208904 | tf_op jit(solution)/shard_map/ppermute | solution.py:512
  37.4 0.0 collective-permute-done.5.refs_1_.refs_13_
  37.4 0.0 collective-permute-start.11
  37.4 0.0 collective-permute-done.6.refs_2_.refs_14_
  37.4 1.5 %collective-permute-done.7.refs_3_.refs_15_ = f32[136,128]{1,0:T(8,128)S(1)} collective-permute-done((f32[136,128]{1,0:T(8,128)S(1)}, f32[136,128]{1,0:T(8,128)S(1)}, u32[]{:S(2)}, u32[]{:S(2)}) %collective-permute-start.7) | collective-permute-done | bytes 69664 | tf_op jit(solution)/shard_map/ppermute | solution.py:512
  38.9 2.4 %shard_map.116 = (f32[4,256,128]{2,1,0:T(8,128)S(1)}, bf16[512,128]{1,0:T(8,128)(2,1)}, f32[4,256,128]{2,1,0:T(8,128)S(1)}, bf16[512,128]{1,0:T(8,128)(2,1)}, f32[4,256,128]{2,1,0:T(8,128)S(1)}) custom-call(f32[136,128]{1,0:T(8,128)S(1)} %get-tuple-element.83.refs_0_.refs_12_, f32[136,128]{1,0:T(8,128)S(1)} %collective-permute-done.5.refs_1_.refs_13_, ...), custom_call_target="tpu_custom_call" | custom-call | flops 1000 | tf_op jit(solution)/shard_map/pallas_call | solution.py:500
  41.2 0.0 collective-permute-done.9.refs_5_.refs_9_
  41.2 0.0 collective-permute-done.10.refs_6_.refs_10_
  41.3 1.3 %collective-permute-done.11.refs_7_.refs_11_ = f32[136,128]{1,0:T(8,128)S(1)} collective-permute-done((f32[136,128]{1,0:T(8,128)S(1)}, f32[136,128]{1,0:T(8,128)S(1)}, u32[]{:S(2)}, u32[]{:S(2)}) %collective-permute-start.11) | collective-permute-done | bytes 69664 | tf_op jit(solution)/shard_map/ppermute | solution.py:512
  42.6 0.1 collective-permute-start.14
  42.7 1.6 %collective-permute-start.13 = (f32[1,128]{1,0:T(1,128)S(1)}, f32[1,128]{1,0:T(1,128)S(1)}, u32[]{:S(2)}, u32[]{:S(2)}) collective-permute-start(f32[1,128]{1,0:T(1,128)S(1)} %shard_map.117.refs_16_), channel_id=1, source_target_pairs={{0,2},{1,3},{2,0},{3,1},{4,6},{5,7},{6,4},{7,5},{8,10},{9,11},{10,... | collective-permute-start | bytes 1544 | tf_op jit(solution)/shard_map/ppermute | solution.py:703
  44.2 0.3 collective-permute-start.12
  44.5 2.4 %shard_map.118 = (f32[8,128]{1,0:T(8,128)}, bf16[1024,128]{1,0:T(8,128)(2,1)}, bf16[1024,128]{1,0:T(8,128)(2,1)}) custom-call(f32[1024,128]{1,0:T(8,128)S(1)} %get-tuple-element.56.refs_0_, f32[256,4]{1,0:T(8,128)S(1)} %get-tuple-element.58.refs_2_.refs_10_.refs_1_, f32[2,256,128]{2,1,0:T(8,128)S(1)} %get-tuple-element.66.refs_3_.refs_17_.refs_2_, ...), custom_call_target="tpu_custom_call" | custom-call | flops 1000 | tf_op jit(solution)/shard_map/pallas_call | solution.py:500
  46.9 0.0 collective-permute-done.14
  46.9 0.0 collective-permute-done.13
  46.9 0.0 collective-permute-done.12
  46.9 0.5 %add_bitcast_fusion = f32[128]{0:T(128)} fusion(f32[1,128]{1,0:T(1,128)S(1)} %shard_map.117.refs_16_, f32[1,128]{1,0:T(1,128)S(1)} %collective-permute-done.14, f32[1,128]{1,0:T(1,128)S(1)} %collective-permute-done.12, f32[1,128]{1,0:T(1,128)S(1)} %collective-permute-done.13), kind=kLoop, calls=%fused_computation | loop fusion | flops 384 | bytes 2560 | tf_op jit(solution)/shard_map/reshape | solution.py:714
  (1 shorter events, 0.0 us)
Async XLA Ops:
  4.8 10.7 %collective-permute-start = (f32[128,640]{1,0:T(8,128)S(1)}, f32[128,640]{1,0:T(8,128)S(1)}, u32[]{:S(2)}, u32[]{:S(2)}) collective-permute-start(f32[128,640]{1,0:T(8,128)S(1)} %get-tuple-element.61.refs_5_), channel_id=1, source_target_pairs={{0,4},{4,0},{8,12},{12,8},{16,20},{20,16},{24,28},{28,24},{1,5},{5... | collective-permute-start | bytes 983048 | tf_op jit(solution)/shard_map/ppermute | solution.py:512
  7.8 11.9 %collective-permute-start.1 = (f32[128,640]{1,0:T(8,128)S(1)}, f32[128,640]{1,0:T(8,128)S(1)}, u32[]{:S(2)}, u32[]{:S(2)}) collective-permute-start(f32[128,640]{1,0:T(8,128)S(1)} %get-tuple-element.62.refs_6_), channel_id=1, source_target_pairs={{0,8},{4,12},{8,0},{12,4},{16,24},{20,28},{24,16},{28,20},{1,9},{5... | collective-permute-start | bytes 983048 | tf_op jit(solution)/shard_map/ppermute | solution.py:512
  11.8 7.9 %collective-permute-start.2 = (f32[128,256]{1,0:T(8,128)S(1)}, f32[128,256]{1,0:T(8,128)S(1)}, u32[]{:S(2)}, u32[]{:S(2)}) collective-permute-start(f32[128,256]{1,0:T(8,128)S(1)} %get-tuple-element.63), channel_id=1, source_target_pairs={{0,12},{4,8},{8,4},{12,0},{16,28},{20,24},{24,20},{28,16},{1,13},{... | collective-permute-start | bytes 393224 | tf_op jit(solution)/shard_map/ppermute | solution.py:512
  16.5 9.4 %collective-permute-start.4 = (f32[128,384]{1,0:T(8,128)S(1)}, f32[128,384]{1,0:T(8,128)S(1)}, u32[]{:S(2)}, u32[]{:S(2)}) collective-permute-start(f32[128,384]{1,0:T(8,128)S(1)} %get-tuple-element.77.refs_7_), channel_id=1, source_target_pairs={{0,12},{4,8},{8,4},{12,0},{16,28},{20,24},{24,20},{28,16},{1,13},{... | collective-permute-start | bytes 589832 | tf_op jit(solution)/shard_map/ppermute | solution.py:512
  20.3 5.6 %collective-permute-start.3 = (f32[128,128]{1,0:T(8,128)S(1)}, f32[128,128]{1,0:T(8,128)S(1)}, u32[]{:S(2)}, u32[]{:S(2)}) collective-permute-start(f32[128,128]{1,0:T(8,128)S(1)} %get-tuple-element.75), channel_id=1, source_target_pairs={{0,16},{4,20},{8,24},{12,28},{16,0},{20,4},{24,8},{28,12},{1,17},{... | collective-permute-start | bytes 196616 | tf_op jit(solution)/shard_map/ppermute | solution.py:607
  27.3 6.3 %collective-permute-start.8 = (f32[136,128]{1,0:T(8,128)S(1)}, f32[136,128]{1,0:T(8,128)S(1)}, u32[]{:S(2)}, u32[]{:S(2)}) collective-permute-start(f32[136,128]{1,0:T(8,128)S(1)} %get-tuple-element.91), channel_id=1, source_target_pairs={{0,16},{4,20},{8,24},{12,28},{16,0},{20,4},{24,8},{28,12},{1,17},{... | collective-permute-start | bytes 208904 | tf_op jit(solution)/shard_map/ppermute | solution.py:639
  29.9 7.5 %collective-permute-start.5 = (f32[136,128]{1,0:T(8,128)S(1)}, f32[136,128]{1,0:T(8,128)S(1)}, u32[]{:S(2)}, u32[]{:S(2)}) collective-permute-start(f32[136,128]{1,0:T(8,128)S(1)} %get-tuple-element.84), channel_id=1, source_target_pairs={{0,4},{4,0},{8,12},{12,8},{16,20},{20,16},{24,28},{28,24},{1,5},{5... | collective-permute-start | bytes 208904 | tf_op jit(solution)/shard_map/ppermute | solution.py:512
  31.4 6.0 %collective-permute-start.6 = (f32[136,128]{1,0:T(8,128)S(1)}, f32[136,128]{1,0:T(8,128)S(1)}, u32[]{:S(2)}, u32[]{:S(2)}) collective-permute-start(f32[136,128]{1,0:T(8,128)S(1)} %get-tuple-element.85), channel_id=1, source_target_pairs={{0,8},{4,12},{8,0},{12,4},{16,24},{20,28},{24,16},{28,20},{1,9},{5... | collective-permute-start | bytes 208904 | tf_op jit(solution)/shard_map/ppermute | solution.py:512
  33.5 5.3 %collective-permute-start.7 = (f32[136,128]{1,0:T(8,128)S(1)}, f32[136,128]{1,0:T(8,128)S(1)}, u32[]{:S(2)}, u32[]{:S(2)}) collective-permute-start(f32[136,128]{1,0:T(8,128)S(1)} %get-tuple-element.86), channel_id=1, source_target_pairs={{0,12},{4,8},{8,4},{12,0},{16,28},{20,24},{24,20},{28,16},{1,13},{... | collective-permute-start | bytes 208904 | tf_op jit(solution)/shard_map/ppermute | solution.py:512
  33.8 7.4 %collective-permute-start.9 = (f32[136,128]{1,0:T(8,128)S(1)}, f32[136,128]{1,0:T(8,128)S(1)}, u32[]{:S(2)}, u32[]{:S(2)}) collective-permute-start(f32[136,128]{1,0:T(8,128)S(1)} %get-tuple-element.100), channel_id=1, source_target_pairs={{0,4},{4,0},{8,12},{12,8},{16,20},{20,16},{24,28},{28,24},{1,5},{5... | collective-permute-start | bytes 208904 | tf_op jit(solution)/shard_map/ppermute | solution.py:512
  35.4 5.9 %collective-permute-start.10 = (f32[136,128]{1,0:T(8,128)S(1)}, f32[136,128]{1,0:T(8,128)S(1)}, u32[]{:S(2)}, u32[]{:S(2)}) collective-permute-start(f32[136,128]{1,0:T(8,128)S(1)} %get-tuple-element.101), channel_id=1, source_target_pairs={{0,8},{4,12},{8,0},{12,4},{16,24},{20,28},{24,16},{28,20},{1,9},{5... | collective-permute-start | bytes 208904 | tf_op jit(solution)/shard_map/ppermute | solution.py:512
  37.4 5.2 %collective-permute-start.11 = (f32[136,128]{1,0:T(8,128)S(1)}, f32[136,128]{1,0:T(8,128)S(1)}, u32[]{:S(2)}, u32[]{:S(2)}) collective-permute-start(f32[136,128]{1,0:T(8,128)S(1)} %get-tuple-element.102), channel_id=1, source_target_pairs={{0,12},{4,8},{8,4},{12,0},{16,28},{20,24},{24,20},{28,16},{1,13},{... | collective-permute-start | bytes 208904 | tf_op jit(solution)/shard_map/ppermute | solution.py:512
  42.6 4.3 %collective-permute-start.14 = (f32[1,128]{1,0:T(1,128)S(1)}, f32[1,128]{1,0:T(1,128)S(1)}, u32[]{:S(2)}, u32[]{:S(2)}) collective-permute-start(f32[1,128]{1,0:T(1,128)S(1)} %shard_map.117.refs_16_), channel_id=1, source_target_pairs={{0,3},{1,2},{2,1},{3,0},{4,7},{5,6},{6,5},{7,4},{8,11},{9,10},{10,... | collective-permute-start | bytes 1544 | tf_op jit(solution)/shard_map/ppermute | solution.py:703
  42.7 4.2 %collective-permute-start.13 = (f32[1,128]{1,0:T(1,128)S(1)}, f32[1,128]{1,0:T(1,128)S(1)}, u32[]{:S(2)}, u32[]{:S(2)}) collective-permute-start(f32[1,128]{1,0:T(1,128)S(1)} %shard_map.117.refs_16_), channel_id=1, source_target_pairs={{0,2},{1,3},{2,0},{3,1},{4,6},{5,7},{6,4},{7,5},{8,10},{9,11},{10,... | collective-permute-start | bytes 1544 | tf_op jit(solution)/shard_map/ppermute | solution.py:703
  44.2 2.7 %collective-permute-start.12 = (f32[1,128]{1,0:T(1,128)S(1)}, f32[1,128]{1,0:T(1,128)S(1)}, u32[]{:S(2)}, u32[]{:S(2)}) collective-permute-start(f32[1,128]{1,0:T(1,128)S(1)} %shard_map.117.refs_16_), channel_id=1, source_target_pairs={{0,1},{1,0},{2,3},{3,2},{4,5},{5,4},{6,7},{7,6},{8,9},{9,8},{10,11... | collective-permute-start | bytes 1544 | tf_op jit(solution)/shard_map/ppermute | solution.py:703

commit v6 on v5

--- a/solution.py
+++ b/solution.py
@@ -114,7 +114,7 @@
     ref[pl.ds(head, rows, stride=ref.shape[0] // rows), :] = value
 
 
-SOONER, LATER = (1, 2), (3, 0)
+SOONER, LATER = (2, 1), (3, 0)
 
 
 def take(pairs, heads):
@@ -231,7 +231,7 @@
     qs = [strided(o.qf, me ^ h, tokens) for h in heads]
     given = [strided(o.gf, me ^ h, tokens) for h in heads]
     solved = chunk(me, heads, o.kf, lambda: vals, rates, o.rows, o, None)
-    reads(heads, qs, given, rates, *solved, me, o)
+    reads(heads, qs, given, rates, *solved, me, o, [o.maps[0], o.later_reads])
 
 
 def next_kernel(group, heads, n, o):
@@ -241,7 +241,7 @@
     chunk(me, heads, n.kf, lambda: vals, n.rates[...], n.rows, o, None)
 
 
-def reads(heads, qs, given, rates, keys, w, e, me, o):
+def reads(heads, qs, given, rates, keys, w, e, me, o, outs):
     tokens = qs[0].shape[0]
     steps = 2 * tokens
     count = range(len(heads))
@@ -254,7 +254,7 @@
     for i in count:
         o.q_unit[i] = units[i]
         o.scores[i] = scores[i]
-        out = o.reads[i]
+        out = outs[i]
         skip = out.shape[1] - 3 * HALF
         out[:, skip : skip + HALF] = units[i] - rows[i][:, :HALF]
         out[:, skip + HALF : skip + 2 * HALF] = rows[i][:, HALF:]
@@ -272,9 +272,13 @@
     rate = [rate_column(rates, me ^ i) for i in every]
     units, inverse = (take(x, every) for x in (n.unit, n.inverse))
     spread = [units[i] - mm(inverse[i], rate[i] * units[i], ta=True) for i in every]
-    reads(heads, qs, given, rates, keys, w, e, me, o)
+    reads(heads, qs, given, rates, keys, w, e, me, o, o.reads)
     for i in every:
         o.kx[i] = spread[i]
+
+
+def hold_kernel(n, o):
+    o.y[...] = n.x[...]
 
 
 def join_kernel(group, n, o):
@@ -527,9 +531,9 @@
     v2 = values.reshape(steps * heads, dim)
     packed = betas.transpose(1, 2, 0).reshape(substeps * heads, tokens)
 
-    def chunk_outs(width):
+    def chunk_outs(*widths):
         return dict(
-            maps=[f32(dim, width) for _ in SOONER],
+            maps=[f32(dim, width) for width in widths],
             unit=f32(2, steps, dim),
             inverse=f32(2, steps, steps),
             w=f32(2, steps, dim),
@@ -551,8 +555,9 @@
             )
         },
         dict(
-            chunk_outs(5 * dim),
+            chunk_outs(5 * dim, 2 * dim),
             **read_outs,
+            later_reads=f32(tokens, 3 * dim),
             rates=f32(steps, heads),
             rows=f32(heads, steps),
             kf=f32(steps * heads, dim),
@@ -565,13 +570,12 @@
         + [pltpu.VMEM((tokens * heads, dim), BF16)] * 2
         + [(substeps * heads, tokens), pltpu.SemaphoreType.DMA((6,))],
         hbm=("k", "v", "q", "og", "packed", "gain"),
-        shared=dict(reads="maps"),
     )
     got = {h: swap(a.maps[i], h) for i, h in enumerate(SOONER)}
     b = call(
         bind(next_kernel, group, LATER),
         dict(kf=a.kf, vf=a.vf, rates=a.rates, rows=a.rows),
-        chunk_outs(2 * dim),
+        chunk_outs(2 * dim, 2 * dim),
     )
     for i, h in enumerate(LATER):
         got[h] = swap(b.maps[i], h) if h else b.maps[i]
@@ -583,15 +587,19 @@
         bind(second_kernel, group, LATER),
         dict(qf=a.qf, gf=a.gf, rates=rates, unit=unit, inverse=inverse, w=w, e=e),
         dict(read_outs, reads=[f32(tokens, 3 * dim)] * 2, kx=f32(heads, steps, dim)),
-        after=[got[SOONER[0]]],
+        after=[got[SOONER[1]]],
         flops=10**9,
     )
     q_unit, scores = [a.q_unit, c.q_unit], [a.scores, c.scores]
-    own_reads, got_reads = {}, {}
-    for i in range(2):
-        own_reads[SOONER[i]], own_reads[LATER[i]] = a.maps[i], c.reads[i]
-        got_reads[SOONER[i]] = got[SOONER[i]]
-        got_reads[LATER[i]] = swap(c.reads[i], LATER[i]) if LATER[i] else c.reads[i]
+    one = call(hold_kernel, dict(x=a.later_reads), dict(y=f32(tokens, 3 * dim)), after=[b.unit]).y
+    own_reads = dict(zip(SOONER + LATER, [a.maps[0], one] + c.reads))
+    got_reads = dict(own_reads)
+    got_reads[SOONER[0]] = got[SOONER[0]]
+    got_reads[SOONER[1]] = swap(one, SOONER[1])
+    held = call(
+        hold_kernel, dict(x=c.reads[0]), dict(y=f32(tokens, 3 * dim)), after=[got[SOONER[0]]]
+    ).y
+    got_reads[LATER[0]] = swap(held, LATER[0])
     own_reads, got_reads = ([x[h] for h in range(heads)] for x in (own_reads, got_reads))
     j = call(
         bind(join_kernel, group),

time: 47.6 us -> 46.8 us (0.983)
  waiting for transfers between devices: 8.6 us -> 5.97 us
  starting transfers between devices: 22.6 us -> 24.4 us
    ppermute x10 -> x11, waiting for transfers between devices: 6.56 us -> 4.64 us  [swap(): lax.ppermute(piece, 'seq', [(d, d ^ i) for d in range(lax.axis_size('seq'...]
    ppermute x10 -> x11, starting transfers between devices: 15 us -> 16.9 us  [swap(): lax.ppermute(piece, 'seq', [(d, d ^ i) for d in range(lax.axis_size('seq'...]
    ppermute x1, waiting for transfers between devices: 2.03 us -> 1.32 us  [local(): entry = lax.ppermute(j.total, 'seq', across if two else ahead)]
    pallas_call x10 -> x12, Pallas kernels: 15 us -> 15 us  [call(): pl.pallas_call(kernel, out_shape=flat_outs, in_specs=specs + [pl.BlockSpe...]
  transfers between devices with their start and end apart: 15 -> 16, of which waited for: 5 -> 5; matrix products, arithmetic and copies ran while one was open for 0% -> 0% of each run, Pallas kernels for 20% -> 21%
where the time goes in v6:
time: 46.8 us; the launch traced here: 46.6 us
  starting transfers between devices  24.4 us (52%)
  Pallas kernels  15 us (32%)
  waiting for transfers between devices  5.97 us (13%)
  between operations  0.71 us (2%)
  other arithmetic  0.52 us (1%)
    ppermute x11, starting transfers between devices, swap(): lax.ppermute(piece, 'seq', [(d, d ^ i) for d in range(lax.axis_size('seq'...  16.9 us
    pallas_call x12, Pallas kernels, call(): pl.pallas_call(kernel, out_shape=flat_outs, in_specs=specs + [pl.BlockSpe...  15 us
    ppermute x11, waiting for transfers between devices, swap(): lax.ppermute(piece, 'seq', [(d, d ^ i) for d in range(lax.axis_size('seq'...  4.64 us
    ppermute x1, starting transfers between devices, local(): entry = lax.ppermute(j.total, 'seq', across if two else ahead)  2.79 us
    ppermute x1, starting transfers between devices, local(): entry = lax.ppermute(own.total, 'seq', across if two else behind)  2.79 us
    ppermute x3, starting transfers between devices, local(): lax.ppermute(sums, 'head', [(d, d ^ flip) for d in range(size)])  1.92 us
    ppermute x1, waiting for transfers between devices, local(): entry = lax.ppermute(j.total, 'seq', across if two else ahead)  1.32 us
  transfers between devices with their start and end apart: 16, of which 5 were waited for; matrix products, arithmetic and copies ran while one was open for 0% of the time, Pallas kernels for 21%

profile of v6, /device:TPU:0, one launch (start us, length us, event | category | flops | bytes accessed | tf_op | source)
XLA Modules:
  0.0 46.6 jit_solution(11450950218577453957)
XLA Ops:
  0.6 4.2 %shard_map.109 = (f32[2,256,128]{2,1,0:T(8,128)S(1)}, f32[1,128]{1,0:T(1,128)S(1)}, f32[512,128]{1,0:T(8,128)S(1)}, f32[2,256,256]{2,1,0:T(8,128)S(1)}, f32[1024...) custom-call(bf16[1024,128]{1,0:T(8,128)(2,1)} %bitcast.17, ...), custom_call_target="tpu_custom_call" | custom-call | flops 1000 | tf_op jit(solution)/shard_map/pallas_call | solution.py:504
  4.8 3.1 %collective-permute-start.1 = (f32[128,640]{1,0:T(8,128)S(1)}, f32[128,640]{1,0:T(8,128)S(1)}, u32[]{:S(2)}, u32[]{:S(2)}) collective-permute-start(f32[128,640]{1,0:T(8,128)S(1)} %get-tuple-element.63.refs_6_), channel_id=1, source_target_pairs={{0,8},{4,12},{8,0},{12,4},{16,24},{20,28},{24,16},{28,20},{1,9},{5... | collective-permute-start | bytes 983048 | tf_op jit(solution)/shard_map/ppermute | solution.py:516
  7.9 1.5 %collective-permute-start = (f32[128,256]{1,0:T(8,128)S(1)}, f32[128,256]{1,0:T(8,128)S(1)}, u32[]{:S(2)}, u32[]{:S(2)}) collective-permute-start(f32[128,256]{1,0:T(8,128)S(1)} %get-tuple-element.62), channel_id=1, source_target_pairs={{0,4},{4,0},{8,12},{12,8},{16,20},{20,16},{24,28},{28,24},{1,5},{5... | collective-permute-start | bytes 393224 | tf_op jit(solution)/shard_map/ppermute | solution.py:516
  9.4 2.4 %shard_map.110 = (f32[2,256,128]{2,1,0:T(8,128)S(1)}, f32[2,256,256]{2,1,0:T(8,128)S(1)}, f32[128,256]{1,0:T(8,128)S(1)}, f32[128,256]{1,0:T(8,128)S(1)}, f32[2,...) custom-call(f32[1024,128]{1,0:T(8,128)S(1)} %get-tuple-element.57.refs_0_, f32[1024,128]{1,0:T(8,128)S(1)} %get-tuple-element.58.refs_1_, ...), custom_call_target="tpu_custom_call" | custom-call | flops 1000 | tf_op jit(solution)/shard_map/pallas_call | solution.py:504
  11.8 0.1 collective-permute-start.2
  11.9 2.0 %collective-permute-start.4 = (f32[128,384]{1,0:T(8,128)S(1)}, f32[128,384]{1,0:T(8,128)S(1)}, u32[]{:S(2)}, u32[]{:S(2)}) collective-permute-start(f32[128,384]{1,0:T(8,128)S(1)} %shard_map.113.refs_5_), channel_id=1, source_target_pairs={{0,4},{4,0},{8,12},{12,8},{16,20},{20,16},{24,28},{28,24},{1,5},{5... | collective-permute-start | bytes 589832 | tf_op jit(solution)/shard_map/ppermute | solution.py:516
  13.9 0.0 collective-permute-done.refs_11_.refs_1_
  13.9 1.0 %shard_map.111 = (f32[4,256,128]{2,1,0:T(8,128)S(1)}, f32[2,128,128]{2,1,0:T(8,128)S(1)}, f32[128,384]{1,0:T(8,128)S(1)}, f32[128,384]{1,0:T(8,128)S(1)}, f32[2,128,256]{2,1,0:T(8,128)S(1)}) custom-call(f32[512,128]{1,0:T(8,128)S(1)} %get-tuple-element.65.refs_0_.refs_9_, f32[512,128]{1,0:T(8,128)S(1)} %get-tuple-element.66.refs_1_, ...), custom_call_target="tpu_custom_call" | custom-call | flops 1000000000 | tf_op jit(solution)/shard_map/pallas_call | solution.py:504
  14.9 1.5 %collective-permute-done.1.refs_2_.refs_1_.refs_3_ = f32[128,640]{1,0:T(8,128)S(1)} collective-permute-done((f32[128,640]{1,0:T(8,128)S(1)}, f32[128,640]{1,0:T(8,128)S(1)}, u32[]{:S(2)}, u32[]{:S(2)}) %collective-permute-start.1) | collective-permute-done | bytes 327712 | tf_op jit(solution)/shard_map/ppermute | solution.py:516
  16.4 3.1 %collective-permute-start.5 = (f32[128,384]{1,0:T(8,128)S(1)}, f32[128,384]{1,0:T(8,128)S(1)}, u32[]{:S(2)}, u32[]{:S(2)}) collective-permute-start(f32[128,384]{1,0:T(8,128)S(1)} %shard_map.114), channel_id=1, source_target_pairs={{0,12},{4,8},{8,4},{12,0},{16,28},{20,24},{24,20},{28,16},{1,13},{... | collective-permute-start | bytes 589832 | tf_op jit(solution)/shard_map/ppermute | solution.py:516
  19.5 1.1 %collective-permute-done.2.refs_3_ = f32[128,256]{1,0:T(8,128)S(1)} collective-permute-done((f32[128,256]{1,0:T(8,128)S(1)}, f32[128,256]{1,0:T(8,128)S(1)}, u32[]{:S(2)}, u32[]{:S(2)}) %collective-permute-start.2) | collective-permute-done | bytes 131104 | tf_op jit(solution)/shard_map/ppermute | solution.py:516
  20.6 0.6 %shard_map.112 = (f32[4,128,256]{2,1,0:T(8,128)S(1)}, f32[4,128,128]{2,1,0:T(8,128)S(1)}, f32[128,128]{1,0:T(8,128)S(1)}) custom-call(f32[128,256]{1,0:T(8,128)S(1)} %get-tuple-element.61.refs_0_, f32[128,256]{1,0:T(8,128)S(1)} %collective-permute-done.refs_11_.refs_1_, f32[128,640]{1,0:T(8,128)S(1)} %collective-permute-done.1.refs_2_.refs_1_.refs_3_, ...), custom_call_target="tpu_custom_call" | custom-call | flops 1000 | tf_op jit(solution)/shard_map/pallas_call | solution.py:504
  21.2 2.8 %collective-permute-start.3 = (f32[128,128]{1,0:T(8,128)S(1)}, f32[128,128]{1,0:T(8,128)S(1)}, u32[]{:S(2)}, u32[]{:S(2)}) collective-permute-start(f32[128,128]{1,0:T(8,128)S(1)} %get-tuple-element.76), channel_id=1, source_target_pairs={{0,16},{4,20},{8,24},{12,28},{16,0},{20,4},{24,8},{28,12},{1,17},{... | collective-permute-start | bytes 196616 | tf_op jit(solution)/shard_map/ppermute | solution.py:615
  24.0 0.5 %shard_map.115 = (f32[4,128,128]{2,1,0:T(8,128)S(1)}, f32[5,128,128]{2,1,0:T(8,128)S(1)}, f32[128,128]{1,0:T(8,128)S(1)}) custom-call(f32[4,128,256]{2,1,0:T(8,128)S(1)} %get-tuple-element.81.refs_0_.refs_6_), custom_call_target="tpu_custom_call" | custom-call | flops 1000 | tf_op jit(solution)/shard_map/pallas_call | solution.py:504
  24.5 0.6 %collective-permute-done.4.refs_2_ = f32[128,384]{1,0:T(8,128)S(1)} collective-permute-done((f32[128,384]{1,0:T(8,128)S(1)}, f32[128,384]{1,0:T(8,128)S(1)}, u32[]{:S(2)}, u32[]{:S(2)}) %collective-permute-start.4) | collective-permute-done | bytes 196640 | tf_op jit(solution)/shard_map/ppermute | solution.py:516
  25.1 1.3 %collective-permute-done.3.refs_0_ = f32[128,128]{1,0:T(8,128)S(1)} collective-permute-done((f32[128,128]{1,0:T(8,128)S(1)}, f32[128,128]{1,0:T(8,128)S(1)}, u32[]{:S(2)}, u32[]{:S(2)}) %collective-permute-start.3) | collective-permute-done | bytes 65568 | tf_op jit(solution)/shard_map/ppermute | solution.py:615
  26.4 0.0 collective-permute-done.5.refs_4_
  26.4 1.3 %shard_map.116 = (f32[4,128,128]{2,1,0:T(8,128)}, f32[4,128,128]{2,1,0:T(8,128)S(1)}, f32[136,128]{1,0:T(8,128)S(1)}, f32[136,128]{1,0:T(8,128)S(1)}, f32[136,12...) custom-call(f32[128,128]{1,0:T(8,128)S(1)} %collective-permute-done.3.refs_0_, ...), custom_call_target="tpu_custom_call" | custom-call | flops 1000 | tf_op jit(solution)/shard_map/pallas_call | solution.py:504
  27.7 2.8 %collective-permute-start.9 = (f32[136,128]{1,0:T(8,128)S(1)}, f32[136,128]{1,0:T(8,128)S(1)}, u32[]{:S(2)}, u32[]{:S(2)}) collective-permute-start(f32[136,128]{1,0:T(8,128)S(1)} %get-tuple-element.93), channel_id=1, source_target_pairs={{0,16},{4,20},{8,24},{12,28},{16,0},{20,4},{24,8},{28,12},{1,17},{... | collective-permute-start | bytes 208904 | tf_op jit(solution)/shard_map/ppermute | solution.py:647
  30.5 0.1 collective-permute-start.6
  30.6 2.0 %collective-permute-start.7 = (f32[136,128]{1,0:T(8,128)S(1)}, f32[136,128]{1,0:T(8,128)S(1)}, u32[]{:S(2)}, u32[]{:S(2)}) collective-permute-start(f32[136,128]{1,0:T(8,128)S(1)} %get-tuple-element.87), channel_id=1, source_target_pairs={{0,8},{4,12},{8,0},{12,4},{16,24},{20,28},{24,16},{28,20},{1,9},{5... | collective-permute-start | bytes 208904 | tf_op jit(solution)/shard_map/ppermute | solution.py:516
  32.6 1.5 %collective-permute-start.8 = (f32[136,128]{1,0:T(8,128)S(1)}, f32[136,128]{1,0:T(8,128)S(1)}, u32[]{:S(2)}, u32[]{:S(2)}) collective-permute-start(f32[136,128]{1,0:T(8,128)S(1)} %get-tuple-element.88), channel_id=1, source_target_pairs={{0,12},{4,8},{8,4},{12,0},{16,28},{20,24},{24,20},{28,16},{1,13},{... | collective-permute-start | bytes 208904 | tf_op jit(solution)/shard_map/ppermute | solution.py:516
  34.1 0.0 collective-permute-done.9.refs_0_
  34.1 0.3 shard_map.117
  34.4 0.6 %collective-permute-start.10 = (f32[136,128]{1,0:T(8,128)S(1)}, f32[136,128]{1,0:T(8,128)S(1)}, u32[]{:S(2)}, u32[]{:S(2)}) collective-permute-start(f32[136,128]{1,0:T(8,128)S(1)} %get-tuple-element.102), channel_id=1, source_target_pairs={{0,4},{4,0},{8,12},{12,8},{16,20},{20,16},{24,28},{28,24},{1,5},{5... | collective-permute-start | bytes 208904 | tf_op jit(solution)/shard_map/ppermute | solution.py:516
  35.0 1.5 %collective-permute-start.11 = (f32[136,128]{1,0:T(8,128)S(1)}, f32[136,128]{1,0:T(8,128)S(1)}, u32[]{:S(2)}, u32[]{:S(2)}) collective-permute-start(f32[136,128]{1,0:T(8,128)S(1)} %get-tuple-element.103), channel_id=1, source_target_pairs={{0,8},{4,12},{8,0},{12,4},{16,24},{20,28},{24,16},{28,20},{1,9},{5... | collective-permute-start | bytes 208904 | tf_op jit(solution)/shard_map/ppermute | solution.py:516
  36.6 0.0 collective-permute-done.6.refs_1_.refs_13_
  36.6 1.4 %collective-permute-start.12 = (f32[136,128]{1,0:T(8,128)S(1)}, f32[136,128]{1,0:T(8,128)S(1)}, u32[]{:S(2)}, u32[]{:S(2)}) collective-permute-start(f32[136,128]{1,0:T(8,128)S(1)} %get-tuple-element.104), channel_id=1, source_target_pairs={{0,12},{4,8},{8,4},{12,0},{16,28},{20,24},{24,20},{28,16},{1,13},{... | collective-permute-start | bytes 208904 | tf_op jit(solution)/shard_map/ppermute | solution.py:516
  37.9 0.0 collective-permute-done.7.refs_2_.refs_14_
  37.9 0.0 collective-permute-done.8.refs_3_.refs_15_
  38.0 2.4 %shard_map.118 = (f32[4,256,128]{2,1,0:T(8,128)S(1)}, bf16[512,128]{1,0:T(8,128)(2,1)}, f32[4,256,128]{2,1,0:T(8,128)S(1)}, bf16[512,128]{1,0:T(8,128)(2,1)}, f32[4,256,128]{2,1,0:T(8,128)S(1)}) custom-call(f32[136,128]{1,0:T(8,128)S(1)} %get-tuple-element.85.refs_0_.refs_12_, f32[136,128]{1,0:T(8,128)S(1)} %collective-permute-done.6.refs_1_.refs_13_, ...), custom_call_target="tpu_custom_call" | custom-call | flops 1000 | tf_op jit(solution)/shard_map/pallas_call | solution.py:504
  40.4 0.0 collective-permute-done.10.refs_5_.refs_9_
  40.4 0.0 collective-permute-done.11.refs_6_.refs_10_
  40.4 1.4 %collective-permute-done.12.refs_7_.refs_11_ = f32[136,128]{1,0:T(8,128)S(1)} collective-permute-done((f32[136,128]{1,0:T(8,128)S(1)}, f32[136,128]{1,0:T(8,128)S(1)}, u32[]{:S(2)}, u32[]{:S(2)}) %collective-permute-start.12) | collective-permute-done | bytes 69664 | tf_op jit(solution)/shard_map/ppermute | solution.py:516
  41.8 0.1 collective-permute-start.15
  41.9 1.6 %collective-permute-start.14 = (f32[1,128]{1,0:T(1,128)S(1)}, f32[1,128]{1,0:T(1,128)S(1)}, u32[]{:S(2)}, u32[]{:S(2)}) collective-permute-start(f32[1,128]{1,0:T(1,128)S(1)} %shard_map.119.refs_16_), channel_id=1, source_target_pairs={{0,2},{1,3},{2,0},{3,1},{4,6},{5,7},{6,4},{7,5},{8,10},{9,11},{10,... | collective-permute-start | bytes 1544 | tf_op jit(solution)/shard_map/ppermute | solution.py:711
  43.4 0.3 collective-permute-start.13
  43.7 2.4 %shard_map.120 = (f32[8,128]{1,0:T(8,128)}, bf16[1024,128]{1,0:T(8,128)(2,1)}, bf16[1024,128]{1,0:T(8,128)(2,1)}) custom-call(f32[1024,128]{1,0:T(8,128)S(1)} %get-tuple-element.57.refs_0_, f32[256,4]{1,0:T(8,128)S(1)} %get-tuple-element.59.refs_2_.refs_10_.refs_1_, f32[2,256,128]{2,1,0:T(8,128)S(1)} %get-tuple-element.67.refs_3_.refs_17_.refs_2_, ...), custom_call_target="tpu_custom_call" | custom-call | flops 1000 | tf_op jit(solution)/shard_map/pallas_call | solution.py:504
  46.1 0.0 collective-permute-done.15
  46.1 0.0 collective-permute-done.14
  46.1 0.0 collective-permute-done.13
  46.1 0.5 %add_bitcast_fusion = f32[128]{0:T(128)} fusion(f32[1,128]{1,0:T(1,128)S(1)} %shard_map.119.refs_16_, f32[1,128]{1,0:T(1,128)S(1)} %collective-permute-done.15, f32[1,128]{1,0:T(1,128)S(1)} %collective-permute-done.13, f32[1,128]{1,0:T(1,128)S(1)} %collective-permute-done.14), kind=kLoop, calls=%fused_computation | loop fusion | flops 384 | bytes 2560 | tf_op jit(solution)/shard_map/reshape | solution.py:722
  (3 shorter events, 0.0 us)
Async XLA Ops:
  4.8 11.6 %collective-permute-start.1 = (f32[128,640]{1,0:T(8,128)S(1)}, f32[128,640]{1,0:T(8,128)S(1)}, u32[]{:S(2)}, u32[]{:S(2)}) collective-permute-start(f32[128,640]{1,0:T(8,128)S(1)} %get-tuple-element.63.refs_6_), channel_id=1, source_target_pairs={{0,8},{4,12},{8,0},{12,4},{16,24},{20,28},{24,16},{28,20},{1,9},{5... | collective-permute-start | bytes 983048 | tf_op jit(solution)/shard_map/ppermute | solution.py:516
  7.9 6.0 %collective-permute-start = (f32[128,256]{1,0:T(8,128)S(1)}, f32[128,256]{1,0:T(8,128)S(1)}, u32[]{:S(2)}, u32[]{:S(2)}) collective-permute-start(f32[128,256]{1,0:T(8,128)S(1)} %get-tuple-element.62), channel_id=1, source_target_pairs={{0,4},{4,0},{8,12},{12,8},{16,20},{20,16},{24,28},{28,24},{1,5},{5... | collective-permute-start | bytes 393224 | tf_op jit(solution)/shard_map/ppermute | solution.py:516
  11.8 8.8 %collective-permute-start.2 = (f32[128,256]{1,0:T(8,128)S(1)}, f32[128,256]{1,0:T(8,128)S(1)}, u32[]{:S(2)}, u32[]{:S(2)}) collective-permute-start(f32[128,256]{1,0:T(8,128)S(1)} %get-tuple-element.64), channel_id=1, source_target_pairs={{0,12},{4,8},{8,4},{12,0},{16,28},{20,24},{24,20},{28,16},{1,13},{... | collective-permute-start | bytes 393224 | tf_op jit(solution)/shard_map/ppermute | solution.py:516
  11.9 13.2 %collective-permute-start.4 = (f32[128,384]{1,0:T(8,128)S(1)}, f32[128,384]{1,0:T(8,128)S(1)}, u32[]{:S(2)}, u32[]{:S(2)}) collective-permute-start(f32[128,384]{1,0:T(8,128)S(1)} %shard_map.113.refs_5_), channel_id=1, source_target_pairs={{0,4},{4,0},{8,12},{12,8},{16,20},{20,16},{24,28},{28,24},{1,5},{5... | collective-permute-start | bytes 589832 | tf_op jit(solution)/shard_map/ppermute | solution.py:516
  16.4 10.0 %collective-permute-start.5 = (f32[128,384]{1,0:T(8,128)S(1)}, f32[128,384]{1,0:T(8,128)S(1)}, u32[]{:S(2)}, u32[]{:S(2)}) collective-permute-start(f32[128,384]{1,0:T(8,128)S(1)} %shard_map.114), channel_id=1, source_target_pairs={{0,12},{4,8},{8,4},{12,0},{16,28},{20,24},{24,20},{28,16},{1,13},{... | collective-permute-start | bytes 589832 | tf_op jit(solution)/shard_map/ppermute | solution.py:516
  21.2 5.2 %collective-permute-start.3 = (f32[128,128]{1,0:T(8,128)S(1)}, f32[128,128]{1,0:T(8,128)S(1)}, u32[]{:S(2)}, u32[]{:S(2)}) collective-permute-start(f32[128,128]{1,0:T(8,128)S(1)} %get-tuple-element.76), channel_id=1, source_target_pairs={{0,16},{4,20},{8,24},{12,28},{16,0},{20,4},{24,8},{28,12},{1,17},{... | collective-permute-start | bytes 196616 | tf_op jit(solution)/shard_map/ppermute | solution.py:615
  27.7 6.4 %collective-permute-start.9 = (f32[136,128]{1,0:T(8,128)S(1)}, f32[136,128]{1,0:T(8,128)S(1)}, u32[]{:S(2)}, u32[]{:S(2)}) collective-permute-start(f32[136,128]{1,0:T(8,128)S(1)} %get-tuple-element.93), channel_id=1, source_target_pairs={{0,16},{4,20},{8,24},{12,28},{16,0},{20,4},{24,8},{28,12},{1,17},{... | collective-permute-start | bytes 208904 | tf_op jit(solution)/shard_map/ppermute | solution.py:647
  30.5 6.0 %collective-permute-start.6 = (f32[136,128]{1,0:T(8,128)S(1)}, f32[136,128]{1,0:T(8,128)S(1)}, u32[]{:S(2)}, u32[]{:S(2)}) collective-permute-start(f32[136,128]{1,0:T(8,128)S(1)} %get-tuple-element.86), channel_id=1, source_target_pairs={{0,4},{4,0},{8,12},{12,8},{16,20},{20,16},{24,28},{28,24},{1,5},{5... | collective-permute-start | bytes 208904 | tf_op jit(solution)/shard_map/ppermute | solution.py:516
  30.6 7.3 %collective-permute-start.7 = (f32[136,128]{1,0:T(8,128)S(1)}, f32[136,128]{1,0:T(8,128)S(1)}, u32[]{:S(2)}, u32[]{:S(2)}) collective-permute-start(f32[136,128]{1,0:T(8,128)S(1)} %get-tuple-element.87), channel_id=1, source_target_pairs={{0,8},{4,12},{8,0},{12,4},{16,24},{20,28},{24,16},{28,20},{1,9},{5... | collective-permute-start | bytes 208904 | tf_op jit(solution)/shard_map/ppermute | solution.py:516
  32.6 5.3 %collective-permute-start.8 = (f32[136,128]{1,0:T(8,128)S(1)}, f32[136,128]{1,0:T(8,128)S(1)}, u32[]{:S(2)}, u32[]{:S(2)}) collective-permute-start(f32[136,128]{1,0:T(8,128)S(1)} %get-tuple-element.88), channel_id=1, source_target_pairs={{0,12},{4,8},{8,4},{12,0},{16,28},{20,24},{24,20},{28,16},{1,13},{... | collective-permute-start | bytes 208904 | tf_op jit(solution)/shard_map/ppermute | solution.py:516
  34.4 6.0 %collective-permute-start.10 = (f32[136,128]{1,0:T(8,128)S(1)}, f32[136,128]{1,0:T(8,128)S(1)}, u32[]{:S(2)}, u32[]{:S(2)}) collective-permute-start(f32[136,128]{1,0:T(8,128)S(1)} %get-tuple-element.102), channel_id=1, source_target_pairs={{0,4},{4,0},{8,12},{12,8},{16,20},{20,16},{24,28},{28,24},{1,5},{5... | collective-permute-start | bytes 208904 | tf_op jit(solution)/shard_map/ppermute | solution.py:516
  35.0 5.3 %collective-permute-start.11 = (f32[136,128]{1,0:T(8,128)S(1)}, f32[136,128]{1,0:T(8,128)S(1)}, u32[]{:S(2)}, u32[]{:S(2)}) collective-permute-start(f32[136,128]{1,0:T(8,128)S(1)} %get-tuple-element.103), channel_id=1, source_target_pairs={{0,8},{4,12},{8,0},{12,4},{16,24},{20,28},{24,16},{28,20},{1,9},{5... | collective-permute-start | bytes 208904 | tf_op jit(solution)/shard_map/ppermute | solution.py:516
  36.6 5.2 %collective-permute-start.12 = (f32[136,128]{1,0:T(8,128)S(1)}, f32[136,128]{1,0:T(8,128)S(1)}, u32[]{:S(2)}, u32[]{:S(2)}) collective-permute-start(f32[136,128]{1,0:T(8,128)S(1)} %get-tuple-element.104), channel_id=1, source_target_pairs={{0,12},{4,8},{8,4},{12,0},{16,28},{20,24},{24,20},{28,16},{1,13},{... | collective-permute-start | bytes 208904 | tf_op jit(solution)/shard_map/ppermute | solution.py:516
  41.8 4.3 %collective-permute-start.15 = (f32[1,128]{1,0:T(1,128)S(1)}, f32[1,128]{1,0:T(1,128)S(1)}, u32[]{:S(2)}, u32[]{:S(2)}) collective-permute-start(f32[1,128]{1,0:T(1,128)S(1)} %shard_map.119.refs_16_), channel_id=1, source_target_pairs={{0,3},{1,2},{2,1},{3,0},{4,7},{5,6},{6,5},{7,4},{8,11},{9,10},{10,... | collective-permute-start | bytes 1544 | tf_op jit(solution)/shard_map/ppermute | solution.py:711
  41.9 4.2 %collective-permute-start.14 = (f32[1,128]{1,0:T(1,128)S(1)}, f32[1,128]{1,0:T(1,128)S(1)}, u32[]{:S(2)}, u32[]{:S(2)}) collective-permute-start(f32[1,128]{1,0:T(1,128)S(1)} %shard_map.119.refs_16_), channel_id=1, source_target_pairs={{0,2},{1,3},{2,0},{3,1},{4,6},{5,7},{6,4},{7,5},{8,10},{9,11},{10,... | collective-permute-start | bytes 1544 | tf_op jit(solution)/shard_map/ppermute | solution.py:711
  43.4 2.7 %collective-permute-start.13 = (f32[1,128]{1,0:T(1,128)S(1)}, f32[1,128]{1,0:T(1,128)S(1)}, u32[]{:S(2)}, u32[]{:S(2)}) collective-permute-start(f32[1,128]{1,0:T(1,128)S(1)} %shard_map.119.refs_16_), channel_id=1, source_target_pairs={{0,1},{1,0},{2,3},{3,2},{4,5},{5,4},{6,7},{7,6},{8,9},{9,8},{10,11... | collective-permute-start | bytes 1544 | tf_op jit(solution)/shard_map/ppermute | solution.py:711

commit v7 on v6

--- a/solution.py
+++ b/solution.py
@@ -679,7 +679,7 @@
             z=f32(heads, steps, dim),
         ),
         scratch=[(tokens * heads, dim)] * 2,
-        after=[first_adjoint],
+        after=[first_adjoint, adjoints[1], adjoints[2]],
     )
     sums = call(
         gain_kernel, dict(states=states, adjoints=adjoints), dict(gain=f32(1, dim)), after=[t.err]

time: 46.8 us -> 46.7 us (level)
  transfers between devices with their start and end apart: 16 -> 16, of which waited for: 5 -> 7; matrix products, arithmetic and copies ran while one was open for 0% -> 0% of each run, Pallas kernels for 21% -> 20%
where the time goes in v7:
time: 46.7 us; the launch traced here: 46.5 us
  starting transfers between devices  24.4 us (52%)
  Pallas kernels  14.9 us (32%)
  waiting for transfers between devices  6.05 us (13%)
  between operations  0.71 us (2%)
  other arithmetic  0.52 us (1%)
    ppermute x11, starting transfers between devices, swap(): lax.ppermute(piece, 'seq', [(d, d ^ i) for d in range(lax.axis_size('seq'...  16.9 us
    pallas_call x12, Pallas kernels, call(): pl.pallas_call(kernel, out_shape=flat_outs, in_specs=specs + [pl.BlockSpe...  14.9 us
    ppermute x11, waiting for transfers between devices, swap(): lax.ppermute(piece, 'seq', [(d, d ^ i) for d in range(lax.axis_size('seq'...  4.73 us
    ppermute x1, starting transfers between devices, local(): entry = lax.ppermute(j.total, 'seq', across if two else ahead)  2.8 us
    ppermute x1, starting transfers between devices, local(): entry = lax.ppermute(own.total, 'seq', across if two else behind)  2.79 us
    ppermute x3, starting transfers between devices, local(): lax.ppermute(sums, 'head', [(d, d ^ flip) for d in range(size)])  1.92 us
    ppermute x1, waiting for transfers between devices, local(): entry = lax.ppermute(j.total, 'seq', across if two else ahead)  1.32 us
  transfers between devices with their start and end apart: 16, of which 7 were waited for; matrix products, arithmetic and copies ran while one was open for 0% of the time, Pallas kernels for 20%

profile of v7, /device:TPU:0, one launch (start us, length us, event | category | flops | bytes accessed | tf_op | source)
XLA Modules:
  0.0 46.5 jit_solution(14087965304017003263)
XLA Ops:
  0.6 4.1 %shard_map.109 = (f32[2,256,128]{2,1,0:T(8,128)S(1)}, f32[1,128]{1,0:T(1,128)S(1)}, f32[512,128]{1,0:T(8,128)S(1)}, f32[2,256,256]{2,1,0:T(8,128)S(1)}, f32[1024...) custom-call(bf16[1024,128]{1,0:T(8,128)(2,1)} %bitcast.17, ...), custom_call_target="tpu_custom_call" | custom-call | flops 1000 | tf_op jit(solution)/shard_map/pallas_call | solution.py:504
  4.8 3.1 %collective-permute-start.1 = (f32[128,640]{1,0:T(8,128)S(1)}, f32[128,640]{1,0:T(8,128)S(1)}, u32[]{:S(2)}, u32[]{:S(2)}) collective-permute-start(f32[128,640]{1,0:T(8,128)S(1)} %get-tuple-element.63.refs_6_), channel_id=1, source_target_pairs={{0,8},{4,12},{8,0},{12,4},{16,24},{20,28},{24,16},{28,20},{1,9},{5... | collective-permute-start | bytes 983048 | tf_op jit(solution)/shard_map/ppermute | solution.py:516
  7.9 1.5 %collective-permute-start = (f32[128,256]{1,0:T(8,128)S(1)}, f32[128,256]{1,0:T(8,128)S(1)}, u32[]{:S(2)}, u32[]{:S(2)}) collective-permute-start(f32[128,256]{1,0:T(8,128)S(1)} %get-tuple-element.62), channel_id=1, source_target_pairs={{0,4},{4,0},{8,12},{12,8},{16,20},{20,16},{24,28},{28,24},{1,5},{5... | collective-permute-start | bytes 393224 | tf_op jit(solution)/shard_map/ppermute | solution.py:516
  9.4 2.4 %shard_map.110 = (f32[2,256,128]{2,1,0:T(8,128)S(1)}, f32[2,256,256]{2,1,0:T(8,128)S(1)}, f32[128,256]{1,0:T(8,128)S(1)}, f32[128,256]{1,0:T(8,128)S(1)}, f32[2,...) custom-call(f32[1024,128]{1,0:T(8,128)S(1)} %get-tuple-element.57.refs_0_, f32[1024,128]{1,0:T(8,128)S(1)} %get-tuple-element.58.refs_1_, ...), custom_call_target="tpu_custom_call" | custom-call | flops 1000 | tf_op jit(solution)/shard_map/pallas_call | solution.py:504
  11.8 0.1 collective-permute-start.2
  11.9 2.0 %collective-permute-start.4 = (f32[128,384]{1,0:T(8,128)S(1)}, f32[128,384]{1,0:T(8,128)S(1)}, u32[]{:S(2)}, u32[]{:S(2)}) collective-permute-start(f32[128,384]{1,0:T(8,128)S(1)} %shard_map.113.refs_5_), channel_id=1, source_target_pairs={{0,4},{4,0},{8,12},{12,8},{16,20},{20,16},{24,28},{28,24},{1,5},{5... | collective-permute-start | bytes 589832 | tf_op jit(solution)/shard_map/ppermute | solution.py:516
  13.9 0.0 collective-permute-done.refs_11_.refs_1_
  13.9 1.0 %shard_map.111 = (f32[4,256,128]{2,1,0:T(8,128)S(1)}, f32[2,128,128]{2,1,0:T(8,128)S(1)}, f32[128,384]{1,0:T(8,128)S(1)}, f32[128,384]{1,0:T(8,128)S(1)}, f32[2,128,256]{2,1,0:T(8,128)S(1)}) custom-call(f32[512,128]{1,0:T(8,128)S(1)} %get-tuple-element.65.refs_0_.refs_9_, f32[512,128]{1,0:T(8,128)S(1)} %get-tuple-element.66.refs_1_, ...), custom_call_target="tpu_custom_call" | custom-call | flops 1000000000 | tf_op jit(solution)/shard_map/pallas_call | solution.py:504
  14.9 1.5 %collective-permute-done.1.refs_2_.refs_1_.refs_3_ = f32[128,640]{1,0:T(8,128)S(1)} collective-permute-done((f32[128,640]{1,0:T(8,128)S(1)}, f32[128,640]{1,0:T(8,128)S(1)}, u32[]{:S(2)}, u32[]{:S(2)}) %collective-permute-start.1) | collective-permute-done | bytes 327712 | tf_op jit(solution)/shard_map/ppermute | solution.py:516
  16.4 3.1 %collective-permute-start.5 = (f32[128,384]{1,0:T(8,128)S(1)}, f32[128,384]{1,0:T(8,128)S(1)}, u32[]{:S(2)}, u32[]{:S(2)}) collective-permute-start(f32[128,384]{1,0:T(8,128)S(1)} %shard_map.114), channel_id=1, source_target_pairs={{0,12},{4,8},{8,4},{12,0},{16,28},{20,24},{24,20},{28,16},{1,13},{... | collective-permute-start | bytes 589832 | tf_op jit(solution)/shard_map/ppermute | solution.py:516
  19.5 1.1 %collective-permute-done.2.refs_3_ = f32[128,256]{1,0:T(8,128)S(1)} collective-permute-done((f32[128,256]{1,0:T(8,128)S(1)}, f32[128,256]{1,0:T(8,128)S(1)}, u32[]{:S(2)}, u32[]{:S(2)}) %collective-permute-start.2) | collective-permute-done | bytes 131104 | tf_op jit(solution)/shard_map/ppermute | solution.py:516
  20.6 0.6 %shard_map.112 = (f32[4,128,256]{2,1,0:T(8,128)S(1)}, f32[4,128,128]{2,1,0:T(8,128)S(1)}, f32[128,128]{1,0:T(8,128)S(1)}) custom-call(f32[128,256]{1,0:T(8,128)S(1)} %get-tuple-element.61.refs_0_, f32[128,256]{1,0:T(8,128)S(1)} %collective-permute-done.refs_11_.refs_1_, f32[128,640]{1,0:T(8,128)S(1)} %collective-permute-done.1.refs_2_.refs_1_.refs_3_, ...), custom_call_target="tpu_custom_call" | custom-call | flops 1000 | tf_op jit(solution)/shard_map/pallas_call | solution.py:504
  21.2 2.8 %collective-permute-start.3 = (f32[128,128]{1,0:T(8,128)S(1)}, f32[128,128]{1,0:T(8,128)S(1)}, u32[]{:S(2)}, u32[]{:S(2)}) collective-permute-start(f32[128,128]{1,0:T(8,128)S(1)} %get-tuple-element.76), channel_id=1, source_target_pairs={{0,16},{4,20},{8,24},{12,28},{16,0},{20,4},{24,8},{28,12},{1,17},{... | collective-permute-start | bytes 196616 | tf_op jit(solution)/shard_map/ppermute | solution.py:615
  24.0 0.5 %shard_map.115 = (f32[4,128,128]{2,1,0:T(8,128)S(1)}, f32[5,128,128]{2,1,0:T(8,128)S(1)}, f32[128,128]{1,0:T(8,128)S(1)}) custom-call(f32[4,128,256]{2,1,0:T(8,128)S(1)} %get-tuple-element.81.refs_0_.refs_6_), custom_call_target="tpu_custom_call" | custom-call | flops 1000 | tf_op jit(solution)/shard_map/pallas_call | solution.py:504
  24.5 0.6 %collective-permute-done.4.refs_2_ = f32[128,384]{1,0:T(8,128)S(1)} collective-permute-done((f32[128,384]{1,0:T(8,128)S(1)}, f32[128,384]{1,0:T(8,128)S(1)}, u32[]{:S(2)}, u32[]{:S(2)}) %collective-permute-start.4) | collective-permute-done | bytes 196640 | tf_op jit(solution)/shard_map/ppermute | solution.py:516
  25.1 1.3 %collective-permute-done.3.refs_0_ = f32[128,128]{1,0:T(8,128)S(1)} collective-permute-done((f32[128,128]{1,0:T(8,128)S(1)}, f32[128,128]{1,0:T(8,128)S(1)}, u32[]{:S(2)}, u32[]{:S(2)}) %collective-permute-start.3) | collective-permute-done | bytes 65568 | tf_op jit(solution)/shard_map/ppermute | solution.py:615
  26.4 0.0 collective-permute-done.5.refs_4_
  26.4 1.3 %shard_map.116 = (f32[4,128,128]{2,1,0:T(8,128)}, f32[4,128,128]{2,1,0:T(8,128)S(1)}, f32[136,128]{1,0:T(8,128)S(1)}, f32[136,128]{1,0:T(8,128)S(1)}, f32[136,12...) custom-call(f32[128,128]{1,0:T(8,128)S(1)} %collective-permute-done.3.refs_0_, ...), custom_call_target="tpu_custom_call" | custom-call | flops 1000 | tf_op jit(solution)/shard_map/pallas_call | solution.py:504
  27.7 2.8 %collective-permute-start.9 = (f32[136,128]{1,0:T(8,128)S(1)}, f32[136,128]{1,0:T(8,128)S(1)}, u32[]{:S(2)}, u32[]{:S(2)}) collective-permute-start(f32[136,128]{1,0:T(8,128)S(1)} %get-tuple-element.93), channel_id=1, source_target_pairs={{0,16},{4,20},{8,24},{12,28},{16,0},{20,4},{24,8},{28,12},{1,17},{... | collective-permute-start | bytes 208904 | tf_op jit(solution)/shard_map/ppermute | solution.py:647
  30.5 0.1 collective-permute-start.6
  30.6 2.0 %collective-permute-start.7 = (f32[136,128]{1,0:T(8,128)S(1)}, f32[136,128]{1,0:T(8,128)S(1)}, u32[]{:S(2)}, u32[]{:S(2)}) collective-permute-start(f32[136,128]{1,0:T(8,128)S(1)} %get-tuple-element.87), channel_id=1, source_target_pairs={{0,8},{4,12},{8,0},{12,4},{16,24},{20,28},{24,16},{28,20},{1,9},{5... | collective-permute-start | bytes 208904 | tf_op jit(solution)/shard_map/ppermute | solution.py:516
  32.6 1.5 %collective-permute-start.8 = (f32[136,128]{1,0:T(8,128)S(1)}, f32[136,128]{1,0:T(8,128)S(1)}, u32[]{:S(2)}, u32[]{:S(2)}) collective-permute-start(f32[136,128]{1,0:T(8,128)S(1)} %get-tuple-element.88), channel_id=1, source_target_pairs={{0,12},{4,8},{8,4},{12,0},{16,28},{20,24},{24,20},{28,16},{1,13},{... | collective-permute-start | bytes 208904 | tf_op jit(solution)/shard_map/ppermute | solution.py:516
  34.1 0.0 collective-permute-done.9.refs_0_
  34.1 0.3 shard_map.117
  34.4 0.6 %collective-permute-start.10 = (f32[136,128]{1,0:T(8,128)S(1)}, f32[136,128]{1,0:T(8,128)S(1)}, u32[]{:S(2)}, u32[]{:S(2)}) collective-permute-start(f32[136,128]{1,0:T(8,128)S(1)} %get-tuple-element.97), channel_id=1, source_target_pairs={{0,4},{4,0},{8,12},{12,8},{16,20},{20,16},{24,28},{28,24},{1,5},{5... | collective-permute-start | bytes 208904 | tf_op jit(solution)/shard_map/ppermute | solution.py:516
  35.0 1.5 %collective-permute-start.11 = (f32[136,128]{1,0:T(8,128)S(1)}, f32[136,128]{1,0:T(8,128)S(1)}, u32[]{:S(2)}, u32[]{:S(2)}) collective-permute-start(f32[136,128]{1,0:T(8,128)S(1)} %get-tuple-element.98), channel_id=1, source_target_pairs={{0,8},{4,12},{8,0},{12,4},{16,24},{20,28},{24,16},{28,20},{1,9},{5... | collective-permute-start | bytes 208904 | tf_op jit(solution)/shard_map/ppermute | solution.py:516
  36.5 0.0 collective-permute-done.6.refs_1_.refs_13_
  36.5 1.4 %collective-permute-start.12 = (f32[136,128]{1,0:T(8,128)S(1)}, f32[136,128]{1,0:T(8,128)S(1)}, u32[]{:S(2)}, u32[]{:S(2)}) collective-permute-start(f32[136,128]{1,0:T(8,128)S(1)} %get-tuple-element.104), channel_id=1, source_target_pairs={{0,12},{4,8},{8,4},{12,0},{16,28},{20,24},{24,20},{28,16},{1,13},{... | collective-permute-start | bytes 208904 | tf_op jit(solution)/shard_map/ppermute | solution.py:516
  37.9 0.0 collective-permute-done.7.refs_2_.refs_14_
  37.9 0.0 collective-permute-done.8.refs_3_.refs_15_
  37.9 0.8 %collective-permute-done.10.refs_24_.refs_5_.refs_9_ = f32[136,128]{1,0:T(8,128)S(1)} collective-permute-done((f32[136,128]{1,0:T(8,128)S(1)}, f32[136,128]{1,0:T(8,128)S(1)}, u32[]{:S(2)}, u32[]{:S(2)}) %collective-permute-start.10) | collective-permute-done | bytes 69664 | tf_op jit(solution)/shard_map/ppermute | solution.py:516
  38.7 0.6 %collective-permute-done.11.refs_25_.refs_6_.refs_10_ = f32[136,128]{1,0:T(8,128)S(1)} collective-permute-done((f32[136,128]{1,0:T(8,128)S(1)}, f32[136,128]{1,0:T(8,128)S(1)}, u32[]{:S(2)}, u32[]{:S(2)}) %collective-permute-start.11) | collective-permute-done | bytes 69664 | tf_op jit(solution)/shard_map/ppermute | solution.py:516
  39.3 2.3 %shard_map.118 = (f32[4,256,128]{2,1,0:T(8,128)S(1)}, bf16[512,128]{1,0:T(8,128)(2,1)}, f32[4,256,128]{2,1,0:T(8,128)S(1)}, bf16[512,128]{1,0:T(8,128)(2,1)}, f32[4,256,128]{2,1,0:T(8,128)S(1)}) custom-call(f32[136,128]{1,0:T(8,128)S(1)} %get-tuple-element.85.refs_0_.refs_12_, f32[136,128]{1,0:T(8,128)S(1)} %collective-permute-done.6.refs_1_.refs_13_, ...), custom_call_target="tpu_custom_call" | custom-call | flops 1000 | tf_op jit(solution)/shard_map/pallas_call | solution.py:504
  41.6 0.1 collective-permute-done.12.refs_7_.refs_11_
  41.8 0.1 collective-permute-start.15
  41.8 1.6 %collective-permute-start.14 = (f32[1,128]{1,0:T(1,128)S(1)}, f32[1,128]{1,0:T(1,128)S(1)}, u32[]{:S(2)}, u32[]{:S(2)}) collective-permute-start(f32[1,128]{1,0:T(1,128)S(1)} %shard_map.119.refs_16_), channel_id=1, source_target_pairs={{0,2},{1,3},{2,0},{3,1},{4,6},{5,7},{6,4},{7,5},{8,10},{9,11},{10,... | collective-permute-start | bytes 1544 | tf_op jit(solution)/shard_map/ppermute | solution.py:711
  43.4 0.3 collective-permute-start.13
  43.7 2.3 %shard_map.120 = (f32[8,128]{1,0:T(8,128)}, bf16[1024,128]{1,0:T(8,128)(2,1)}, bf16[1024,128]{1,0:T(8,128)(2,1)}) custom-call(f32[1024,128]{1,0:T(8,128)S(1)} %get-tuple-element.57.refs_0_, f32[256,4]{1,0:T(8,128)S(1)} %get-tuple-element.59.refs_2_.refs_10_.refs_1_, f32[2,256,128]{2,1,0:T(8,128)S(1)} %get-tuple-element.67.refs_3_.refs_17_.refs_2_, ...), custom_call_target="tpu_custom_call" | custom-call | flops 1000 | tf_op jit(solution)/shard_map/pallas_call | solution.py:504
  46.0 0.0 collective-permute-done.15
  46.0 0.0 collective-permute-done.14
  46.0 0.0 collective-permute-done.13
  46.0 0.5 %add_bitcast_fusion = f32[128]{0:T(128)} fusion(f32[1,128]{1,0:T(1,128)S(1)} %shard_map.119.refs_16_, f32[1,128]{1,0:T(1,128)S(1)} %collective-permute-done.15, f32[1,128]{1,0:T(1,128)S(1)} %collective-permute-done.13, f32[1,128]{1,0:T(1,128)S(1)} %collective-permute-done.14), kind=kLoop, calls=%fused_computation | loop fusion | flops 384 | bytes 2560 | tf_op jit(solution)/shard_map/reshape | solution.py:722
  (3 shorter events, 0.0 us)
Async XLA Ops:
  4.8 11.6 %collective-permute-start.1 = (f32[128,640]{1,0:T(8,128)S(1)}, f32[128,640]{1,0:T(8,128)S(1)}, u32[]{:S(2)}, u32[]{:S(2)}) collective-permute-start(f32[128,640]{1,0:T(8,128)S(1)} %get-tuple-element.63.refs_6_), channel_id=1, source_target_pairs={{0,8},{4,12},{8,0},{12,4},{16,24},{20,28},{24,16},{28,20},{1,9},{5... | collective-permute-start | bytes 983048 | tf_op jit(solution)/shard_map/ppermute | solution.py:516
  7.9 6.0 %collective-permute-start = (f32[128,256]{1,0:T(8,128)S(1)}, f32[128,256]{1,0:T(8,128)S(1)}, u32[]{:S(2)}, u32[]{:S(2)}) collective-permute-start(f32[128,256]{1,0:T(8,128)S(1)} %get-tuple-element.62), channel_id=1, source_target_pairs={{0,4},{4,0},{8,12},{12,8},{16,20},{20,16},{24,28},{28,24},{1,5},{5... | collective-permute-start | bytes 393224 | tf_op jit(solution)/shard_map/ppermute | solution.py:516
  11.8 8.8 %collective-permute-start.2 = (f32[128,256]{1,0:T(8,128)S(1)}, f32[128,256]{1,0:T(8,128)S(1)}, u32[]{:S(2)}, u32[]{:S(2)}) collective-permute-start(f32[128,256]{1,0:T(8,128)S(1)} %get-tuple-element.64), channel_id=1, source_target_pairs={{0,12},{4,8},{8,4},{12,0},{16,28},{20,24},{24,20},{28,16},{1,13},{... | collective-permute-start | bytes 393224 | tf_op jit(solution)/shard_map/ppermute | solution.py:516
  11.9 13.2 %collective-permute-start.4 = (f32[128,384]{1,0:T(8,128)S(1)}, f32[128,384]{1,0:T(8,128)S(1)}, u32[]{:S(2)}, u32[]{:S(2)}) collective-permute-start(f32[128,384]{1,0:T(8,128)S(1)} %shard_map.113.refs_5_), channel_id=1, source_target_pairs={{0,4},{4,0},{8,12},{12,8},{16,20},{20,16},{24,28},{28,24},{1,5},{5... | collective-permute-start | bytes 589832 | tf_op jit(solution)/shard_map/ppermute | solution.py:516
  16.4 10.0 %collective-permute-start.5 = (f32[128,384]{1,0:T(8,128)S(1)}, f32[128,384]{1,0:T(8,128)S(1)}, u32[]{:S(2)}, u32[]{:S(2)}) collective-permute-start(f32[128,384]{1,0:T(8,128)S(1)} %shard_map.114), channel_id=1, source_target_pairs={{0,12},{4,8},{8,4},{12,0},{16,28},{20,24},{24,20},{28,16},{1,13},{... | collective-permute-start | bytes 589832 | tf_op jit(solution)/shard_map/ppermute | solution.py:516
  21.2 5.2 %collective-permute-start.3 = (f32[128,128]{1,0:T(8,128)S(1)}, f32[128,128]{1,0:T(8,128)S(1)}, u32[]{:S(2)}, u32[]{:S(2)}) collective-permute-start(f32[128,128]{1,0:T(8,128)S(1)} %get-tuple-element.76), channel_id=1, source_target_pairs={{0,16},{4,20},{8,24},{12,28},{16,0},{20,4},{24,8},{28,12},{1,17},{... | collective-permute-start | bytes 196616 | tf_op jit(solution)/shard_map/ppermute | solution.py:615
  27.7 6.4 %collective-permute-start.9 = (f32[136,128]{1,0:T(8,128)S(1)}, f32[136,128]{1,0:T(8,128)S(1)}, u32[]{:S(2)}, u32[]{:S(2)}) collective-permute-start(f32[136,128]{1,0:T(8,128)S(1)} %get-tuple-element.93), channel_id=1, source_target_pairs={{0,16},{4,20},{8,24},{12,28},{16,0},{20,4},{24,8},{28,12},{1,17},{... | collective-permute-start | bytes 208904 | tf_op jit(solution)/shard_map/ppermute | solution.py:647
  30.5 6.0 %collective-permute-start.6 = (f32[136,128]{1,0:T(8,128)S(1)}, f32[136,128]{1,0:T(8,128)S(1)}, u32[]{:S(2)}, u32[]{:S(2)}) collective-permute-start(f32[136,128]{1,0:T(8,128)S(1)} %get-tuple-element.86), channel_id=1, source_target_pairs={{0,4},{4,0},{8,12},{12,8},{16,20},{20,16},{24,28},{28,24},{1,5},{5... | collective-permute-start | bytes 208904 | tf_op jit(solution)/shard_map/ppermute | solution.py:516
  30.6 7.3 %collective-permute-start.7 = (f32[136,128]{1,0:T(8,128)S(1)}, f32[136,128]{1,0:T(8,128)S(1)}, u32[]{:S(2)}, u32[]{:S(2)}) collective-permute-start(f32[136,128]{1,0:T(8,128)S(1)} %get-tuple-element.87), channel_id=1, source_target_pairs={{0,8},{4,12},{8,0},{12,4},{16,24},{20,28},{24,16},{28,20},{1,9},{5... | collective-permute-start | bytes 208904 | tf_op jit(solution)/shard_map/ppermute | solution.py:516
  32.6 5.3 %collective-permute-start.8 = (f32[136,128]{1,0:T(8,128)S(1)}, f32[136,128]{1,0:T(8,128)S(1)}, u32[]{:S(2)}, u32[]{:S(2)}) collective-permute-start(f32[136,128]{1,0:T(8,128)S(1)} %get-tuple-element.88), channel_id=1, source_target_pairs={{0,12},{4,8},{8,4},{12,0},{16,28},{20,24},{24,20},{28,16},{1,13},{... | collective-permute-start | bytes 208904 | tf_op jit(solution)/shard_map/ppermute | solution.py:516
  34.4 4.4 %collective-permute-start.10 = (f32[136,128]{1,0:T(8,128)S(1)}, f32[136,128]{1,0:T(8,128)S(1)}, u32[]{:S(2)}, u32[]{:S(2)}) collective-permute-start(f32[136,128]{1,0:T(8,128)S(1)} %get-tuple-element.97), channel_id=1, source_target_pairs={{0,4},{4,0},{8,12},{12,8},{16,20},{20,16},{24,28},{28,24},{1,5},{5... | collective-permute-start | bytes 208904 | tf_op jit(solution)/shard_map/ppermute | solution.py:516
  35.0 4.3 %collective-permute-start.11 = (f32[136,128]{1,0:T(8,128)S(1)}, f32[136,128]{1,0:T(8,128)S(1)}, u32[]{:S(2)}, u32[]{:S(2)}) collective-permute-start(f32[136,128]{1,0:T(8,128)S(1)} %get-tuple-element.98), channel_id=1, source_target_pairs={{0,8},{4,12},{8,0},{12,4},{16,24},{20,28},{24,16},{28,20},{1,9},{5... | collective-permute-start | bytes 208904 | tf_op jit(solution)/shard_map/ppermute | solution.py:516
  36.5 5.2 %collective-permute-start.12 = (f32[136,128]{1,0:T(8,128)S(1)}, f32[136,128]{1,0:T(8,128)S(1)}, u32[]{:S(2)}, u32[]{:S(2)}) collective-permute-start(f32[136,128]{1,0:T(8,128)S(1)} %get-tuple-element.104), channel_id=1, source_target_pairs={{0,12},{4,8},{8,4},{12,0},{16,28},{20,24},{24,20},{28,16},{1,13},{... | collective-permute-start | bytes 208904 | tf_op jit(solution)/shard_map/ppermute | solution.py:516
  41.8 4.2 %collective-permute-start.15 = (f32[1,128]{1,0:T(1,128)S(1)}, f32[1,128]{1,0:T(1,128)S(1)}, u32[]{:S(2)}, u32[]{:S(2)}) collective-permute-start(f32[1,128]{1,0:T(1,128)S(1)} %shard_map.119.refs_16_), channel_id=1, source_target_pairs={{0,3},{1,2},{2,1},{3,0},{4,7},{5,6},{6,5},{7,4},{8,11},{9,10},{10,... | collective-permute-start | bytes 1544 | tf_op jit(solution)/shard_map/ppermute | solution.py:711
  41.8 4.1 %collective-permute-start.14 = (f32[1,128]{1,0:T(1,128)S(1)}, f32[1,128]{1,0:T(1,128)S(1)}, u32[]{:S(2)}, u32[]{:S(2)}) collective-permute-start(f32[1,128]{1,0:T(1,128)S(1)} %shard_map.119.refs_16_), channel_id=1, source_target_pairs={{0,2},{1,3},{2,0},{3,1},{4,6},{5,7},{6,4},{7,5},{8,10},{9,11},{10,... | collective-permute-start | bytes 1544 | tf_op jit(solution)/shard_map/ppermute | solution.py:711
  43.4 2.6 %collective-permute-start.13 = (f32[1,128]{1,0:T(1,128)S(1)}, f32[1,128]{1,0:T(1,128)S(1)}, u32[]{:S(2)}, u32[]{:S(2)}) collective-permute-start(f32[1,128]{1,0:T(1,128)S(1)} %shard_map.119.refs_16_), channel_id=1, source_target_pairs={{0,1},{1,0},{2,3},{3,2},{4,5},{5,4},{6,7},{7,6},{8,9},{9,8},{10,11... | collective-permute-start | bytes 1544 | tf_op jit(solution)/shard_map/ppermute | solution.py:711
